TPU v7x, 512 devices: a whole 4x4x16 slice. The times are simulated.
512 devices in a mesh: dp: 16 (over z), row: 4 (over x), col: 8 (over y, core).
Axes of the slice: x: 4, y: 4, z: 16, core: 2. Of those that a mesh axis runs over, the one named last changes fastest.
Arguments:
- gradients: float32 [16, 2, 8192, 1024], P('dp', None, 'row', 'col'), may hold values from -20 to 20
- weight: float32 [2, 8192, 1024], P(None, 'row', 'col'), may hold values from -3 to 3
- row_state: float32 [2, 8192], P(None, 'row'), may hold values from 1e-06 to 30
- col_state: float32 [2, 1024], P(None, 'col'), may hold values from 1e-06 to 30
Outputs:
- new_weight: float32 [2, 8192, 1024], P(None, 'row', 'col')
- row_new: float32 [2, 8192], P(None, 'row')
- col_new: float32 [2, 1024], P(None, 'col')
All inputs are finite; a program needn't handle non-finite values.
Results may differ from a plain program's by a relative error of at most 0.0003.
Values sent between devices are 32-bit elements; how exact they have to be, the bound alone decides.
No kernel may reach another device: no remote copies, remote signals or barrier semaphores. Data moves between devices by JAX's collectives and lax.ppermute only.
A program may use at most 64 MiB of HBM per device.

v0:
```python
import jax
import jax.numpy as jnp
from jax import lax
from jax.sharding import PartitionSpec as P

D = 8192
KV = 1024


epsilon_one = 1e-30
decay_rate = 0.8
clip_limit = 1.0
step_size = 0.25


def local(gradients, weight, row_state, col_state):
    mine = gradients[0]
    summed = lax.psum(mine, "dp")
    squares = summed * summed + epsilon_one
    row_part = jnp.sum(squares, axis=2)
    col_part = jnp.sum(squares, axis=1)
    state_part = jnp.sum(row_state, axis=1)
    row_sum = lax.psum(row_part, "col")
    col_sum, state_sum = lax.psum((col_part, state_part), "row")
    grand = lax.psum(jnp.sum(col_sum, axis=1), "col")
    row_fresh = decay_rate * row_state + (1.0 - decay_rate) * (row_sum / KV)
    col_new = decay_rate * col_state + (1.0 - decay_rate) * (col_sum / D)
    row_total = decay_rate * state_sum + (1.0 - decay_rate) * (grand / KV)
    second = row_fresh[:, :, None] * col_new[:, None, :] * (D / row_total)[:, None, None]
    update = summed * lax.rsqrt(second)
    local_square = jnp.sum(update * update, axis=(1, 2))
    square_sum = lax.psum(local_square, ("row", "col"))
    mean_square = square_sum / (D * KV)
    divisor = jnp.maximum(1.0, jnp.sqrt(mean_square) / clip_limit)
    fresh_weight = weight - step_size * update / divisor[:, None, None]
    return (fresh_weight, row_fresh, col_new)


def solution(mesh):
    in_specs = (P("dp", None, "row", "col"), P(None, "row", "col"), P(None, "row"), P(None, "col"))
    out_specs = (P(None, "row", "col"), P(None, "row"), P(None, "col"))
    return jax.shard_map(local, mesh=mesh, in_specs=in_specs, out_specs=out_specs, check_vma=False)
```

profile of v0, /device:TPU:1, one launch (start us, length us, event | category | flops | bytes accessed | tf_op | source)
XLA Modules:
  0.0 269.7 jit_solution(10071896448458839620)
XLA Ops:
  7.2 0.0 copy-start.2
  7.2 0.0 all-reduce.4.cloned.1.call-start
  7.2 0.0 copy-start.4
  7.2 0.7 all-reduce.4.cloned.1.call-update
  7.9 0.0 copy-done.2
  7.9 0.1 reduce_sum.47
  8.1 142.9 %all-reduce.4.cloned.1.call-done = f32[2,2048,128]{2,1,0:T(8,128)} async-done(((f32[2,2048,128]{2,1,0:T(8,128)}), f32[2,2048,128]{2,1,0:T(8,128)}) %all-reduce.4.cloned.1.call-update) | async-done | bytes 2097168 | tf_op jit(solution)/shard_map/psum | solution.py:18
  151.0 0.0 copy-start
  151.0 2.4 fusion.1
  153.3 9.1 %all-reduce.1 = (f32[2,128]{1,0:T(2,128)S(1)}, f32[2]{0:T(128)S(1)}) all-reduce(f32[2,128]{1,0:T(2,128)S(1)} %get-tuple-element.4, f32[2]{0:T(128)S(1)} %reduce_sum.47), channel_id=1, replica_groups=mesh['dp'=16,'row'=4,'col'=8] {'row'}, use_global_device_ids=true, to_apply=%region_4.0 | all-reduce | flops 258 | bytes 2064 | tf_op jit(solution)/shard_map/psum | solution.py:24
  162.4 0.0 copy-done.4
  162.4 0.1 multiply_add_fusion.2
  162.5 0.0 copy-start.3
  162.5 30.9 %all-reduce = (f32[2]{0:T(128)S(1)}, f32[2,2048]{1,0:T(2,128)S(1)}) all-reduce(f32[2]{0:T(128)S(1)} %get-tuple-element.10, f32[2,2048]{1,0:T(2,128)S(1)} %get-tuple-element.3), channel_id=1, replica_groups=mesh['dp'=16,'row'=4,'col'=8] {'col'}, use_global_device_ids=true, to_apply=%region_8.0 | all-reduce | flops 4098 | bytes 32784 | tf_op jit(solution)/shard_map/psum | solution.py:25
  193.5 0.0 copy-start.1
  193.5 0.0 copy-done
  193.5 0.9 multiply_reduce_fusion
  194.4 65.6 %psum.47 = f32[2]{0:T(128)S(1)} all-reduce(f32[2]{0:T(128)S(1)} %multiply_reduce_fusion), channel_id=1, replica_groups=mesh['dp'=16,'row'=4,'col'=8] {'row','col'}, use_global_device_ids=true, to_apply=%region_10.0 | all-reduce | flops 2 | bytes 16 | tf_op jit(solution)/shard_map/psum | solution.py:32
  260.0 2.9 %divide_subtract_fusion = f32[2,2048,128]{2,1,0:T(8,128)} fusion(f32[2,2048,128]{2,1,0:T(8,128)} %param.5, f32[2,2048,128]{2,1,0:T(8,128)S(1)} %copy-done, f32[2]{0:T(128)S(1)} %sqrt_maximum_fusion, f32[2]{0:T(128)S(1)} %add_divide_fusion, f32[2,128]{1,0:T(2,128)S(1)} %get-tuple-element.9, f32[2,2048]{1,0:T(2,128)S(1)} %multiply_add_fusion.1), kind=kLoop, calls=%fused_computation | loop fusion | flops 3145728 | bytes 6308880 | tf_op jit(solution)/shard_map/sub | solution.py:35
  262.9 0.0 copy-done.3
  262.9 0.0 copy-done.1
  (3 shorter events, 0.0 us)
Async XLA Ops:
  7.2 0.7 copy-start.2
  7.2 143.8 %all-reduce.4.cloned.1.call-start = ((), (), s32[]{:S(2)}) async-start(), calls=%async_computation | async-start | bytes 4194304 | tf_op jit(solution)/shard_map/psum | solution.py:18
  7.2 155.2 %copy-start.4 = (f32[2,128]{1,0:T(2,128)S(1)}, f32[2,128]{1,0:T(2,128)}, u32[]{:S(2)}) copy-start(f32[2,128]{1,0:T(2,128)} %param.7) | copy-start | bytes 3076
  151.0 42.6 %copy-start = (f32[2,2048,128]{2,1,0:T(8,128)S(1)}, f32[2,2048,128]{2,1,0:T(8,128)}, u32[]{:S(2)}) copy-start(f32[2,2048,128]{2,1,0:T(8,128)} %all-reduce.4.cloned.1.call-done) | copy-start | bytes 6291460
  162.5 100.3 %copy-start.3 = (f32[2,128]{1,0:T(2,128)}, f32[2,128]{1,0:T(2,128)S(1)}, u32[]{:S(2)}) copy-start(f32[2,128]{1,0:T(2,128)S(1)} %get-tuple-element.9) | copy-start | bytes 3076
  193.5 69.4 %copy-start.1 = (f32[2,2048]{1,0:T(2,128)}, f32[2,2048]{1,0:T(2,128)S(1)}, u32[]{:S(2)}) copy-start(f32[2,2048]{1,0:T(2,128)S(1)} %multiply_add_fusion.1) | copy-start | bytes 49156
Sparse Core Ops, SparseCore 0:
  10.4 140.5 all-reduce.3
where the time goes:
time: 270 us
  waiting for transfers between devices  144 us (53%)
  blocking collectives  106 us (39%)
  between operations  14.1 us (5%)
  other arithmetic  6.46 us (2%)
    psum x1, waiting for transfers between devices, local(): summed = lax.psum(mine, 'dp')  143 us
    psum x1, blocking collectives, local(): square_sum = lax.psum(local_square, ('row', 'col'))  65.6 us
    psum x1, blocking collectives, local(): grand = lax.psum(jnp.sum(col_sum, axis=1), 'col')  30.9 us
    psum x1, blocking collectives, local(): col_sum, state_sum = lax.psum((col_part, state_part), 'row')  9.08 us
  transfers between devices with their start and end apart: 1, of which 1 were waited for; matrix products, arithmetic and copies ran while one was open for 0% of the time, Pallas kernels for 0%

commit v1 on v0

v1 whole, which is shorter than its diff:
```python
import jax
import jax.numpy as jnp
from jax import lax
from jax.sharding import PartitionSpec as P

D = 8192
KV = 1024

epsilon_one = 1e-30
decay_rate = 0.8
clip_limit = 1.0
step_size = 0.25


def statistics(part, row_state, col_state, rows):
    mats, count, width = part.shape
    squares = part * part + epsilon_one
    old = lax.dynamic_slice_in_dim(row_state, lax.axis_index("dp") * count, count, axis=1)
    row_part = jnp.sum(squares, axis=2)
    row_sum = jnp.sum(lax.all_gather(row_part, "col"), axis=0)
    row_fresh = decay_rate * old + (1.0 - decay_rate) * (row_sum / KV)
    col_part = jnp.sum(squares, axis=1)
    weighted = jnp.sum(squares * (1.0 / row_fresh)[:, :, None], axis=1)
    total = jnp.broadcast_to(jnp.sum(row_fresh, axis=1, keepdims=True), (mats, width))
    packed = jnp.concatenate([row_fresh, col_part, weighted, total], axis=0)
    everyone = lax.all_gather(packed, "dp")
    row_new = jnp.transpose(everyone[:, :mats], (1, 0, 2)).reshape(mats, rows)
    sums = jnp.sum(everyone[:, mats:], axis=0)
    sums = jnp.sum(lax.all_gather(sums, "row"), axis=0)
    col_sum, weighted, total = sums[:mats], sums[mats : 2 * mats], sums[2 * mats :]
    row_total = total[:, 0]
    col_new = decay_rate * col_state + (1.0 - decay_rate) * (col_sum / D)
    own = jnp.sum(weighted / col_new, axis=1)
    own = jnp.broadcast_to(own[:, None], (mats, width))
    ratio = jnp.sum(lax.all_gather(own, "col"), axis=0)[:, 0]
    mean_square = ratio * (row_total / D) / (D * KV)
    divisor = jnp.maximum(1.0, jnp.sqrt(mean_square) / clip_limit)
    scale = step_size * jnp.sqrt(row_total / D) / divisor
    return row_new, col_new, scale


def local(gradients, weight, row_state, col_state):
    mine = gradients[0]
    rows = mine.shape[1]
    part = lax.psum_scatter(mine, "dp", scatter_dimension=1, tiled=True)
    summed = lax.all_gather(part, "dp", axis=1, tiled=True)
    row_new, col_new, scale = statistics(part, row_state, col_state, rows)
    left = scale[:, None] * lax.rsqrt(row_new)
    right = lax.rsqrt(col_new)
    new_weight = weight - summed * left[:, :, None] * right[:, None, :]
    return (new_weight, row_new, col_new)


def solution(mesh):
    in_specs = (P("dp", None, "row", "col"), P(None, "row", "col"), P(None, "row"), P(None, "col"))
    out_specs = (P(None, "row", "col"), P(None, "row"), P(None, "col"))
    return jax.shard_map(local, mesh=mesh, in_specs=in_specs, out_specs=out_specs, check_vma=False)
```

time: 270 us -> 172 us (0.64); the launches traced: 270 us -> 169 us
  waiting for transfers between devices: 144 us -> 71.8 us
  blocking collectives: 106 us -> 73.5 us
    psum x1 -> x0, waiting for transfers between devices: 143 us -> none  [local(): summed = lax.psum(mine, 'dp')]
    psum x3 -> x0, blocking collectives: 106 us -> none  [the longest x1 65.6 us: local(): square_sum = lax.psum(local_square, ('row', 'col'))]
    reduce_scatter x0 -> x1, waiting for transfers between devices: none -> 71.1 us  [local(): part = lax.psum_scatter(mine, 'dp', scatter_dimension=1, tiled=True)]
    all_gather x0 -> x3, blocking collectives: none -> 53.8 us  [the longest x1 22.4 us: statistics(): everyone = lax.all_gather(packed, 'dp')]
    unnamed x0 -> x1, blocking collectives: none -> 19.7 us
  transfers between devices with their start and end apart: 1 -> 2, of which waited for: 1 -> 1; matrix products, arithmetic and copies ran while one was open for 0% -> 3% of each run, Pallas kernels for 0% -> 0%
where the time goes in v1:
time: 172 us; the launch traced here: 169 us
  blocking collectives  73.5 us (43%)
  waiting for transfers between devices  71.8 us (42%)
  between operations  14.8 us (9%)
  other arithmetic  6.8 us (4%)
  local copies, waits for them, and re-layouts  1.77 us (1%)
    reduce_scatter x1, waiting for transfers between devices, local(): part = lax.psum_scatter(mine, 'dp', scatter_dimension=1, tiled=True)  71.1 us
    all_gather x1, blocking collectives, statistics(): everyone = lax.all_gather(packed, 'dp')  22.4 us
    all_gather x1, blocking collectives, statistics(): row_sum = jnp.sum(lax.all_gather(row_part, 'col'), axis=0)  21.4 us
    unnamed x1, blocking collectives  19.7 us
    all_gather x1, blocking collectives, statistics(): sums = jnp.sum(lax.all_gather(sums, 'row'), axis=0)  9.97 us
  transfers between devices with their start and end apart: 2, of which 1 were waited for; matrix products, arithmetic and copies ran while one was open for 3% of the time, Pallas kernels for 0%

profile of v1, /device:TPU:1, one launch (start us, length us, event | category | flops | bytes accessed | tf_op | source)
XLA Modules:
  0.0 168.8 jit_solution(11474407534089017500)
XLA Ops:
  7.2 0.0 copy-start.2
  7.2 0.0 copy-start
  7.2 0.0 reduce-scatter.2.cloned.1.call-start
  7.2 0.7 reduce-scatter.2.cloned.1.call-update
  7.9 0.0 all-gather.8.cloned.1.call-start
  8.0 71.1 %reduce-scatter.2.cloned.1.call-done = f32[2,128,128]{2,1,0:T(8,128)} async-done(((f32[2,2048,128]{2,1,0:T(8,128)}), f32[2,128,128]{2,1,0:T(8,128)}) %reduce-scatter.2.cloned.1.call-update) | async-done | bytes 131088 | tf_op jit(solution)/shard_map/reduce_scatter | solution.py:45
  79.1 0.0 all-gather.8.cloned.1.call-update
  79.1 1.3 dynamic-slice
  81.0 1.0 fusion.1
  82.0 21.4 %all-gather.4 = f32[8,2,128]{2,1,0:T(2,128)S(1)} all-gather(f32[1,2,128]{2,1,0:T(2,128)S(1)} %bitcast.14), channel_id=3, replica_groups=mesh['dp'=16,'row'=4,'col'=8] {'col'}, dimensions={0}, use_global_device_ids=true | all-gather | bytes 9216 | tf_op jit(solution)/shard_map/all_gather | solution.py:20
  103.5 0.8 fusion.4
  104.2 0.1 pad.3.clone
  104.3 1.0 fusion
  105.3 0.1 maximum_maximum_fusion
  105.4 22.4 %all-gather.1 = f32[128,128]{1,0:T(8,128)S(1)} all-gather(f32[8,128]{1,0:T(8,128)S(1)} %maximum_maximum_fusion), channel_id=4, replica_groups=mesh['dp'=16,'row'=4,'col'=8] {'dp'}, dimensions={0}, use_global_device_ids=true | all-gather | bytes 69632 | tf_op jit(solution)/shard_map/all_gather | solution.py:26
  127.9 10.0 %all-gather.5 = f32[4,6,128]{2,1,0:T(8,128)S(1)} all-gather(f32[1,6,128]{2,1,0:T(8,128)S(1)} %bitcast.13), channel_id=5, replica_groups=mesh['dp'=16,'row'=4,'col'=8] {'row'}, dimensions={0}, use_global_device_ids=true | all-gather | bytes 15360 | tf_op jit(solution)/shard_map/all_gather | solution.py:29
  137.9 0.0 copy-done.2
  137.9 0.1 fusion.2
  138.0 0.0 copy-start.1
  138.0 0.2 dynamic-update-slice
  138.3 19.7 %all-reduce = f32[16]{0:T(128)S(1)} all-reduce(f32[16]{0:T(128)S(1)} %dynamic-update-slice), channel_id=6, replica_groups=mesh['dp'=16,'row'=4,'col'=8] {'col'}, use_global_device_ids=true, to_apply=%add | all-reduce | flops 16 | bytes 128
  158.0 0.1 reshape.40
  158.1 0.1 copy.12
  158.2 0.1 broadcast_reduce_fusion
  158.3 0.1 fusion.3
  158.4 0.6 rsqrt_multiply_fusion
  159.0 0.0 all-gather.8.cloned.1.call-done
  159.0 0.0 copy-done
  159.0 2.9 %multiply_subtract_fusion = f32[2,2048,128]{2,1,0:T(8,128)} fusion(f32[2,2048,128]{2,1,0:T(8,128)S(1)} %copy-done, f32[2,2048,128]{2,1,0:T(8,128)} %all-gather.8.cloned.1.call-done, f32[2,128]{1,0:T(2,128)S(1)} %rsqrt.11, f32[2,2048]{1,0:T(2,128)S(1)} %get-tuple-element.5), kind=kLoop, calls=%fused_computation | loop fusion | flops 1572864 | bytes 6308864 | tf_op jit(solution)/shard_map/sub | solution.py:50
  161.9 0.0 copy-done.1
  (6 shorter events, 0.1 us)
Async XLA Ops:
  7.2 130.7 %copy-start.2 = (f32[2,128]{1,0:T(2,128)S(1)}, f32[2,128]{1,0:T(2,128)}, u32[]{:S(2)}) copy-start(f32[2,128]{1,0:T(2,128)} %param.7) | copy-start | bytes 3076
  7.2 151.8 %copy-start = (f32[2,2048,128]{2,1,0:T(8,128)S(1)}, f32[2,2048,128]{2,1,0:T(8,128)}, u32[]{:S(2)}) copy-start(f32[2,2048,128]{2,1,0:T(8,128)} %param.5) | copy-start | bytes 6291460
  7.2 71.9 %reduce-scatter.2.cloned.1.call-start = ((), (), s32[]{:S(2)}) async-start(), calls=%async_computation.1 | async-start | bytes 2228224 | tf_op jit(solution)/shard_map/reduce_scatter | solution.py:45
  7.9 151.1 %all-gather.8.cloned.1.call-start = ((), (), s32[]{:S(2)}) async-start(), calls=%async_computation.2 | async-start | bytes 2228224 | tf_op jit(solution)/shard_map/all_gather | solution.py:46
  138.0 23.9 %copy-start.1 = (f32[2,128]{1,0:T(2,128)}, f32[2,128]{1,0:T(2,128)S(1)}, u32[]{:S(2)}) copy-start(f32[2,128]{1,0:T(2,128)S(1)} %get-tuple-element.8) | copy-start | bytes 3076
Sparse Core Ops, SparseCore 0:
  10.8 68.1 reduce-scatter.1
  81.2 73.0 all-gather.7

commit v2 on v1

--- a/solution.py
+++ b/solution.py
@@ -1,6 +1,9 @@
 import jax
 import jax.numpy as jnp
+import numpy as np
 from jax import lax
+from jax.experimental import pallas as pl
+from jax.experimental.pallas import tpu as pltpu
 from jax.sharding import PartitionSpec as P
 
 D = 8192
@@ -11,11 +14,66 @@
 clip_limit = 1.0
 step_size = 0.25
 
+REACH = (1, -1, 3, -5)
 
-def statistics(part, row_state, col_state, rows):
+
+def partner(r, step, size, shift):
+    r = (r - shift) % size
+    r = r + REACH[step] if r % 2 == 0 else r - REACH[step]
+    return (r + shift) % size
+
+
+def owners(size, shift):
+    def reach(r, step):
+        if step == len(REACH):
+            return frozenset([r])
+        return reach(r, step + 1) | reach(partner(r, step, size, shift), step + 1)
+
+    place, spans = [0] * size, [frozenset(range(size))]
+    for step in range(len(REACH)):
+        spans = [half for span in spans for half in (reach(min(span), step + 1), span - reach(min(span), step + 1))]
+    for position, span in enumerate(spans):
+        (only,) = span
+        place[only] = position
+    return place
+
+
+def lookup(table, index):
+    words = [sum(v << (4 * i) for i, v in enumerate(table[k : k + 7])) for k in (0, 7, 14)]
+    word = jnp.where(index < 7, words[0], jnp.where(index < 14, words[1], words[2]))
+    return (word >> (4 * (index % 7))) & 15
+
+
+def halvings(x, place, shift, size):
+    label = lookup(place, lax.axis_index("dp"))
+    keep, base, count = x, jnp.int32(0), size
+    arrived = None
+    for step in range(len(REACH)):
+        count //= 2
+        bit = (label // count) % 2
+        go, stay = (1 - bit) * count, bit * count
+        take = lambda a, at: lax.dynamic_slice_in_dim(a, at, count, axis=0)
+        if arrived is None:
+            out = take(keep, go)
+            base = stay
+        else:
+            out = take(keep, base + go) + take(arrived, go)
+        pairs = [(r, partner(r, step, size, shift)) for r in range(size)]
+        landed = lax.ppermute(out, "dp", pairs)
+        if arrived is not None:
+            keep, base = take(keep, base + stay) + take(arrived, stay), jnp.int32(0)
+        arrived = landed
+    return lax.dynamic_slice_in_dim(keep, base, 1, axis=0)[0] + arrived[0]
+
+
+def statistics(part, row_state, col_state, places):
     mats, count, width = part.shape
+    size = len(places[0])
     squares = part * part + epsilon_one
-    old = lax.dynamic_slice_in_dim(row_state, lax.axis_index("dp") * count, count, axis=1)
+    me = lax.axis_index("dp")
+    old = jnp.concatenate(
+        [lax.dynamic_slice(row_state, (m, lookup(places[m], me) * count), (1, count)) for m in range(mats)], axis=0
+    )
     row_part = jnp.sum(squares, axis=2)
     row_sum = jnp.sum(lax.all_gather(row_part, "col"), axis=0)
     row_fresh = decay_rate * old + (1.0 - decay_rate) * (row_sum / KV)
@@ -24,7 +82,9 @@
     total = jnp.broadcast_to(jnp.sum(row_fresh, axis=1, keepdims=True), (mats, width))
     packed = jnp.concatenate([row_fresh, col_part, weighted, total], axis=0)
     everyone = lax.all_gather(packed, "dp")
-    row_new = jnp.transpose(everyone[:, :mats], (1, 0, 2)).reshape(mats, rows)
+    row_new = jnp.stack(
+        [jnp.concatenate([everyone[place.index(b), m] for b in range(size)]) for m, place in enumerate(places)]
+    )
     sums = jnp.sum(everyone[:, mats:], axis=0)
     sums = jnp.sum(lax.all_gather(sums, "row"), axis=0)
     col_sum, weighted, total = sums[:mats], sums[mats : 2 * mats], sums[2 * mats :]
@@ -39,15 +99,54 @@
     return row_new, col_new, scale
 
 
+GROUP = 4
+
+
+def finish_kernel(table, left_ref, right_ref, *refs):
+    blocks, weight_ref, out_ref = refs[:GROUP], refs[GROUP], refs[GROUP + 1]
+    right = right_ref[0]
+    columns = jnp.transpose(left_ref[0, 0])
+    for k in range(GROUP):
+        factor = columns[:, k : k + 1] * right[0:1]
+        out_ref[0, k] = weight_ref[0, k] - blocks[k][0, 0] * factor
+
+
+def finish(summed, weight, left, right, places):
+    mats, size, rows, width = weight.shape
+    table = jnp.asarray(np.array([[place.index(b) for b in range(size)] for place in places], np.int32))
+    left = jnp.pad(left.reshape(mats, size // GROUP, GROUP, rows), ((0, 0), (0, 0), (0, 8 - GROUP), (0, 0)))
+    right = jnp.broadcast_to(right[:, None, :], (mats, 8, width))
+    block = lambda k: pl.BlockSpec((1, 1, rows, width), lambda m, g, t: (m, t[m, g * GROUP + k], 0, 0))
+    tile = pl.BlockSpec((1, GROUP, rows, width), lambda m, g, t: (m, g, 0, 0))
+    return pl.pallas_call(
+        finish_kernel,
+        grid_spec=pltpu.PrefetchScalarGridSpec(
+            num_scalar_prefetch=1,
+            grid=(mats, size // GROUP),
+            in_specs=[
+                pl.BlockSpec((1, 1, 8, rows), lambda m, g, t: (m, g, 0, 0)),
+                pl.BlockSpec((1, 8, width), lambda m, g, t: (m, 0, 0)),
+            ]
+            + [block(k) for k in range(GROUP)]
+            + [tile],
+            out_specs=tile,
+        ),
+        out_shape=jax.ShapeDtypeStruct(weight.shape, weight.dtype),
+    )(table, left, right, *[summed] * GROUP, weight)
+
+
 def local(gradients, weight, row_state, col_state):
-    mine = gradients[0]
-    rows = mine.shape[1]
-    part = lax.psum_scatter(mine, "dp", scatter_dimension=1, tiled=True)
+    mats, rows, width = weight.shape
+    size = lax.axis_size("dp")
+    places = [owners(size, m) for m in range(mats)]
+    mine = gradients.reshape(mats, size, rows // size, width)
+    part = jnp.stack([halvings(mine[m], places[m], m, size) for m in range(mats)])
     summed = lax.all_gather(part, "dp", axis=1, tiled=True)
-    row_new, col_new, scale = statistics(part, row_state, col_state, rows)
+    row_new, col_new, scale = statistics(part, row_state, col_state, places)
     left = scale[:, None] * lax.rsqrt(row_new)
     right = lax.rsqrt(col_new)
-    new_weight = weight - summed * left[:, :, None] * right[:, None, :]
+    blocks = lambda a: a.reshape(mats, size, rows // size, width)
+    new_weight = finish(blocks(summed), blocks(weight), left, right, places).reshape(weight.shape)
     return (new_weight, row_new, col_new)
 
 

time: 172 us -> 168 us (0.977)
  the two profiles are of different devices: /device:TPU:1 before, /device:TPU:8 now
where the time goes in v2:
time: 168 us; the launch traced here: 167 us
  blocking collectives  60.6 us (36%)
  starting transfers between devices  47.7 us (28%)
  waiting for transfers between devices  25.9 us (15%)
  between operations  15.3 us (9%)
  Pallas kernels  7.6 us (5%)
  local copies, waits for them, and re-layouts  7.27 us (4%)
  other arithmetic  3.02 us (2%)
    ppermute x8, starting transfers between devices, halvings(): landed = lax.ppermute(out, 'dp', pairs)  47.7 us
    all_gather x1, blocking collectives, statistics(): everyone = lax.all_gather(packed, 'dp')  28 us
    all_gather x1, waiting for transfers between devices, local(): summed = lax.all_gather(part, 'dp', axis=1, tiled=True)  14.6 us
    all_gather x1, blocking collectives, statistics(): sums = jnp.sum(lax.all_gather(sums, 'row'), axis=0)  12.3 us
    unnamed x1, blocking collectives  11.6 us
    ppermute x8, waiting for transfers between devices, halvings(): landed = lax.ppermute(out, 'dp', pairs)  11.3 us
    all_gather x1, blocking collectives, statistics(): row_sum = jnp.sum(lax.all_gather(row_part, 'col'), axis=0)  8.77 us
    pallas_call x1, Pallas kernels, finish(): pl.pallas_call(finish_kernel, grid_spec=pltpu.PrefetchScalarGridSpec(num_...  7.6 us
  transfers between devices with their start and end apart: 9, of which 6 were waited for; matrix products, arithmetic and copies ran while one was open for 4% of the time, Pallas kernels for 0%

profile of v2, /device:TPU:8, one launch (start us, length us, event | category | flops | bytes accessed | tf_op | source)
XLA Modules:
  0.0 167.4 jit_solution(192018193822522209)
XLA Ops:
  7.2 0.0 all-gather.8.cloned.1.call-start
  7.3 1.7 %fusion.9 = (f32[1,1,2048,128]{3,2,1,0:T(8,128)S(1)}, f32[1,1,2048,128]{3,2,1,0:T(8,128)S(1)}) fusion(f32[1,2,2048,128]{3,2,1,0:T(8,128)} %param.5), kind=kLoop, calls=%fused_computation.101 | loop fusion | bytes 4194304 | tf_op jit(solution)/shard_map/slice | solution.py:143
  9.0 0.8 constant_dynamic-slice_fusion.1
  9.8 3.8 %collective-permute-start = (f32[8,128,128]{2,1,0:T(8,128)}, f32[8,128,128]{2,1,0:T(8,128)S(1)}, u32[]{:S(2)}, u32[]{:S(2)}) collective-permute-start(f32[8,128,128]{2,1,0:T(8,128)} %constant_dynamic-slice_fusion.1), channel_id=1, source_target_pairs={{0,32},{32,0},{64,96},{96,64},{128,160},{160,128},{192,224},{224,1... | collective-permute-start | bytes 1572872 | tf_op jit(solution)/shard_map/ppermute | solution.py:62
  13.7 0.8 constant_dynamic-slice_fusion
  14.5 10.5 %collective-permute-start.4 = (f32[8,128,128]{2,1,0:T(8,128)}, f32[8,128,128]{2,1,0:T(8,128)S(1)}, u32[]{:S(2)}, u32[]{:S(2)}) collective-permute-start(f32[8,128,128]{2,1,0:T(8,128)} %constant_dynamic-slice_fusion), channel_id=1, source_target_pairs={{0,480},{32,64},{64,32},{96,128},{128,96},{160,192},{192,160},{224... | collective-permute-start | bytes 1572872 | tf_op jit(solution)/shard_map/ppermute | solution.py:62
  25.1 0.6 collective-permute-done
  25.7 0.8 dynamic-slice_add_fusion.3
  26.5 11.2 %collective-permute-start.1 = (f32[4,128,128]{2,1,0:T(8,128)}, f32[4,128,128]{2,1,0:T(8,128)S(1)}, u32[]{:S(2)}, u32[]{:S(2)}) collective-permute-start(f32[4,128,128]{2,1,0:T(8,128)} %get-tuple-element.12), channel_id=1, source_target_pairs={{0,480},{32,64},{64,32},{96,128},{128,96},{160,192},{192,160},{224... | collective-permute-start | bytes 786440 | tf_op jit(solution)/shard_map/ppermute | solution.py:62
  37.7 0.0 collective-permute-done.4
  37.7 0.1 dynamic-slice_add_fusion.1
  37.8 0.0 copy-start.1
  37.8 1.9 %collective-permute-start.5 = (f32[4,128,128]{2,1,0:T(8,128)S(1)}, f32[4,128,128]{2,1,0:T(8,128)S(1)}, u32[]{:S(2)}, u32[]{:S(2)}) collective-permute-start(f32[4,128,128]{2,1,0:T(8,128)S(1)} %get-tuple-element.14), channel_id=1, source_target_pairs={{0,32},{32,0},{64,96},{96,64},{128,160},{160,128},{192,224},{224,1... | collective-permute-start | bytes 786440 | tf_op jit(solution)/shard_map/ppermute | solution.py:62
  39.8 3.5 %collective-permute-done.1 = f32[4,128,128]{2,1,0:T(8,128)S(1)} collective-permute-done((f32[4,128,128]{2,1,0:T(8,128)}, f32[4,128,128]{2,1,0:T(8,128)S(1)}, u32[]{:S(2)}, u32[]{:S(2)}) %collective-permute-start.1) | collective-permute-done | bytes 262176 | tf_op jit(solution)/shard_map/ppermute | solution.py:62
  43.4 1.9 %collective-permute-start.2 = (f32[2,128,128]{2,1,0:T(8,128)S(1)}, f32[2,128,128]{2,1,0:T(8,128)S(1)}, u32[]{:S(2)}, u32[]{:S(2)}) collective-permute-start(f32[2,128,128]{2,1,0:T(8,128)S(1)} %get-tuple-element.16), channel_id=1, source_target_pairs={{0,96},{32,448},{64,160},{96,0},{128,224},{160,64},{192,288},{224,... | collective-permute-start | bytes 393224 | tf_op jit(solution)/shard_map/ppermute | solution.py:62
  45.3 1.3 collective-permute-done.5
  46.6 6.4 %collective-permute-start.6 = (f32[2,128,128]{2,1,0:T(8,128)S(1)}, f32[2,128,128]{2,1,0:T(8,128)S(1)}, u32[]{:S(2)}, u32[]{:S(2)}) collective-permute-start(f32[2,128,128]{2,1,0:T(8,128)S(1)} %get-tuple-element.18), channel_id=1, source_target_pairs={{0,416},{32,128},{64,480},{96,192},{128,32},{160,256},{192,96},{22... | collective-permute-start | bytes 393224 | tf_op jit(solution)/shard_map/ppermute | solution.py:62
  53.0 0.8 constant_dynamic-slice_fusion.2
  53.8 1.3 dynamic-slice
  55.7 0.0 collective-permute-done.2
  55.8 6.8 %collective-permute-start.3 = (f32[1,128,128]{2,1,0:T(8,128)S(1)}, f32[1,128,128]{2,1,0:T(8,128)S(1)}, u32[]{:S(2)}, u32[]{:S(2)}) collective-permute-start(f32[1,128,128]{2,1,0:T(8,128)S(1)} %dynamic-slice_add_fusion.9), channel_id=1, source_target_pairs={{0,352},{32,192},{64,416},{96,256},{128,480},{160,320},{192,32},{2... | collective-permute-start | bytes 196616 | tf_op jit(solution)/shard_map/ppermute | solution.py:62
  62.6 0.0 collective-permute-done.6
  62.6 5.2 %collective-permute-start.7 = (f32[1,128,128]{2,1,0:T(8,128)S(1)}, f32[1,128,128]{2,1,0:T(8,128)S(1)}, u32[]{:S(2)}, u32[]{:S(2)}) collective-permute-start(f32[1,128,128]{2,1,0:T(8,128)S(1)} %dynamic-slice_add_fusion.8), channel_id=1, source_target_pairs={{0,160},{32,384},{64,224},{96,448},{128,288},{160,0},{192,352},{22... | collective-permute-start | bytes 196616 | tf_op jit(solution)/shard_map/ppermute | solution.py:62
  67.8 0.1 collective-permute-done.3
  68.0 5.6 %collective-permute-done.7 = f32[1,128,128]{2,1,0:T(8,128)S(1)} collective-permute-done((f32[1,128,128]{2,1,0:T(8,128)S(1)}, f32[1,128,128]{2,1,0:T(8,128)S(1)}, u32[]{:S(2)}, u32[]{:S(2)}) %collective-permute-start.7) | collective-permute-done | bytes 65568 | tf_op jit(solution)/shard_map/ppermute | solution.py:62
  73.6 0.1 fusion
  73.7 8.8 %all-gather.4 = f32[8,2,128]{2,1,0:T(2,128)S(1)} all-gather(f32[1,2,128]{2,1,0:T(2,128)S(1)} %bitcast.173), channel_id=3, replica_groups=mesh['dp'=16,'row'=4,'col'=8] {'col'}, dimensions={0}, use_global_device_ids=true | all-gather | bytes 9216 | tf_op jit(solution)/shard_map/all_gather | solution.py:78
  82.5 0.1 fusion.7
  82.7 0.7 pad_maximum_fusion
  83.3 0.0 all-gather.8.cloned.1.call-update
  83.4 0.1 pad.12.clone
  83.4 0.1 maximum_maximum_fusion
  83.5 28.0 %all-gather.1 = f32[128,128]{1,0:T(8,128)S(1)} all-gather(f32[8,128]{1,0:T(8,128)S(1)} %maximum_maximum_fusion), channel_id=4, replica_groups=mesh['dp'=16,'row'=4,'col'=8] {'dp'}, dimensions={0}, use_global_device_ids=true | all-gather | bytes 69632 | tf_op jit(solution)/shard_map/all_gather | solution.py:84
  111.5 12.3 %all-gather.5 = f32[4,6,128]{2,1,0:T(8,128)S(1)} all-gather(f32[1,6,128]{2,1,0:T(8,128)S(1)} %bitcast.172), channel_id=5, replica_groups=mesh['dp'=16,'row'=4,'col'=8] {'row'}, dimensions={0}, use_global_device_ids=true | all-gather | bytes 15360 | tf_op jit(solution)/shard_map/all_gather | solution.py:89
  123.9 0.0 copy-start
  123.9 0.1 fusion.4
  124.0 0.2 dynamic-update-slice
  124.2 11.6 %all-reduce.1 = f32[16]{0:T(128)S(1)} all-reduce(f32[16]{0:T(128)S(1)} %dynamic-update-slice), channel_id=6, replica_groups=mesh['dp'=16,'row'=4,'col'=8] {'col'}, use_global_device_ids=true, to_apply=%add.1 | all-reduce | flops 16 | bytes 128
  135.8 0.1 reshape.60
  135.9 0.1 copy.9
  136.0 0.1 broadcast_reduce_fusion
  136.1 0.1 fusion.5
  136.4 0.1 fusion.2
  136.5 0.6 pad.4.left_ref
  137.1 0.6 pad_maximum_fusion.1
  137.7 14.6 %all-gather.8.cloned.1.call-done = f32[2,2048,128]{2,1,0:T(8,128)} async-done(((f32[2,128,128]{2,1,0:T(8,128)}), f32[2,2048,128]{2,1,0:T(8,128)}) %all-gather.8.cloned.1.call-update) | async-done | bytes 2097168 | tf_op jit(solution)/shard_map/all_gather | solution.py:144
  152.3 0.6 broadcast_in_dim.5.right_ref
  152.9 7.6 %shard_map.76 = f32[2,16,128,128]{3,2,1,0:T(8,128)} custom-call(s32[2,16]{1,0:T(2,128)} %constant.183.clone.table, f32[2,4,8,128]{3,2,1,0:T(8,128)} %pad.4.left_ref, f32[2,8,128]{2,1,0:T(8,128)} %broadcast_in_dim.5.right_ref, f32[2,16,128,128]{3,2,1,0:T(8,128)} %bitcast.141, f32[2,16,128,128]{3,2,1,0:T(8,128)} %bitcast.142, f32[2,16,128,128]{3,2,1,0:T(8,128)} %bitcast.143, ...), custom_call_target="tpu_custom_call" | custom-call | tf_op jit(solution)/shard_map/pallas_call | solution.py:121
  (32 shorter events, 0.3 us)
Async XLA Ops:
  7.2 145.2 %all-gather.8.cloned.1.call-start = ((), (), s32[]{:S(2)}) async-start(), calls=%async_computation | async-start | bytes 2228224 | tf_op jit(solution)/shard_map/all_gather | solution.py:144
  9.8 15.9 %collective-permute-start = (f32[8,128,128]{2,1,0:T(8,128)}, f32[8,128,128]{2,1,0:T(8,128)S(1)}, u32[]{:S(2)}, u32[]{:S(2)}) collective-permute-start(f32[8,128,128]{2,1,0:T(8,128)} %constant_dynamic-slice_fusion.1), channel_id=1, source_target_pairs={{0,32},{32,0},{64,96},{96,64},{128,160},{160,128},{192,224},{224,1... | collective-permute-start | bytes 1572872 | tf_op jit(solution)/shard_map/ppermute | solution.py:62
  14.5 23.2 %collective-permute-start.4 = (f32[8,128,128]{2,1,0:T(8,128)}, f32[8,128,128]{2,1,0:T(8,128)S(1)}, u32[]{:S(2)}, u32[]{:S(2)}) collective-permute-start(f32[8,128,128]{2,1,0:T(8,128)} %constant_dynamic-slice_fusion), channel_id=1, source_target_pairs={{0,480},{32,64},{64,32},{96,128},{128,96},{160,192},{192,160},{224... | collective-permute-start | bytes 1572872 | tf_op jit(solution)/shard_map/ppermute | solution.py:62
  26.5 16.8 %collective-permute-start.1 = (f32[4,128,128]{2,1,0:T(8,128)}, f32[4,128,128]{2,1,0:T(8,128)S(1)}, u32[]{:S(2)}, u32[]{:S(2)}) collective-permute-start(f32[4,128,128]{2,1,0:T(8,128)} %get-tuple-element.12), channel_id=1, source_target_pairs={{0,480},{32,64},{64,32},{96,128},{128,96},{160,192},{192,160},{224... | collective-permute-start | bytes 786440 | tf_op jit(solution)/shard_map/ppermute | solution.py:62
  37.8 86.0 %copy-start.1 = (f32[2,128]{1,0:T(2,128)S(1)}, f32[2,128]{1,0:T(2,128)}, u32[]{:S(2)}) copy-start(f32[2,128]{1,0:T(2,128)} %param.8) | copy-start | bytes 3076
  37.8 8.8 %collective-permute-start.5 = (f32[4,128,128]{2,1,0:T(8,128)S(1)}, f32[4,128,128]{2,1,0:T(8,128)S(1)}, u32[]{:S(2)}, u32[]{:S(2)}) collective-permute-start(f32[4,128,128]{2,1,0:T(8,128)S(1)} %get-tuple-element.14), channel_id=1, source_target_pairs={{0,32},{32,0},{64,96},{96,64},{128,160},{160,128},{192,224},{224,1... | collective-permute-start | bytes 786440 | tf_op jit(solution)/shard_map/ppermute | solution.py:62
  43.4 12.4 %collective-permute-start.2 = (f32[2,128,128]{2,1,0:T(8,128)S(1)}, f32[2,128,128]{2,1,0:T(8,128)S(1)}, u32[]{:S(2)}, u32[]{:S(2)}) collective-permute-start(f32[2,128,128]{2,1,0:T(8,128)S(1)} %get-tuple-element.16), channel_id=1, source_target_pairs={{0,96},{32,448},{64,160},{96,0},{128,224},{160,64},{192,288},{224,... | collective-permute-start | bytes 393224 | tf_op jit(solution)/shard_map/ppermute | solution.py:62
  46.6 16.0 %collective-permute-start.6 = (f32[2,128,128]{2,1,0:T(8,128)S(1)}, f32[2,128,128]{2,1,0:T(8,128)S(1)}, u32[]{:S(2)}, u32[]{:S(2)}) collective-permute-start(f32[2,128,128]{2,1,0:T(8,128)S(1)} %get-tuple-element.18), channel_id=1, source_target_pairs={{0,416},{32,128},{64,480},{96,192},{128,32},{160,256},{192,96},{22... | collective-permute-start | bytes 393224 | tf_op jit(solution)/shard_map/ppermute | solution.py:62
  55.8 12.2 %collective-permute-start.3 = (f32[1,128,128]{2,1,0:T(8,128)S(1)}, f32[1,128,128]{2,1,0:T(8,128)S(1)}, u32[]{:S(2)}, u32[]{:S(2)}) collective-permute-start(f32[1,128,128]{2,1,0:T(8,128)S(1)} %dynamic-slice_add_fusion.9), channel_id=1, source_target_pairs={{0,352},{32,192},{64,416},{96,256},{128,480},{160,320},{192,32},{2... | collective-permute-start | bytes 196616 | tf_op jit(solution)/shard_map/ppermute | solution.py:62
  62.6 11.0 %collective-permute-start.7 = (f32[1,128,128]{2,1,0:T(8,128)S(1)}, f32[1,128,128]{2,1,0:T(8,128)S(1)}, u32[]{:S(2)}, u32[]{:S(2)}) collective-permute-start(f32[1,128,128]{2,1,0:T(8,128)S(1)} %dynamic-slice_add_fusion.8), channel_id=1, source_target_pairs={{0,160},{32,384},{64,224},{96,448},{128,288},{160,0},{192,352},{22... | collective-permute-start | bytes 196616 | tf_op jit(solution)/shard_map/ppermute | solution.py:62
  123.9 36.7 %copy-start = (f32[2,128]{1,0:T(2,128)}, f32[2,128]{1,0:T(2,128)S(1)}, u32[]{:S(2)}) copy-start(f32[2,128]{1,0:T(2,128)S(1)} %get-tuple-element.6) | copy-start | bytes 3076
Sparse Core Ops, SparseCore 0:
  83.5 68.7 all-gather.7

commit v3 on v1

v3 whole, which is shorter than its diff:
```python
import functools

import jax
import jax.numpy as jnp
from jax import lax
from jax.experimental import pallas as pl
from jax.experimental.layout import Layout, with_layout_constraint
from jax.experimental.pallas import tpu as pltpu
from jax.sharding import PartitionSpec as P

D = 8192
KV = 1024

epsilon_one = 1e-30
decay_rate = 0.8
clip_limit = 1.0
step_size = 0.25

REACH = (1, -1, 3, -5)


def partner(r, step, size, core):
    r = (r - core) % size
    r = r + REACH[step] if r % 2 == 0 else r - REACH[step]
    return (r + core) % size


def owners(size):
    def reach(r, step):
        if step == len(REACH):
            return frozenset([r])
        return reach(r, step + 1) | reach(partner(r, step, size, 0), step + 1)

    place, spans = [0] * size, [frozenset(range(size))]
    for step in range(len(REACH)):
        spans = [half for span in spans for half in (reach(min(span), step + 1), span - reach(min(span), step + 1))]
    for position, span in enumerate(spans):
        (only,) = span
        place[only] = position
    return place


def lookup(table, index):
    words = [sum(v << (4 * i) for i, v in enumerate(table[k : k + 7])) for k in (0, 7, 14)]
    word = jnp.where(index < 7, words[0], jnp.where(index < 14, words[1], words[2]))
    part = jnp.where(index < 7, index, jnp.where(index < 14, index - 7, index - 14))
    return (word >> (4 * part)) & 15


def plain(x):
    return with_layout_constraint(x, Layout(major_to_minor=tuple(range(x.ndim))))


def exchange(x, target, size, cols):
    pairs = []
    for r in range(size):
        for c in range(cols):
            other, core = target(r, c % 2)
            pairs.append((r * cols + c, other * cols + c - c % 2 + core))
    return lax.ppermute(x, ("dp", "col"), pairs)


def halvings(x, label, size, cols):
    keep, base, count, arrived = x, jnp.int32(0), size, None
    for step in range(len(REACH)):
        count //= 2
        bit = (label // count) & 1
        go, stay = (1 - bit) * count, bit * count
        take = lambda a, at: lax.dynamic_slice_in_dim(a, at, count, axis=1)
        if arrived is None:
            out = take(keep, go)
            base = stay
        else:
            out = take(keep, base + go) + take(arrived, go)
        out = plain(out[:, 0] if count == 1 else out)
        landed = exchange(out, lambda r, core: (partner(r, step, size, core), core), size, cols)
        if arrived is not None:
            keep, base = take(keep, base + stay) + take(arrived, stay), jnp.int32(0)
        arrived = plain(landed)
    return lax.optimization_barrier(lax.dynamic_slice_in_dim(keep, base, 1, axis=1)[:, 0] + arrived)


def statistics(part, row_state, col_state, label, core, place, cols):
    mats, count, width = part.shape
    size = len(place)
    squares = part * part + epsilon_one
    old = lax.dynamic_slice(row_state, (0, label * count), (mats, count))
    row_part = lax.all_gather(jnp.sum(squares, axis=2), "col")
    row_part = row_part.reshape(cols // 2, 2, mats, count)
    own = jnp.sum(jnp.where(core == 0, row_part[:, 0], row_part[:, 1]), axis=0)
    other = exchange(own, lambda r, c: ((r + 1 - 2 * c) % size, 1 - c), size, cols)
    row_fresh = decay_rate * old + (1.0 - decay_rate) * ((own + other) / KV)
    col_part = jnp.sum(squares, axis=1)
    weighted = jnp.sum(squares * (1.0 / row_fresh)[:, :, None], axis=1)
    total = jnp.broadcast_to(jnp.sum(row_fresh, axis=1, keepdims=True), (mats, width))
    packed = jnp.concatenate([row_fresh, col_part, weighted, total], axis=0)
    everyone = lax.all_gather(packed, "dp")
    fresh = everyone[:, :mats]
    fresh = jnp.where(core == 0, fresh, jnp.roll(fresh, -1, axis=0))
    row_new = jnp.stack([fresh[place.index(b)] for b in range(size)], axis=1)
    sums = jnp.sum(everyone[:, mats:], axis=0)
    sums = jnp.sum(lax.all_gather(sums, "row"), axis=0)
    col_sum, weighted, total = sums[:mats], sums[mats : 2 * mats], sums[2 * mats :]
    row_total = total[:, 0]
    col_new = decay_rate * col_state + (1.0 - decay_rate) * (col_sum / D)
    share = jnp.sum(weighted / col_new, axis=1)
    share = jnp.broadcast_to(share[:, None], (mats, width))
    ratio = jnp.sum(lax.all_gather(share, "col"), axis=0)[:, 0]
    mean_square = ratio * (row_total / D) / (D * KV)
    divisor = jnp.maximum(1.0, jnp.sqrt(mean_square) / clip_limit)
    scale = step_size * jnp.sqrt(row_total / D) / divisor
    return row_new, col_new, scale


def finish_kernel(place, core_ref, left_ref, right_ref, weight_ref, summed_ref, out_ref, held, in_sem, out_sem):
    size = len(place)

    def arrival(b):
        source = (place.index(b) + core_ref[0]) & (size - 1)
        return pltpu.make_async_copy(summed_ref.at[source], held.at[:, b], in_sem.at[b])

    def departure(b):
        return pltpu.make_async_copy(held.at[:, b], out_ref.at[:, b], out_sem.at[b])

    for b in range(size):
        arrival(b).start()
    mats = weight_ref.shape[0]
    columns = [jnp.transpose(left_ref[m]) for m in range(mats)]
    for b in range(size):
        arrival(b).wait()
        for m in range(mats):
            factor = columns[m][:, b : b + 1] * right_ref[m : m + 1]
            held[m, b] = weight_ref[m, b] - held[m, b] * factor
        departure(b).start()
    for b in range(size):
        departure(b).wait()


def finish(summed, weight, left, right, core, place):
    whole = lambda space: pl.BlockSpec(memory_space=space)
    return pl.pallas_call(
        functools.partial(finish_kernel, place),
        in_specs=[whole(pltpu.SMEM)] + [whole(pltpu.VMEM)] * 3 + [whole(pltpu.HBM)],
        out_specs=whole(pltpu.HBM),
        out_shape=jax.ShapeDtypeStruct(weight.shape, weight.dtype),
        scratch_shapes=[
            pltpu.VMEM(weight.shape, weight.dtype),
            pltpu.SemaphoreType.DMA((len(place),)),
            pltpu.SemaphoreType.DMA((len(place),)),
        ],
        compiler_params=pltpu.CompilerParams(vmem_limit_bytes=60 << 20),
        cost_estimate=pl.CostEstimate(flops=2**21, bytes_accessed=6 * 2**20, transcendentals=0),
    )(core.reshape(1), left, right, weight, summed)


def local(gradients, weight, row_state, col_state):
    mats, rows, width = weight.shape
    size, cols = lax.axis_size("dp"), lax.axis_size("col")
    place = owners(size)
    core = lax.axis_index("col") & 1
    label = lookup(place, (lax.axis_index("dp") - core) & (size - 1))
    blocks = lambda a: a.reshape(mats, size, rows // size, width)
    part = halvings(blocks(gradients), label, size, cols)
    summed = lax.all_gather(part, "dp")
    row_new, col_new, scale = statistics(part, row_state, col_state, label, core, place, cols)
    left = scale[:, None, None] * lax.rsqrt(row_new)
    right = lax.rsqrt(col_new)
    new_weight = finish(summed, blocks(weight), left, right, core, place).reshape(weight.shape)
    return (new_weight, row_new.reshape(mats, rows), col_new)


def solution(mesh):
    in_specs = (P("dp", None, "row", "col"), P(None, "row", "col"), P(None, "row"), P(None, "col"))
    out_specs = (P(None, "row", "col"), P(None, "row"), P(None, "col"))
    return jax.shard_map(local, mesh=mesh, in_specs=in_specs, out_specs=out_specs, check_vma=False)
```

time: 172 us -> 166 us (0.965); the launches traced: 169 us -> 166 us
  waiting for transfers between devices: 71.8 us -> 39.4 us
  starting transfers between devices: 0.08 us -> 30.2 us
  blocking collectives: 73.5 us -> 64.9 us
  Pallas kernels: 0 us -> 5.14 us
  local copies, waits for them, and re-layouts: 1.77 us -> 3.95 us
    reduce_scatter x1 -> x0, waiting for transfers between devices: 71.1 us -> none  [local(): part = lax.psum_scatter(mine, 'dp', scatter_dimension=1, tiled=True)]
    ppermute x0 -> x5, waiting for transfers between devices: none -> 39.3 us  [exchange(): return lax.ppermute(x, ('dp', 'col'), pairs)]
    ppermute x0 -> x5, starting transfers between devices: none -> 30.2 us  [exchange(): return lax.ppermute(x, ('dp', 'col'), pairs)]
    all_gather x1, blocking collectives: 21.4 us -> 11.9 us  [statistics(): row_part = lax.all_gather(jnp.sum(squares, axis=2), 'col')]
    pallas_call x0 -> x1, Pallas kernels: none -> 5.14 us  [finish(): pl.pallas_call(functools.partial(finish_kernel, place), in_specs=[whole(p...]
    sub x1 -> x0, other arithmetic: 2.9 us -> none  [local(): new_weight = weight - summed * left[:, :, None] * right[:, None, :]]
    unnamed x1, blocking collectives: 19.7 us -> 22 us
    dynamic_slice x0 -> x1, other arithmetic: none -> 2.14 us  [halvings(): take = lambda a, at: lax.dynamic_slice_in_dim(a, at, count, axis=1)]
  transfers between devices with their start and end apart: 2 -> 6, of which waited for: 1 -> 4; matrix products, arithmetic and copies ran while one was open for 3% -> 4% of each run, Pallas kernels for 0% -> 0%
where the time goes in v3:
time: 166 us
  blocking collectives  64.9 us (39%)
  waiting for transfers between devices  39.4 us (24%)
  starting transfers between devices  30.2 us (18%)
  between operations  14.9 us (9%)
  other arithmetic  7.51 us (5%)
  Pallas kernels  5.14 us (3%)
  local copies, waits for them, and re-layouts  3.95 us (2%)
    ppermute x5, waiting for transfers between devices, exchange(): return lax.ppermute(x, ('dp', 'col'), pairs)  39.3 us
    ppermute x5, starting transfers between devices, exchange(): return lax.ppermute(x, ('dp', 'col'), pairs)  30.2 us
    unnamed x1, blocking collectives  22 us
    all_gather x1, blocking collectives, statistics(): everyone = lax.all_gather(packed, 'dp')  21.6 us
    all_gather x1, blocking collectives, statistics(): row_part = lax.all_gather(jnp.sum(squares, axis=2), 'col')  11.9 us
    all_gather x1, blocking collectives, statistics(): sums = jnp.sum(lax.all_gather(sums, 'row'), axis=0)  9.42 us
    pallas_call x1, Pallas kernels, finish(): pl.pallas_call(functools.partial(finish_kernel, place), in_specs=[whole(p...  5.14 us
  transfers between devices with their start and end apart: 6, of which 4 were waited for; matrix products, arithmetic and copies ran while one was open for 4% of the time, Pallas kernels for 0%

profile of v3, /device:TPU:1, one launch (start us, length us, event | category | flops | bytes accessed | tf_op | source)
XLA Modules:
  0.0 166.0 jit_solution(11069611993167896585)
XLA Ops:
  7.2 0.0 copy-start
  7.2 0.0 all-gather.9.cloned.1.call-start
  7.3 1.4 constant_dynamic-slice_fusion.3
  8.7 12.0 %collective-permute-start = (f32[2,8,128,128]{3,2,1,0:T(8,128)S(1)}, f32[2,8,128,128]{3,2,1,0:T(8,128)}, u32[]{:S(2)}, u32[]{:S(2)}) collective-permute-start(f32[2,8,128,128]{3,2,1,0:T(8,128)S(1)} %constant_dynamic-slice_fusion.3), channel_id=1, source_target_pairs={{0,32},{1,481},{2,34},{3,483},{4,36},{5,485},{6,38},{7,487},{32,0}... | collective-permute-start | bytes 3145736 | tf_op jit(solution)/shard_map/ppermute | solution.py:60
  20.7 12.3 %collective-permute-done = f32[2,8,128,128]{3,2,1,0:T(8,128)} collective-permute-done((f32[2,8,128,128]{3,2,1,0:T(8,128)S(1)}, f32[2,8,128,128]{3,2,1,0:T(8,128)}, u32[]{:S(2)}, u32[]{:S(2)}) %collective-permute-start) | collective-permute-done | bytes 1048608 | tf_op jit(solution)/shard_map/ppermute | solution.py:60
  32.9 0.0 copy-done
  32.9 2.1 %constant_dynamic-slice_fusion.4 = (f32[2,4,128,128]{3,2,1,0:T(8,128)S(1)}, f32[2,4,128,128]{3,2,1,0:T(8,128)}, f32[2,4,128,128]{3,2,1,0:T(8,128)S(1)}) fusion(f32[2,16,128,128]{3,2,1,0:T(8,128)S(1)} %bitcast.77, s32[]{:T(128)S(6)} %select_n.85, f32[2,8,128,128]{3,2,1,0:T(8,128)} %collective-permute-done, s32[]{:T(128)S(6)} %select_n.91, s32[]{:T(128)S(6)} %select_n.90, ...), kind=kLoop, calls=%fused_computation.25 | loop fusion | flops 131072 | bytes 3670032 | tf_op jit(solution)/shard_map/dynamic_slice | solution.py:69
  35.1 1.9 %collective-permute-start.1 = (f32[2,4,128,128]{3,2,1,0:T(8,128)}, f32[2,4,128,128]{3,2,1,0:T(8,128)S(1)}, u32[]{:S(2)}, u32[]{:S(2)}) collective-permute-start(f32[2,4,128,128]{3,2,1,0:T(8,128)} %get-tuple-element.10), channel_id=1, source_target_pairs={{0,480},{1,33},{2,482},{3,35},{4,484},{5,37},{6,486},{7,39},{32,64... | collective-permute-start | bytes 1572872 | tf_op jit(solution)/shard_map/ppermute | solution.py:60
  37.0 0.1 copy_add_fusion
  37.1 8.4 %collective-permute-done.1 = f32[2,4,128,128]{3,2,1,0:T(8,128)S(1)} collective-permute-done((f32[2,4,128,128]{3,2,1,0:T(8,128)}, f32[2,4,128,128]{3,2,1,0:T(8,128)S(1)}, u32[]{:S(2)}, u32[]{:S(2)}) %collective-permute-start.1) | collective-permute-done | bytes 524320 | tf_op jit(solution)/shard_map/ppermute | solution.py:60
  45.5 0.0 copy-start.2
  45.6 0.1 copy_add_fusion.2
  45.7 4.7 %collective-permute-start.2 = (f32[2,2,128,128]{3,2,1,0:T(8,128)S(1)}, f32[2,2,128,128]{3,2,1,0:T(8,128)S(1)}, u32[]{:S(2)}, u32[]{:S(2)}) collective-permute-start(f32[2,2,128,128]{3,2,1,0:T(8,128)S(1)} %copy.79), channel_id=1, source_target_pairs={{0,96},{1,417},{2,98},{3,419},{4,100},{5,421},{6,102},{7,423},{32,... | collective-permute-start | bytes 786440 | tf_op jit(solution)/shard_map/ppermute | solution.py:60
  50.4 8.9 %collective-permute-done.2 = f32[2,2,128,128]{3,2,1,0:T(8,128)S(1)} collective-permute-done((f32[2,2,128,128]{3,2,1,0:T(8,128)S(1)}, f32[2,2,128,128]{3,2,1,0:T(8,128)S(1)}, u32[]{:S(2)}, u32[]{:S(2)}) %collective-permute-start.2) | collective-permute-done | bytes 262176 | tf_op jit(solution)/shard_map/ppermute | solution.py:60
  59.4 6.8 %collective-permute-start.3 = (f32[2,128,128]{2,1,0:T(8,128)S(1)}, f32[2,128,128]{2,1,0:T(8,128)S(1)}, u32[]{:S(2)}, u32[]{:S(2)}) collective-permute-start(f32[2,128,128]{2,1,0:T(8,128)S(1)} %fusion), channel_id=1, source_target_pairs={{0,352},{1,161},{2,354},{3,163},{4,356},{5,165},{6,358},{7,167},{3... | collective-permute-start | bytes 393224 | tf_op jit(solution)/shard_map/ppermute | solution.py:60
  66.1 9.7 %collective-permute-done.3 = f32[2,128,128]{2,1,0:T(8,128)S(1)} collective-permute-done((f32[2,128,128]{2,1,0:T(8,128)S(1)}, f32[2,128,128]{2,1,0:T(8,128)S(1)}, u32[]{:S(2)}, u32[]{:S(2)}) %collective-permute-start.3) | collective-permute-done | bytes 131104 | tf_op jit(solution)/shard_map/ppermute | solution.py:60
  75.8 0.7 fusion.2
  76.5 0.0 all-gather.9.cloned.1.call-update
  76.5 1.0 fusion.4
  77.6 11.9 %all-gather.5 = f32[8,2,128]{2,1,0:T(2,128)S(1)} all-gather(f32[1,2,128]{2,1,0:T(2,128)S(1)} %bitcast.89), channel_id=3, replica_groups=mesh['dp'=16,'row'=4,'col'=8] {'col'}, dimensions={0}, use_global_device_ids=true | all-gather | bytes 9216 | tf_op jit(solution)/shard_map/all_gather | solution.py:88
  89.5 4.8 %collective-permute-start.4 = (f32[2,128]{1,0:T(2,128)S(1)}, f32[2,128]{1,0:T(2,128)S(1)}, u32[]{:S(2)}, u32[]{:S(2)}) collective-permute-start(f32[2,128]{1,0:T(2,128)S(1)} %fusion.5), channel_id=1, source_target_pairs={{0,33},{1,480},{2,35},{3,482},{4,37},{5,484},{6,39},{7,486},{32,65... | collective-permute-start | bytes 3080 | tf_op jit(solution)/shard_map/ppermute | solution.py:60
  94.3 1.3 dynamic-slice
  96.3 0.0 collective-permute-done.4
  96.3 0.8 fusion.11
  97.1 0.1 pad.5.clone
  97.2 1.0 fusion.3
  98.2 0.1 maximum_maximum_fusion
  98.2 21.6 %all-gather.1 = f32[128,128]{1,0:T(8,128)S(1)} all-gather(f32[8,128]{1,0:T(8,128)S(1)} %maximum_maximum_fusion), channel_id=4, replica_groups=mesh['dp'=16,'row'=4,'col'=8] {'dp'}, dimensions={0}, use_global_device_ids=true | all-gather | bytes 69632 | tf_op jit(solution)/shard_map/all_gather | solution.py:97
  119.9 9.4 %all-gather.6 = f32[4,6,128]{2,1,0:T(8,128)S(1)} all-gather(f32[1,6,128]{2,1,0:T(8,128)S(1)} %bitcast.87), channel_id=5, replica_groups=mesh['dp'=16,'row'=4,'col'=8] {'row'}, dimensions={0}, use_global_device_ids=true | all-gather | bytes 15360 | tf_op jit(solution)/shard_map/all_gather | solution.py:102
  129.3 0.0 copy-done.2
  129.3 0.6 fusion.10
  129.9 0.0 copy-start.1
  129.9 0.1 fusion.8
  130.0 0.2 dynamic-update-slice
  130.3 22.0 %all-reduce = f32[16]{0:T(128)S(1)} all-reduce(f32[16]{0:T(128)S(1)} %dynamic-update-slice), channel_id=6, replica_groups=mesh['dp'=16,'row'=4,'col'=8] {'col'}, use_global_device_ids=true, to_apply=%add | all-reduce | flops 16 | bytes 128
  152.2 0.1 reshape.67
  152.3 0.1 copy.82
  152.5 0.1 stack.3
  152.5 0.6 copy.110
  153.1 0.1 broadcast_reduce_fusion
  153.2 0.1 fusion.9
  153.3 0.7 rsqrt_multiply_fusion.left_ref
  154.0 0.0 all-gather.9.cloned.1.call-done
  154.0 5.1 %shard_map.67 = f32[2,16,128,128]{3,2,1,0:T(8,128)} custom-call(s32[1]{0:T(128)} %bitcast.core_ref, f32[2,16,128]{2,1,0:T(8,128)} %rsqrt_multiply_fusion.left_ref, f32[2,128]{1,0:T(2,128)} %get-tuple-element.5.right_ref, f32[2,16,128,128]{3,2,1,0:T(8,128)} %bitcast.78, f32[16,2,128,128]{3,2,1,0:T(8,128)} %bitcast.79), custom_call_target="tpu_custom_call" | custom-call | flops 2097152 | bytes 6291456 | tf_op jit(solution)/shard_map/pallas_call | solution.py:141
  159.2 0.0 copy-done.1
  (12 shorter events, 0.1 us)
Async XLA Ops:
  7.2 25.8 %copy-start = (f32[1,2,2048,128]{3,2,1,0:T(8,128)S(1)}, f32[1,2,2048,128]{3,2,1,0:T(8,128)}, u32[]{:S(2)}) copy-start(f32[1,2,2048,128]{3,2,1,0:T(8,128)} %param.4) | copy-start | bytes 6291460
  7.2 146.9 %all-gather.9.cloned.1.call-start = ((), (), s32[]{:S(2)}) async-start(), calls=%async_computation | async-start | bytes 2228224 | tf_op jit(solution)/shard_map/all_gather | solution.py:164
  8.7 24.2 %collective-permute-start = (f32[2,8,128,128]{3,2,1,0:T(8,128)S(1)}, f32[2,8,128,128]{3,2,1,0:T(8,128)}, u32[]{:S(2)}, u32[]{:S(2)}) collective-permute-start(f32[2,8,128,128]{3,2,1,0:T(8,128)S(1)} %constant_dynamic-slice_fusion.3), channel_id=1, source_target_pairs={{0,32},{1,481},{2,34},{3,483},{4,36},{5,485},{6,38},{7,487},{32,0}... | collective-permute-start | bytes 3145736 | tf_op jit(solution)/shard_map/ppermute | solution.py:60
  35.1 10.4 %collective-permute-start.1 = (f32[2,4,128,128]{3,2,1,0:T(8,128)}, f32[2,4,128,128]{3,2,1,0:T(8,128)S(1)}, u32[]{:S(2)}, u32[]{:S(2)}) collective-permute-start(f32[2,4,128,128]{3,2,1,0:T(8,128)} %get-tuple-element.10), channel_id=1, source_target_pairs={{0,480},{1,33},{2,482},{3,35},{4,484},{5,37},{6,486},{7,39},{32,64... | collective-permute-start | bytes 1572872 | tf_op jit(solution)/shard_map/ppermute | solution.py:60
  45.5 83.8 %copy-start.2 = (f32[2,128]{1,0:T(2,128)S(1)}, f32[2,128]{1,0:T(2,128)}, u32[]{:S(2)}) copy-start(f32[2,128]{1,0:T(2,128)} %param.7) | copy-start | bytes 3076
  45.7 13.7 %collective-permute-start.2 = (f32[2,2,128,128]{3,2,1,0:T(8,128)S(1)}, f32[2,2,128,128]{3,2,1,0:T(8,128)S(1)}, u32[]{:S(2)}, u32[]{:S(2)}) collective-permute-start(f32[2,2,128,128]{3,2,1,0:T(8,128)S(1)} %copy.79), channel_id=1, source_target_pairs={{0,96},{1,417},{2,98},{3,419},{4,100},{5,421},{6,102},{7,423},{32,... | collective-permute-start | bytes 786440 | tf_op jit(solution)/shard_map/ppermute | solution.py:60
  59.4 16.5 %collective-permute-start.3 = (f32[2,128,128]{2,1,0:T(8,128)S(1)}, f32[2,128,128]{2,1,0:T(8,128)S(1)}, u32[]{:S(2)}, u32[]{:S(2)}) collective-permute-start(f32[2,128,128]{2,1,0:T(8,128)S(1)} %fusion), channel_id=1, source_target_pairs={{0,352},{1,161},{2,354},{3,163},{4,356},{5,165},{6,358},{7,167},{3... | collective-permute-start | bytes 393224 | tf_op jit(solution)/shard_map/ppermute | solution.py:60
  89.5 6.8 %collective-permute-start.4 = (f32[2,128]{1,0:T(2,128)S(1)}, f32[2,128]{1,0:T(2,128)S(1)}, u32[]{:S(2)}, u32[]{:S(2)}) collective-permute-start(f32[2,128]{1,0:T(2,128)S(1)} %fusion.5), channel_id=1, source_target_pairs={{0,33},{1,480},{2,35},{3,482},{4,37},{5,484},{6,39},{7,486},{32,65... | collective-permute-start | bytes 3080 | tf_op jit(solution)/shard_map/ppermute | solution.py:60
  129.9 29.3 %copy-start.1 = (f32[2,128]{1,0:T(2,128)}, f32[2,128]{1,0:T(2,128)S(1)}, u32[]{:S(2)}) copy-start(f32[2,128]{1,0:T(2,128)S(1)} %get-tuple-element.6) | copy-start | bytes 3076
Sparse Core Ops, SparseCore 0:
  76.7 62.9 all-gather.8

commit v4 on v1

v4 whole, which is shorter than its diff:
```python
import functools

import jax
import jax.numpy as jnp
from jax import lax
from jax.experimental import pallas as pl
from jax.experimental.layout import Layout, with_layout_constraint
from jax.experimental.pallas import tpu as pltpu
from jax.sharding import PartitionSpec as P

D = 8192
KV = 1024

epsilon_one = 1e-30
decay_rate = 0.8
clip_limit = 1.0
step_size = 0.25

CLASSES = 4
HOPS = (2, 1, -1)
STEPS = (3, -5)
BACK = tuple(hop if hop % 2 else -hop for hop in HOPS)


def target(r, hop, size):
    return (r + hop if r % 2 == 0 else r - hop) % size


def owners(size):
    place, free = {}, 0
    for r in range(0, size, 2):
        if r not in place:
            other = target(r, STEPS[0], size)
            for q in (r, target(r, STEPS[1], size), other, target(other, STEPS[1], size)):
                place[q], free = free, free + 1
    return [place[r] for r in range(size)]


def lookup(table, index):
    words = [sum(v << (4 * i) for i, v in enumerate(table[k : k + 7])) for k in (0, 7, 14)]
    word = jnp.where(index < 7, words[0], jnp.where(index < 14, words[1], words[2]))
    part = jnp.where(index < 7, index, jnp.where(index < 14, index - 7, index - 14))
    return (word >> (4 * part)) & 15


def plain(x):
    return with_layout_constraint(x, Layout(major_to_minor=tuple(range(x.ndim))))


def reach(x, hop, size):
    return plain(lax.ppermute(plain(x), "dp", [(r, target(r, hop, size)) for r in range(size)]))


def spread(x, place, me):
    size = len(place)
    quarter = size // CLASSES
    mine = lookup(place, me)
    take = lambda which: lax.dynamic_slice_in_dim(x, which * quarter, quarter, axis=1)
    landed = [
        reach(take(lookup([place[target(r, hop, size)] // quarter for r in range(size)], me)), hop, size) for hop in HOPS
    ]
    held = plain(lax.optimization_barrier(take(mine // quarter) + landed[0] + landed[1] + landed[2]))
    half, last = (mine // 2) & 1, mine & 1
    two = lambda a, at: lax.dynamic_slice_in_dim(a, at, 2, axis=1)
    one = lambda a, at: lax.dynamic_index_in_dim(a, at, axis=1, keepdims=False)
    landed = reach(two(held, 2 - 2 * half), STEPS[0], size)
    out = one(held, 2 * half + 1 - last) + one(landed, 1 - last)
    keep = one(held, 2 * half + last) + one(landed, last)
    return lax.optimization_barrier(keep + reach(out, STEPS[1], size))


def join(own, other, bit):
    return jnp.where(bit == 0, jnp.concatenate([own, other]), jnp.concatenate([other, own]))


def pairs_of(part, place, me):
    return plain(join(part[None], reach(part, STEPS[1], len(place))[None], lookup(place, me) & 1))


def class_of(pair, place, me):
    return plain(join(pair, reach(pair, STEPS[0], len(place)), (lookup(place, me) // 2) & 1))


def after(x, other):
    return x + 0.0 * other[0, 0, : x.shape[0]]


def row_statistics(part, row_state, mine):
    mats, count, width = part.shape
    squares = part * part + epsilon_one
    old = lax.dynamic_slice(row_state, (0, mine * count), (mats, count))
    row_sum = jnp.sum(lax.all_gather(jnp.sum(squares, axis=2), "col"), axis=0)
    row_fresh = decay_rate * old + (1.0 - decay_rate) * (row_sum / KV)
    col_part = jnp.sum(squares, axis=1)
    weighted = jnp.sum(squares * (1.0 / row_fresh)[:, :, None], axis=1)
    total = jnp.broadcast_to(jnp.sum(row_fresh, axis=1, keepdims=True), (mats, width))
    return jnp.concatenate([row_fresh, col_part, weighted, total], axis=0)


def col_statistics(sums, col_state):
    mats, width = col_state.shape
    sums = jnp.sum(lax.all_gather(sums, "row"), axis=0)
    row_total = sums[2 * mats :, 0]
    col_new = decay_rate * col_state + (1.0 - decay_rate) * (sums[:mats] / D)
    shares = lax.all_gather(sums[mats : 2 * mats] / col_new, "col")
    ratio = jnp.sum(shares, axis=(0, 2))
    mean_square = ratio * (row_total / D) / (D * KV)
    divisor = jnp.maximum(1.0, jnp.sqrt(mean_square) / clip_limit)
    scale = step_size * jnp.sqrt(row_total / D) / divisor
    return col_new, scale


def finish_kernel(place, class_ref, scale_ref, every_ref, right_ref, weight_ref, *refs):
    parts, (out_ref, row_ref, held, left_ref, sems) = refs[:CLASSES], refs[CLASSES:]
    mats, _, blocks, rows, _ = weight_ref.shape
    for b in range(CLASSES * blocks):
        fresh = every_ref[place.index(b), 0:mats]
        row_ref[:, b] = fresh
        left_ref[b // blocks, b % blocks * mats : (b % blocks + 1) * mats] = lax.rsqrt(fresh)
    right = [right_ref[m : m + 1] * scale_ref[m] for m in range(mats)]
    copies = []
    for k in range(CLASSES):
        which = class_ref[k]
        columns = jnp.transpose(left_ref[which])
        for b in range(blocks):
            for m in range(mats):
                factor = columns[:, b * mats + m : b * mats + m + 1] * right[m]
                held[k, m, b] = weight_ref[m, which, b] - parts[k][b, m] * factor
        copies.append(pltpu.make_async_copy(held.at[k], out_ref.at[:, which], sems.at[k]))
        copies[-1].start()
    for copy in copies:
        copy.wait()


def finish(place, parts, weight, everyone, right, scale, classes):
    whole = lambda space: pl.BlockSpec(memory_space=space)
    mats, _, blocks, rows, width = weight.shape
    return pl.pallas_call(
        functools.partial(finish_kernel, place),
        in_specs=[whole(pltpu.SMEM)] * 2 + [whole(pltpu.VMEM)] * (3 + CLASSES),
        out_specs=[whole(pltpu.HBM), whole(pltpu.VMEM)],
        out_shape=[
            jax.ShapeDtypeStruct(weight.shape, weight.dtype),
            jax.ShapeDtypeStruct((mats, CLASSES * blocks, rows), weight.dtype),
        ],
        scratch_shapes=[
            pltpu.VMEM((CLASSES, mats, blocks, rows, width), weight.dtype),
            pltpu.VMEM((CLASSES, blocks * mats, rows), weight.dtype),
            pltpu.SemaphoreType.DMA((CLASSES,)),
        ],
        compiler_params=pltpu.CompilerParams(vmem_limit_bytes=20 << 20),
        cost_estimate=pl.CostEstimate(flops=2**21, bytes_accessed=6 * 2**20, transcendentals=0),
    )(classes, scale, everyone, right, weight, *parts)


def local(gradients, weight, row_state, col_state):
    mats, rows, width = weight.shape
    size, me = lax.axis_size("dp"), lax.axis_index("dp")
    blocks, count = size // CLASSES, rows // size
    place = owners(size)
    part = spread(gradients.reshape(mats, size, count, width), place, me)
    extra = row_statistics(part, row_state, lookup(place, me))
    pair = pairs_of(part, place, me)
    everyone = lax.all_gather(after(extra, pair), "dp")
    own = class_of(pair, place, me)
    parts = [own] + [reach(own, hop, size) for hop in BACK]
    col_new, scale = col_statistics(after(jnp.sum(everyone, axis=0)[mats:], own), col_state)
    classes = [lookup([p // blocks for p in place], me)]
    for hop in BACK:
        source = {target(r, hop, size): r for r in range(size)}
        classes.append(lookup([place[source[r]] // blocks for r in range(size)], me))
    split = weight.reshape(mats, CLASSES, blocks, count, width)
    new_weight, row_new = finish(place, parts, split, everyone, lax.rsqrt(col_new), scale, jnp.stack(classes))
    return (new_weight.reshape(weight.shape), row_new.reshape(mats, rows), col_new)


def solution(mesh):
    in_specs = (P("dp", None, "row", "col"), P(None, "row", "col"), P(None, "row"), P(None, "col"))
    out_specs = (P(None, "row", "col"), P(None, "row"), P(None, "col"))
    return jax.shard_map(local, mesh=mesh, in_specs=in_specs, out_specs=out_specs, check_vma=False)
```

time: 172 us -> 167 us (0.971); the launches traced: 169 us -> 166 us
  starting transfers between devices: 0.08 us -> 52.1 us
  waiting for transfers between devices: 71.8 us -> 37.1 us
  between operations: 14.8 us -> 0.98 us
  blocking collectives: 73.5 us -> 67.5 us
  other arithmetic: 6.8 us -> 2.9 us
  Pallas kernels: 0 us -> 3.38 us
    reduce_scatter x1 -> x0, waiting for transfers between devices: 71.1 us -> none  [local(): part = lax.psum_scatter(mine, 'dp', scatter_dimension=1, tiled=True)]
    ppermute x0 -> x10, starting transfers between devices: none -> 52.1 us  [reach(): lax.ppermute(plain(x), 'dp', [(r, target(r, hop, size)) for r in range(si...]
    ppermute x0 -> x10, waiting for transfers between devices: none -> 37.1 us  [reach(): lax.ppermute(plain(x), 'dp', [(r, target(r, hop, size)) for r in range(si...]
    unnamed x1 -> x0, blocking collectives: 19.7 us -> none
    all_gather x3 -> x4, blocking collectives: 53.8 us -> 67.5 us  [the longest x1 25.6 us: local(): everyone = lax.all_gather(after(extra, pair), 'dp')]
    pallas_call x0 -> x1, Pallas kernels: none -> 3.38 us  [finish(): pl.pallas_call(functools.partial(finish_kernel, place), in_specs=[whole(p...]
    sub x1 -> x0, other arithmetic: 2.9 us -> none  [local(): new_weight = weight - summed * left[:, :, None] * right[:, None, :]]
    reduce_sum x8 -> x7, other arithmetic: 3.08 us -> 1.19 us  [the longest x1 0.79 us: row_statistics(): jnp.sum(row_fresh, axis=1, keepdims=True)]
  transfers between devices with their start and end apart: 2 -> 10, of which waited for: 1 -> 4; matrix products, arithmetic and copies ran while one was open for 3% -> 1% of each run, Pallas kernels for 0% -> 0%
where the time goes in v4:
time: 167 us; the launch traced here: 166 us
  blocking collectives  67.5 us (40%)
  starting transfers between devices  52.1 us (31%)
  waiting for transfers between devices  37.1 us (22%)
  Pallas kernels  3.38 us (2%)
  other arithmetic  2.9 us (2%)
  local copies, waits for them, and re-layouts  2.21 us (1%)
    ppermute x10, starting transfers between devices, reach(): lax.ppermute(plain(x), 'dp', [(r, target(r, hop, size)) for r in range(si...  52.1 us
    ppermute x10, waiting for transfers between devices, reach(): lax.ppermute(plain(x), 'dp', [(r, target(r, hop, size)) for r in range(si...  37.1 us
    all_gather x1, blocking collectives, local(): everyone = lax.all_gather(after(extra, pair), 'dp')  25.6 us
    all_gather x1, blocking collectives, col_statistics(): shares = lax.all_gather(sums[mats:2 * mats] / col_new, 'col')  18.8 us
    all_gather x1, blocking collectives, row_statistics(): row_sum = jnp.sum(lax.all_gather(jnp.sum(squares, axis=2), 'col'), axis=0)  13.5 us
    all_gather x1, blocking collectives, col_statistics(): sums = jnp.sum(lax.all_gather(sums, 'row'), axis=0)  9.58 us
    pallas_call x1, Pallas kernels, finish(): pl.pallas_call(functools.partial(finish_kernel, place), in_specs=[whole(p...  3.38 us
  transfers between devices with their start and end apart: 10, of which 4 were waited for; matrix products, arithmetic and copies ran while one was open for 1% of the time, Pallas kernels for 0%

profile of v4, /device:TPU:1, one launch (start us, length us, event | category | flops | bytes accessed | tf_op | source)
XLA Modules:
  0.0 166.1 jit_solution(8529452205138412785)
XLA Ops:
  0.7 1.5 constant_dynamic-slice_fusion.3
  2.1 5.7 %collective-permute-start = (f32[2,4,128,128]{3,2,1,0:T(8,128)S(1)}, f32[2,4,128,128]{3,2,1,0:T(8,128)S(1)}, u32[]{:S(2)}, u32[]{:S(2)}) collective-permute-start(f32[2,4,128,128]{3,2,1,0:T(8,128)S(1)} %get-tuple-element.13), channel_id=1, source_target_pairs={{0,64},{32,480},{64,128},{96,32},{128,192},{160,96},{192,256},{224... | collective-permute-start | bytes 1572872 | tf_op jit(solution)/shard_map/ppermute | solution.py:51
  7.9 9.3 %collective-permute-start.2 = (f32[2,4,128,128]{3,2,1,0:T(8,128)S(1)}, f32[2,4,128,128]{3,2,1,0:T(8,128)S(1)}, u32[]{:S(2)}, u32[]{:S(2)}) collective-permute-start(f32[2,4,128,128]{3,2,1,0:T(8,128)S(1)} %get-tuple-element.14), channel_id=1, source_target_pairs={{0,480},{32,64},{64,32},{96,128},{128,96},{160,192},{192,160},{224... | collective-permute-start | bytes 1572872 | tf_op jit(solution)/shard_map/ppermute | solution.py:51
  17.2 1.9 %collective-permute-start.1 = (f32[2,4,128,128]{3,2,1,0:T(8,128)S(1)}, f32[2,4,128,128]{3,2,1,0:T(8,128)}, u32[]{:S(2)}, u32[]{:S(2)}) collective-permute-start(f32[2,4,128,128]{3,2,1,0:T(8,128)S(1)} %get-tuple-element.15), channel_id=1, source_target_pairs={{0,32},{32,0},{64,96},{96,64},{128,160},{160,128},{192,224},{224,1... | collective-permute-start | bytes 1572872 | tf_op jit(solution)/shard_map/ppermute | solution.py:51
  19.2 7.1 %collective-permute-done = f32[2,4,128,128]{3,2,1,0:T(8,128)S(1)} collective-permute-done((f32[2,4,128,128]{3,2,1,0:T(8,128)S(1)}, f32[2,4,128,128]{3,2,1,0:T(8,128)S(1)}, u32[]{:S(2)}, u32[]{:S(2)}) %collective-permute-start) | collective-permute-done | bytes 524320 | tf_op jit(solution)/shard_map/ppermute | solution.py:51
  26.2 11.9 %collective-permute-done.2 = f32[2,4,128,128]{3,2,1,0:T(8,128)S(1)} collective-permute-done((f32[2,4,128,128]{3,2,1,0:T(8,128)S(1)}, f32[2,4,128,128]{3,2,1,0:T(8,128)S(1)}, u32[]{:S(2)}, u32[]{:S(2)}) %collective-permute-start.2) | collective-permute-done | bytes 524320 | tf_op jit(solution)/shard_map/ppermute | solution.py:51
  38.2 0.0 collective-permute-done.1
  38.2 1.3 add_add_fusion
  39.5 0.0 copy-start.2
  39.5 0.0 copy-start
  39.5 2.1 %collective-permute-start.3 = (f32[2,2,128,128]{3,2,1,0:T(8,128)S(1)}, f32[2,2,128,128]{3,2,1,0:T(8,128)S(1)}, u32[]{:S(2)}, u32[]{:S(2)}) collective-permute-start(f32[2,2,128,128]{3,2,1,0:T(8,128)S(1)} %constant_dynamic-slice_fusion), channel_id=1, source_target_pairs={{0,96},{32,448},{64,160},{96,0},{128,224},{160,64},{192,288},{224,... | collective-permute-start | bytes 786440 | tf_op jit(solution)/shard_map/ppermute | solution.py:51
  41.6 14.0 %collective-permute-done.3 = f32[2,2,128,128]{3,2,1,0:T(8,128)S(1)} collective-permute-done((f32[2,2,128,128]{3,2,1,0:T(8,128)S(1)}, f32[2,2,128,128]{3,2,1,0:T(8,128)S(1)}, u32[]{:S(2)}, u32[]{:S(2)}) %collective-permute-start.3) | collective-permute-done | bytes 262176 | tf_op jit(solution)/shard_map/ppermute | solution.py:51
  55.6 8.7 %collective-permute-start.4 = (f32[2,128,128]{2,1,0:T(8,128)S(1)}, f32[2,128,128]{2,1,0:T(8,128)S(1)}, u32[]{:S(2)}, u32[]{:S(2)}) collective-permute-start(f32[2,128,128]{2,1,0:T(8,128)S(1)} %fusion), channel_id=1, source_target_pairs={{0,352},{32,192},{64,416},{96,256},{128,480},{160,320},{192,32},{2... | collective-permute-start | bytes 393224 | tf_op jit(solution)/shard_map/ppermute | solution.py:51
  64.3 0.1 pad_add_fusion.class_ref
  64.4 4.1 %collective-permute-done.4 = f32[2,128,128]{2,1,0:T(8,128)S(1)} collective-permute-done((f32[2,128,128]{2,1,0:T(8,128)S(1)}, f32[2,128,128]{2,1,0:T(8,128)S(1)}, u32[]{:S(2)}, u32[]{:S(2)}) %collective-permute-start.4) | collective-permute-done | bytes 131104 | tf_op jit(solution)/shard_map/ppermute | solution.py:51
  68.5 0.1 fusion.4
  68.6 10.3 %collective-permute-start.5 = (f32[2,128,128]{2,1,0:T(8,128)S(1)}, f32[2,128,128]{2,1,0:T(8,128)S(1)}, u32[]{:S(2)}, u32[]{:S(2)}) collective-permute-start(f32[2,128,128]{2,1,0:T(8,128)S(1)} %fusion.2), channel_id=1, source_target_pairs={{0,352},{32,192},{64,416},{96,256},{128,480},{160,320},{192,32},{2... | collective-permute-start | bytes 393224 | tf_op jit(solution)/shard_map/ppermute | solution.py:51
  78.9 13.5 %all-gather.3 = f32[8,2,128]{2,1,0:T(2,128)S(1)} all-gather(f32[1,2,128]{2,1,0:T(2,128)S(1)} %bitcast.61), channel_id=2, replica_groups=mesh['dp'=16,'row'=4,'col'=8] {'col'}, dimensions={0}, use_global_device_ids=true | all-gather | bytes 9216 | tf_op jit(solution)/shard_map/all_gather | solution.py:92
  92.4 0.8 fusion.14
  93.2 0.0 collective-permute-done.5
  93.2 4.3 %collective-permute-start.6 = (f32[2,2,128,128]{3,2,1,0:T(8,128)S(1)}, f32[2,2,128,128]{3,2,1,0:T(8,128)S(1)}, u32[]{:S(2)}, u32[]{:S(2)}) collective-permute-start(f32[2,2,128,128]{3,2,1,0:T(8,128)S(1)} %maximum_select_fusion.1), channel_id=1, source_target_pairs={{0,96},{32,448},{64,160},{96,0},{128,224},{160,64},{192,288},{224,... | collective-permute-start | bytes 786440 | tf_op jit(solution)/shard_map/ppermute | solution.py:51
  97.5 0.1 fusion.3
  97.6 0.1 pad.11.clone
  97.7 0.1 fusion.9
  97.8 25.6 %all_gather.24.every_ref = f32[16,8,128]{2,1,0:T(8,128)S(1)} all-gather(f32[1,8,128]{2,1,0:T(8,128)S(1)} %fusion.9), channel_id=1, replica_groups=mesh['dp'=16,'row'=4,'col'=8] {'dp'}, dimensions={0}, use_global_device_ids=true | all-gather | bytes 69632 | tf_op jit(solution)/shard_map/all_gather | solution.py:164
  123.4 0.0 collective-permute-done.6
  123.4 3.6 %collective-permute-start.8 = (f32[4,2,128,128]{3,2,1,0:T(8,128)S(1)}, f32[4,2,128,128]{3,2,1,0:T(8,128)S(1)}, u32[]{:S(2)}, u32[]{:S(2)}) collective-permute-start(f32[4,2,128,128]{3,2,1,0:T(8,128)S(1)} %maximum_select_fusion.refs_0_), channel_id=1, source_target_pairs={{0,32},{32,0},{64,96},{96,64},{128,160},{160,128},{192,224},{224,1... | collective-permute-start | bytes 1572872 | tf_op jit(solution)/shard_map/ppermute | solution.py:51
  127.0 3.1 %collective-permute-start.7 = (f32[4,2,128,128]{3,2,1,0:T(8,128)S(1)}, f32[4,2,128,128]{3,2,1,0:T(8,128)}, u32[]{:S(2)}, u32[]{:S(2)}) collective-permute-start(f32[4,2,128,128]{3,2,1,0:T(8,128)S(1)} %maximum_select_fusion.refs_0_), channel_id=1, source_target_pairs={{0,448},{32,96},{64,0},{96,160},{128,64},{160,224},{192,128},{224,... | collective-permute-start | bytes 1572872 | tf_op jit(solution)/shard_map/ppermute | solution.py:51
  130.1 3.1 %collective-permute-start.9 = (f32[4,2,128,128]{3,2,1,0:T(8,128)S(1)}, f32[4,2,128,128]{3,2,1,0:T(8,128)}, u32[]{:S(2)}, u32[]{:S(2)}) collective-permute-start(f32[4,2,128,128]{3,2,1,0:T(8,128)S(1)} %maximum_select_fusion.refs_0_), channel_id=1, source_target_pairs={{0,480},{32,64},{64,32},{96,128},{128,96},{160,192},{192,160},{224... | collective-permute-start | bytes 1572872 | tf_op jit(solution)/shard_map/ppermute | solution.py:51
  133.3 9.6 %all-gather.4 = f32[4,6,128]{2,1,0:T(8,128)S(1)} all-gather(f32[1,6,128]{2,1,0:T(8,128)S(1)} %fusion.7), channel_id=3, replica_groups=mesh['dp'=16,'row'=4,'col'=8] {'row'}, dimensions={0}, use_global_device_ids=true | all-gather | bytes 15360 | tf_op jit(solution)/shard_map/all_gather | solution.py:102
  142.9 0.0 copy-done.2
  142.9 0.0 copy-start.1
  142.9 18.8 %all-gather.5 = f32[8,2,128]{2,1,0:T(2,128)S(1)} all-gather(f32[1,2,128]{2,1,0:T(2,128)S(1)} %fusion.12), channel_id=4, replica_groups=mesh['dp'=16,'row'=4,'col'=8] {'col'}, dimensions={0}, use_global_device_ids=true | all-gather | bytes 9216 | tf_op jit(solution)/shard_map/all_gather | solution.py:105
  161.7 0.1 reduce_sum.79
  161.9 0.1 multiply_reduce_fusion.1
  162.0 0.0 collective-permute-done.8.refs_2_
  162.0 0.0 collective-permute-done.7.refs_1_
  162.0 0.0 collective-permute-done.9.refs_3_
  162.0 0.0 copy-done
  162.0 3.4 %shard_map.67 = (f32[2,4,4,128,128]{4,3,2,1,0:T(8,128)}, f32[2,16,128]{2,1,0:T(8,128)S(1)}) custom-call(s32[4]{0:T(128)S(1)} %pad_add_fusion.class_ref, f32[2]{0:T(128)S(1)} %maximum_divide_fusion.scale_ref, f32[16,8,128]{2,1,0:T(8,128)S(1)} %all_gather.24.every_ref, f32[2,128]{1,0:T(2,128)S(1)} %get-tuple-element.9.right_ref, ...), custom_call_target="tpu_custom_call" | custom-call | flops 2097152 | bytes 6291456 | tf_op jit(solution)/shard_map/pallas_call | solution.py:138
  165.4 0.0 copy-done.1
  165.4 0.6 copy.25
  (13 shorter events, 0.2 us)
Async XLA Ops:
  2.1 24.1 %collective-permute-start = (f32[2,4,128,128]{3,2,1,0:T(8,128)S(1)}, f32[2,4,128,128]{3,2,1,0:T(8,128)S(1)}, u32[]{:S(2)}, u32[]{:S(2)}) collective-permute-start(f32[2,4,128,128]{3,2,1,0:T(8,128)S(1)} %get-tuple-element.13), channel_id=1, source_target_pairs={{0,64},{32,480},{64,128},{96,32},{128,192},{160,96},{192,256},{224... | collective-permute-start | bytes 1572872 | tf_op jit(solution)/shard_map/ppermute | solution.py:51
  7.9 30.3 %collective-permute-start.2 = (f32[2,4,128,128]{3,2,1,0:T(8,128)S(1)}, f32[2,4,128,128]{3,2,1,0:T(8,128)S(1)}, u32[]{:S(2)}, u32[]{:S(2)}) collective-permute-start(f32[2,4,128,128]{3,2,1,0:T(8,128)S(1)} %get-tuple-element.14), channel_id=1, source_target_pairs={{0,480},{32,64},{64,32},{96,128},{128,96},{160,192},{192,160},{224... | collective-permute-start | bytes 1572872 | tf_op jit(solution)/shard_map/ppermute | solution.py:51
  17.2 21.0 %collective-permute-start.1 = (f32[2,4,128,128]{3,2,1,0:T(8,128)S(1)}, f32[2,4,128,128]{3,2,1,0:T(8,128)}, u32[]{:S(2)}, u32[]{:S(2)}) collective-permute-start(f32[2,4,128,128]{3,2,1,0:T(8,128)S(1)} %get-tuple-element.15), channel_id=1, source_target_pairs={{0,32},{32,0},{64,96},{96,64},{128,160},{160,128},{192,224},{224,1... | collective-permute-start | bytes 1572872 | tf_op jit(solution)/shard_map/ppermute | solution.py:51
  39.5 103.4 %copy-start.2 = (f32[2,128]{1,0:T(2,128)S(1)}, f32[2,128]{1,0:T(2,128)}, u32[]{:S(2)}) copy-start(f32[2,128]{1,0:T(2,128)} %param.7) | copy-start | bytes 3076
  39.5 122.6 %copy-start = (f32[2,2048,128]{2,1,0:T(8,128)S(1)}, f32[2,2048,128]{2,1,0:T(8,128)}, u32[]{:S(2)}) copy-start(f32[2,2048,128]{2,1,0:T(8,128)} %param.5) | copy-start | bytes 6291460
  39.5 16.1 %collective-permute-start.3 = (f32[2,2,128,128]{3,2,1,0:T(8,128)S(1)}, f32[2,2,128,128]{3,2,1,0:T(8,128)S(1)}, u32[]{:S(2)}, u32[]{:S(2)}) collective-permute-start(f32[2,2,128,128]{3,2,1,0:T(8,128)S(1)} %constant_dynamic-slice_fusion), channel_id=1, source_target_pairs={{0,96},{32,448},{64,160},{96,0},{128,224},{160,64},{192,288},{224,... | collective-permute-start | bytes 786440 | tf_op jit(solution)/shard_map/ppermute | solution.py:51
  55.6 12.8 %collective-permute-start.4 = (f32[2,128,128]{2,1,0:T(8,128)S(1)}, f32[2,128,128]{2,1,0:T(8,128)S(1)}, u32[]{:S(2)}, u32[]{:S(2)}) collective-permute-start(f32[2,128,128]{2,1,0:T(8,128)S(1)} %fusion), channel_id=1, source_target_pairs={{0,352},{32,192},{64,416},{96,256},{128,480},{160,320},{192,32},{2... | collective-permute-start | bytes 393224 | tf_op jit(solution)/shard_map/ppermute | solution.py:51
  68.6 24.6 %collective-permute-start.5 = (f32[2,128,128]{2,1,0:T(8,128)S(1)}, f32[2,128,128]{2,1,0:T(8,128)S(1)}, u32[]{:S(2)}, u32[]{:S(2)}) collective-permute-start(f32[2,128,128]{2,1,0:T(8,128)S(1)} %fusion.2), channel_id=1, source_target_pairs={{0,352},{32,192},{64,416},{96,256},{128,480},{160,320},{192,32},{2... | collective-permute-start | bytes 393224 | tf_op jit(solution)/shard_map/ppermute | solution.py:51
  93.2 30.1 %collective-permute-start.6 = (f32[2,2,128,128]{3,2,1,0:T(8,128)S(1)}, f32[2,2,128,128]{3,2,1,0:T(8,128)S(1)}, u32[]{:S(2)}, u32[]{:S(2)}) collective-permute-start(f32[2,2,128,128]{3,2,1,0:T(8,128)S(1)} %maximum_select_fusion.1), channel_id=1, source_target_pairs={{0,96},{32,448},{64,160},{96,0},{128,224},{160,64},{192,288},{224,... | collective-permute-start | bytes 786440 | tf_op jit(solution)/shard_map/ppermute | solution.py:51
  123.4 38.6 %collective-permute-start.8 = (f32[4,2,128,128]{3,2,1,0:T(8,128)S(1)}, f32[4,2,128,128]{3,2,1,0:T(8,128)S(1)}, u32[]{:S(2)}, u32[]{:S(2)}) collective-permute-start(f32[4,2,128,128]{3,2,1,0:T(8,128)S(1)} %maximum_select_fusion.refs_0_), channel_id=1, source_target_pairs={{0,32},{32,0},{64,96},{96,64},{128,160},{160,128},{192,224},{224,1... | collective-permute-start | bytes 1572872 | tf_op jit(solution)/shard_map/ppermute | solution.py:51
  127.0 35.0 %collective-permute-start.7 = (f32[4,2,128,128]{3,2,1,0:T(8,128)S(1)}, f32[4,2,128,128]{3,2,1,0:T(8,128)}, u32[]{:S(2)}, u32[]{:S(2)}) collective-permute-start(f32[4,2,128,128]{3,2,1,0:T(8,128)S(1)} %maximum_select_fusion.refs_0_), channel_id=1, source_target_pairs={{0,448},{32,96},{64,0},{96,160},{128,64},{160,224},{192,128},{224,... | collective-permute-start | bytes 1572872 | tf_op jit(solution)/shard_map/ppermute | solution.py:51
  130.1 31.9 %collective-permute-start.9 = (f32[4,2,128,128]{3,2,1,0:T(8,128)S(1)}, f32[4,2,128,128]{3,2,1,0:T(8,128)}, u32[]{:S(2)}, u32[]{:S(2)}) collective-permute-start(f32[4,2,128,128]{3,2,1,0:T(8,128)S(1)} %maximum_select_fusion.refs_0_), channel_id=1, source_target_pairs={{0,480},{32,64},{64,32},{96,128},{128,96},{160,192},{192,160},{224... | collective-permute-start | bytes 1572872 | tf_op jit(solution)/shard_map/ppermute | solution.py:51
  142.9 22.5 %copy-start.1 = (f32[2,128]{1,0:T(2,128)}, f32[2,128]{1,0:T(2,128)S(1)}, u32[]{:S(2)}) copy-start(f32[2,128]{1,0:T(2,128)S(1)} %get-tuple-element.10) | copy-start | bytes 3076

commit v5 on v4

--- a/solution.py
+++ b/solution.py
@@ -81,20 +81,16 @@
     return plain(join(pair, reach(pair, STEPS[0], len(place)), (lookup(place, me) // 2) & 1))
 
 
-def after(x, other):
-    return x + 0.0 * other[0, 0, : x.shape[0]]
-
-
-def row_statistics(part, row_state, mine):
-    mats, count, width = part.shape
-    squares = part * part + epsilon_one
-    old = lax.dynamic_slice(row_state, (0, mine * count), (mats, count))
-    row_sum = jnp.sum(lax.all_gather(jnp.sum(squares, axis=2), "col"), axis=0)
-    row_fresh = decay_rate * old + (1.0 - decay_rate) * (row_sum / KV)
-    col_part = jnp.sum(squares, axis=1)
-    weighted = jnp.sum(squares * (1.0 / row_fresh)[:, :, None], axis=1)
-    total = jnp.broadcast_to(jnp.sum(row_fresh, axis=1, keepdims=True), (mats, width))
-    return jnp.concatenate([row_fresh, col_part, weighted, total], axis=0)
+def class_statistics(own, row_state, which):
+    blocks, mats, count, width = own.shape
+    squares = own * own + epsilon_one
+    old = lax.dynamic_index_in_dim(row_state.reshape(mats, CLASSES, blocks, count), which, axis=1, keepdims=False)
+    row_sum = jnp.sum(lax.all_gather(jnp.sum(squares, axis=3), "col"), axis=0)
+    row_fresh = decay_rate * jnp.transpose(old, (1, 0, 2)) + (1.0 - decay_rate) * (row_sum / KV)
+    col_part = jnp.sum(squares, axis=(0, 2))
+    weighted = jnp.sum(squares * (1.0 / row_fresh)[..., None], axis=(0, 2))
+    total = jnp.broadcast_to(jnp.sum(row_fresh, axis=(0, 2))[:, None], (mats, width))
+    return jnp.concatenate([row_fresh.reshape(blocks * mats, width), col_part, weighted, total, jnp.zeros_like(total)])
 
 
 def col_statistics(sums, col_state):
@@ -110,18 +106,14 @@
     return col_new, scale
 
 
-def finish_kernel(place, class_ref, scale_ref, every_ref, right_ref, weight_ref, *refs):
-    parts, (out_ref, row_ref, held, left_ref, sems) = refs[:CLASSES], refs[CLASSES:]
+def finish_kernel(class_ref, scale_ref, small_ref, right_ref, weight_ref, *refs):
+    parts, (out_ref, held, sems) = refs[:CLASSES], refs[CLASSES:]
     mats, _, blocks, rows, _ = weight_ref.shape
-    for b in range(CLASSES * blocks):
-        fresh = every_ref[place.index(b), 0:mats]
-        row_ref[:, b] = fresh
-        left_ref[b // blocks, b % blocks * mats : (b % blocks + 1) * mats] = lax.rsqrt(fresh)
     right = [right_ref[m : m + 1] * scale_ref[m] for m in range(mats)]
     copies = []
     for k in range(CLASSES):
         which = class_ref[k]
-        columns = jnp.transpose(left_ref[which])
+        columns = jnp.transpose(lax.rsqrt(small_ref[k, 0 : blocks * mats]))
         for b in range(blocks):
             for m in range(mats):
                 factor = columns[:, b * mats + m : b * mats + m + 1] * right[m]
@@ -132,25 +124,21 @@
         copy.wait()
 
 
-def finish(place, parts, weight, everyone, right, scale, classes):
+def finish(parts, weight, smalls, right, scale, classes):
     whole = lambda space: pl.BlockSpec(memory_space=space)
     mats, _, blocks, rows, width = weight.shape
     return pl.pallas_call(
-        functools.partial(finish_kernel, place),
+        finish_kernel,
         in_specs=[whole(pltpu.SMEM)] * 2 + [whole(pltpu.VMEM)] * (3 + CLASSES),
-        out_specs=[whole(pltpu.HBM), whole(pltpu.VMEM)],
-        out_shape=[
-            jax.ShapeDtypeStruct(weight.shape, weight.dtype),
-            jax.ShapeDtypeStruct((mats, CLASSES * blocks, rows), weight.dtype),
-        ],
+        out_specs=whole(pltpu.HBM),
+        out_shape=jax.ShapeDtypeStruct(weight.shape, weight.dtype),
         scratch_shapes=[
             pltpu.VMEM((CLASSES, mats, blocks, rows, width), weight.dtype),
-            pltpu.VMEM((CLASSES, blocks * mats, rows), weight.dtype),
             pltpu.SemaphoreType.DMA((CLASSES,)),
         ],
         compiler_params=pltpu.CompilerParams(vmem_limit_bytes=20 << 20),
         cost_estimate=pl.CostEstimate(flops=2**21, bytes_accessed=6 * 2**20, transcendentals=0),
-    )(classes, scale, everyone, right, weight, *parts)
+    )(classes, scale, smalls, right, weight, *parts)
 
 
 def local(gradients, weight, row_state, col_state):
@@ -159,19 +147,23 @@
     blocks, count = size // CLASSES, rows // size
     place = owners(size)
     part = spread(gradients.reshape(mats, size, count, width), place, me)
-    extra = row_statistics(part, row_state, lookup(place, me))
-    pair = pairs_of(part, place, me)
-    everyone = lax.all_gather(after(extra, pair), "dp")
-    own = class_of(pair, place, me)
+    own = class_of(pairs_of(part, place, me), place, me)
     parts = [own] + [reach(own, hop, size) for hop in BACK]
-    col_new, scale = col_statistics(after(jnp.sum(everyone, axis=0)[mats:], own), col_state)
     classes = [lookup([p // blocks for p in place], me)]
     for hop in BACK:
         source = {target(r, hop, size): r for r in range(size)}
         classes.append(lookup([place[source[r]] // blocks for r in range(size)], me))
+    small = class_statistics(own, row_state, classes[0])
+    smalls = jnp.stack([small] + [reach(small, hop, size) for hop in BACK])
+    placed = jnp.stack(classes)[None, :] == jnp.arange(CLASSES)[:, None]
+    smalls_placed = jnp.sum(jnp.where(placed[:, :, None, None], smalls[None], 0.0), axis=1)
+    fresh = smalls_placed[:, : blocks * mats].reshape(size, mats, count)
+    sums = jnp.sum(smalls_placed[:, blocks * mats : (blocks + 3) * mats], axis=0)
+    col_new, scale = col_statistics(sums, col_state)
     split = weight.reshape(mats, CLASSES, blocks, count, width)
-    new_weight, row_new = finish(place, parts, split, everyone, lax.rsqrt(col_new), scale, jnp.stack(classes))
-    return (new_weight.reshape(weight.shape), row_new.reshape(mats, rows), col_new)
+    new_weight = finish(parts, split, smalls, lax.rsqrt(col_new), scale, jnp.stack(classes))
+    row_new = jnp.transpose(fresh, (1, 0, 2)).reshape(mats, rows)
+    return (new_weight.reshape(weight.shape), row_new, col_new)
 
 
 def solution(mesh):

time: 167 us -> 171 us (1.024)
  blocking collectives: 67.5 us -> 37.6 us
  starting transfers between devices: 52.1 us -> 75.3 us
  waiting for transfers between devices: 37.1 us -> 48.4 us
    all_gather x2 -> x1, blocking collectives: 39.1 us -> 13.6 us  [class_statistics(): row_sum = jnp.sum(lax.all_gather(jnp.sum(squares, axis=3), 'col'), axis=0)]
    ppermute x10 -> x13, starting transfers between devices: 52.1 us -> 75.3 us  [reach(): lax.ppermute(plain(x), 'dp', [(r, target(r, hop, size)) for r in range(si...]
    ppermute x10 -> x13, waiting for transfers between devices: 37.1 us -> 48.4 us  [reach(): lax.ppermute(plain(x), 'dp', [(r, target(r, hop, size)) for r in range(si...]
    all_gather x1, blocking collectives: 18.8 us -> 14.2 us  [col_statistics(): shares = lax.all_gather(sums[mats:2 * mats] / col_new, 'col')]
  transfers between devices with their start and end apart: 10 -> 13, of which waited for: 4 -> 6; matrix products, arithmetic and copies ran while one was open for 1% -> 1% of each run, Pallas kernels for 0% -> 0%
where the time goes in v5:
time: 171 us
  starting transfers between devices  75.3 us (44%)
  waiting for transfers between devices  48.4 us (28%)
  blocking collectives  37.6 us (22%)
  Pallas kernels  3.37 us (2%)
  other arithmetic  2.96 us (2%)
  local copies, waits for them, and re-layouts  2.22 us (1%)
    ppermute x13, starting transfers between devices, reach(): lax.ppermute(plain(x), 'dp', [(r, target(r, hop, size)) for r in range(si...  75.3 us
    ppermute x13, waiting for transfers between devices, reach(): lax.ppermute(plain(x), 'dp', [(r, target(r, hop, size)) for r in range(si...  48.4 us
    all_gather x1, blocking collectives, col_statistics(): shares = lax.all_gather(sums[mats:2 * mats] / col_new, 'col')  14.2 us
    all_gather x1, blocking collectives, class_statistics(): row_sum = jnp.sum(lax.all_gather(jnp.sum(squares, axis=3), 'col'), axis=0)  13.6 us
    all_gather x1, blocking collectives, col_statistics(): sums = jnp.sum(lax.all_gather(sums, 'row'), axis=0)  9.76 us
  transfers between devices with their start and end apart: 13, of which 6 were waited for; matrix products, arithmetic and copies ran while one was open for 1% of the time, Pallas kernels for 0%

profile of v5, /device:TPU:1, one launch (start us, length us, event | category | flops | bytes accessed | tf_op | source)
XLA Modules:
  0.0 170.8 jit_solution(16690351707427224956)
XLA Ops:
  0.7 1.5 constant_dynamic-slice_fusion.3
  2.1 5.7 %collective-permute-start = (f32[2,4,128,128]{3,2,1,0:T(8,128)S(1)}, f32[2,4,128,128]{3,2,1,0:T(8,128)S(1)}, u32[]{:S(2)}, u32[]{:S(2)}) collective-permute-start(f32[2,4,128,128]{3,2,1,0:T(8,128)S(1)} %get-tuple-element.11), channel_id=1, source_target_pairs={{0,64},{32,480},{64,128},{96,32},{128,192},{160,96},{192,256},{224... | collective-permute-start | bytes 1572872 | tf_op jit(solution)/shard_map/ppermute | solution.py:51
  7.9 9.3 %collective-permute-start.2 = (f32[2,4,128,128]{3,2,1,0:T(8,128)S(1)}, f32[2,4,128,128]{3,2,1,0:T(8,128)S(1)}, u32[]{:S(2)}, u32[]{:S(2)}) collective-permute-start(f32[2,4,128,128]{3,2,1,0:T(8,128)S(1)} %get-tuple-element.12), channel_id=1, source_target_pairs={{0,480},{32,64},{64,32},{96,128},{128,96},{160,192},{192,160},{224... | collective-permute-start | bytes 1572872 | tf_op jit(solution)/shard_map/ppermute | solution.py:51
  17.2 1.9 %collective-permute-start.1 = (f32[2,4,128,128]{3,2,1,0:T(8,128)S(1)}, f32[2,4,128,128]{3,2,1,0:T(8,128)S(1)}, u32[]{:S(2)}, u32[]{:S(2)}) collective-permute-start(f32[2,4,128,128]{3,2,1,0:T(8,128)S(1)} %get-tuple-element.13), channel_id=1, source_target_pairs={{0,32},{32,0},{64,96},{96,64},{128,160},{160,128},{192,224},{224,1... | collective-permute-start | bytes 1572872 | tf_op jit(solution)/shard_map/ppermute | solution.py:51
  19.2 7.1 %collective-permute-done = f32[2,4,128,128]{3,2,1,0:T(8,128)S(1)} collective-permute-done((f32[2,4,128,128]{3,2,1,0:T(8,128)S(1)}, f32[2,4,128,128]{3,2,1,0:T(8,128)S(1)}, u32[]{:S(2)}, u32[]{:S(2)}) %collective-permute-start) | collective-permute-done | bytes 524320 | tf_op jit(solution)/shard_map/ppermute | solution.py:51
  26.2 11.9 %collective-permute-done.2 = f32[2,4,128,128]{3,2,1,0:T(8,128)S(1)} collective-permute-done((f32[2,4,128,128]{3,2,1,0:T(8,128)S(1)}, f32[2,4,128,128]{3,2,1,0:T(8,128)S(1)}, u32[]{:S(2)}, u32[]{:S(2)}) %collective-permute-start.2) | collective-permute-done | bytes 524320 | tf_op jit(solution)/shard_map/ppermute | solution.py:51
  38.2 0.0 collective-permute-done.1
  38.2 1.1 add_add_fusion
  39.3 0.0 copy-start.2
  39.3 0.0 copy-start
  39.4 2.1 %collective-permute-start.3 = (f32[2,2,128,128]{3,2,1,0:T(8,128)S(1)}, f32[2,2,128,128]{3,2,1,0:T(8,128)S(1)}, u32[]{:S(2)}, u32[]{:S(2)}) collective-permute-start(f32[2,2,128,128]{3,2,1,0:T(8,128)S(1)} %constant_dynamic-slice_fusion), channel_id=1, source_target_pairs={{0,96},{32,448},{64,160},{96,0},{128,224},{160,64},{192,288},{224,... | collective-permute-start | bytes 786440 | tf_op jit(solution)/shard_map/ppermute | solution.py:51
  41.4 13.9 %collective-permute-done.3 = f32[2,2,128,128]{3,2,1,0:T(8,128)S(1)} collective-permute-done((f32[2,2,128,128]{3,2,1,0:T(8,128)S(1)}, f32[2,2,128,128]{3,2,1,0:T(8,128)S(1)}, u32[]{:S(2)}, u32[]{:S(2)}) %collective-permute-start.3) | collective-permute-done | bytes 262176 | tf_op jit(solution)/shard_map/ppermute | solution.py:51
  55.4 8.7 %collective-permute-start.4 = (f32[2,128,128]{2,1,0:T(8,128)S(1)}, f32[2,128,128]{2,1,0:T(8,128)S(1)}, u32[]{:S(2)}, u32[]{:S(2)}) collective-permute-start(f32[2,128,128]{2,1,0:T(8,128)S(1)} %fusion.2), channel_id=1, source_target_pairs={{0,352},{32,192},{64,416},{96,256},{128,480},{160,320},{192,32},{2... | collective-permute-start | bytes 393224 | tf_op jit(solution)/shard_map/ppermute | solution.py:51
  64.1 4.0 %collective-permute-done.4 = f32[2,128,128]{2,1,0:T(8,128)S(1)} collective-permute-done((f32[2,128,128]{2,1,0:T(8,128)S(1)}, f32[2,128,128]{2,1,0:T(8,128)S(1)}, u32[]{:S(2)}, u32[]{:S(2)}) %collective-permute-start.4) | collective-permute-done | bytes 131104 | tf_op jit(solution)/shard_map/ppermute | solution.py:51
  68.1 10.3 %collective-permute-start.5 = (f32[2,128,128]{2,1,0:T(8,128)S(1)}, f32[2,128,128]{2,1,0:T(8,128)S(1)}, u32[]{:S(2)}, u32[]{:S(2)}) collective-permute-start(f32[2,128,128]{2,1,0:T(8,128)S(1)} %fusion.4), channel_id=1, source_target_pairs={{0,352},{32,192},{64,416},{96,256},{128,480},{160,320},{192,32},{2... | collective-permute-start | bytes 393224 | tf_op jit(solution)/shard_map/ppermute | solution.py:51
  78.4 2.4 %collective-permute-done.5 = f32[2,128,128]{2,1,0:T(8,128)S(1)} collective-permute-done((f32[2,128,128]{2,1,0:T(8,128)S(1)}, f32[2,128,128]{2,1,0:T(8,128)S(1)}, u32[]{:S(2)}, u32[]{:S(2)}) %collective-permute-start.5) | collective-permute-done | bytes 131104 | tf_op jit(solution)/shard_map/ppermute | solution.py:51
  80.9 14.6 %collective-permute-start.6 = (f32[2,2,128,128]{3,2,1,0:T(8,128)S(1)}, f32[2,2,128,128]{3,2,1,0:T(8,128)S(1)}, u32[]{:S(2)}, u32[]{:S(2)}) collective-permute-start(f32[2,2,128,128]{3,2,1,0:T(8,128)S(1)} %maximum_select_fusion.1), channel_id=1, source_target_pairs={{0,96},{32,448},{64,160},{96,0},{128,224},{160,64},{192,288},{224,... | collective-permute-start | bytes 786440 | tf_op jit(solution)/shard_map/ppermute | solution.py:51
  95.5 0.1 pad_add_fusion.class_ref
  95.6 9.0 %collective-permute-done.6 = f32[2,2,128,128]{3,2,1,0:T(8,128)S(1)} collective-permute-done((f32[2,2,128,128]{3,2,1,0:T(8,128)S(1)}, f32[2,2,128,128]{3,2,1,0:T(8,128)S(1)}, u32[]{:S(2)}, u32[]{:S(2)}) %collective-permute-start.6) | collective-permute-done | bytes 262176 | tf_op jit(solution)/shard_map/ppermute | solution.py:51
  104.5 0.2 fusion.1
  104.8 13.6 %all-gather = f32[32,2,128]{2,1,0:T(2,128)S(1)} all-gather(f32[4,2,128]{2,1,0:T(2,128)S(1)} %get-tuple-element.9), channel_id=2, replica_groups=mesh['dp'=16,'row'=4,'col'=8] {'col'}, dimensions={0}, use_global_device_ids=true | all-gather | bytes 36864 | tf_op jit(solution)/shard_map/all_gather | solution.py:88
  118.4 0.8 fusion.7
  119.2 0.2 multiply_reduce_fusion
  119.5 0.1 broadcast_in_dim.43
  119.6 3.6 %collective-permute-start.8 = (f32[16,128]{1,0:T(8,128)S(1)}, f32[16,128]{1,0:T(8,128)S(1)}, u32[]{:S(2)}, u32[]{:S(2)}) collective-permute-start(f32[16,128]{1,0:T(8,128)S(1)} %concatenate.19), channel_id=1, source_target_pairs={{0,32},{32,0},{64,96},{96,64},{128,160},{160,128},{192,224},{224,1... | collective-permute-start | bytes 24584 | tf_op jit(solution)/shard_map/ppermute | solution.py:51
  123.2 7.6 %collective-permute-start.7 = (f32[16,128]{1,0:T(8,128)S(1)}, f32[16,128]{1,0:T(8,128)S(1)}, u32[]{:S(2)}, u32[]{:S(2)}) collective-permute-start(f32[16,128]{1,0:T(8,128)S(1)} %concatenate.19), channel_id=1, source_target_pairs={{0,448},{32,96},{64,0},{96,160},{128,64},{160,224},{192,128},{224,... | collective-permute-start | bytes 24584 | tf_op jit(solution)/shard_map/ppermute | solution.py:51
  130.9 1.9 %collective-permute-start.9 = (f32[16,128]{1,0:T(8,128)S(1)}, f32[16,128]{1,0:T(8,128)S(1)}, u32[]{:S(2)}, u32[]{:S(2)}) collective-permute-start(f32[16,128]{1,0:T(8,128)S(1)} %concatenate.19), channel_id=1, source_target_pairs={{0,480},{32,64},{64,32},{96,128},{128,96},{160,192},{192,160},{224... | collective-permute-start | bytes 24584 | tf_op jit(solution)/shard_map/ppermute | solution.py:51
  132.8 1.9 %collective-permute-start.11 = (f32[4,2,128,128]{3,2,1,0:T(8,128)S(1)}, f32[4,2,128,128]{3,2,1,0:T(8,128)S(1)}, u32[]{:S(2)}, u32[]{:S(2)}) collective-permute-start(f32[4,2,128,128]{3,2,1,0:T(8,128)S(1)} %get-tuple-element.10.refs_0_), channel_id=1, source_target_pairs={{0,32},{32,0},{64,96},{96,64},{128,160},{160,128},{192,224},{224,1... | collective-permute-start | bytes 1572872 | tf_op jit(solution)/shard_map/ppermute | solution.py:51
  134.7 5.7 %collective-permute-start.10 = (f32[4,2,128,128]{3,2,1,0:T(8,128)S(1)}, f32[4,2,128,128]{3,2,1,0:T(8,128)}, u32[]{:S(2)}, u32[]{:S(2)}) collective-permute-start(f32[4,2,128,128]{3,2,1,0:T(8,128)S(1)} %get-tuple-element.10.refs_0_), channel_id=1, source_target_pairs={{0,448},{32,96},{64,0},{96,160},{128,64},{160,224},{192,128},{224,... | collective-permute-start | bytes 1572872 | tf_op jit(solution)/shard_map/ppermute | solution.py:51
  140.5 0.0 collective-permute-done.8
  140.5 1.9 %collective-permute-start.12 = (f32[4,2,128,128]{3,2,1,0:T(8,128)S(1)}, f32[4,2,128,128]{3,2,1,0:T(8,128)}, u32[]{:S(2)}, u32[]{:S(2)}) collective-permute-start(f32[4,2,128,128]{3,2,1,0:T(8,128)S(1)} %get-tuple-element.10.refs_0_), channel_id=1, source_target_pairs={{0,480},{32,64},{64,32},{96,128},{128,96},{160,192},{192,160},{224... | collective-permute-start | bytes 1572872 | tf_op jit(solution)/shard_map/ppermute | solution.py:51
  142.4 0.0 collective-permute-done.7
  142.4 0.0 collective-permute-done.9
  142.5 0.1 select_reduce_fusion
  142.6 0.6 slice.21
  143.2 9.8 %all-gather.3 = f32[4,6,128]{2,1,0:T(8,128)S(1)} all-gather(f32[1,6,128]{2,1,0:T(8,128)S(1)} %bitcast.58), channel_id=3, replica_groups=mesh['dp'=16,'row'=4,'col'=8] {'row'}, dimensions={0}, use_global_device_ids=true | all-gather | bytes 15360 | tf_op jit(solution)/shard_map/all_gather | solution.py:98
  152.9 0.0 copy-done.2
  153.0 0.0 copy-start.1
  153.0 14.2 %all-gather.4 = f32[8,2,128]{2,1,0:T(2,128)S(1)} all-gather(f32[1,2,128]{2,1,0:T(2,128)S(1)} %fusion.5), channel_id=4, replica_groups=mesh['dp'=16,'row'=4,'col'=8] {'col'}, dimensions={0}, use_global_device_ids=true | all-gather | bytes 9216 | tf_op jit(solution)/shard_map/all_gather | solution.py:101
  167.2 0.1 reduce_sum.89
  167.3 0.1 multiply_reduce_fusion.1
  167.4 0.0 collective-permute-done.11.refs_2_
  167.4 0.0 collective-permute-done.10.refs_1_
  167.4 0.0 collective-permute-done.12.refs_3_
  167.5 0.0 copy-done
  167.5 3.4 %shard_map.67 = f32[2,4,4,128,128]{4,3,2,1,0:T(8,128)} custom-call(s32[4]{0:T(128)S(1)} %pad_add_fusion.class_ref, f32[2]{0:T(128)S(1)} %maximum_divide_fusion.scale_ref, f32[4,16,128]{2,1,0:T(8,128)S(1)} %pad_maximum_fusion.small_ref, f32[2,128]{1,0:T(2,128)S(1)} %get-tuple-element.5.right_ref, f32[2,4,4,128,128]{4,3,2,1,0:T(8,128)S(1)} %bitcast.49, ...), custom_call_target="tpu_custom_call" | custom-call | flops 2097152 | bytes 6291456 | tf_op jit(solution)/shard_map/pallas_call | solution.py:130
  170.8 0.0 copy-done.1
  (15 shorter events, 0.2 us)
Async XLA Ops:
  2.1 24.1 %collective-permute-start = (f32[2,4,128,128]{3,2,1,0:T(8,128)S(1)}, f32[2,4,128,128]{3,2,1,0:T(8,128)S(1)}, u32[]{:S(2)}, u32[]{:S(2)}) collective-permute-start(f32[2,4,128,128]{3,2,1,0:T(8,128)S(1)} %get-tuple-element.11), channel_id=1, source_target_pairs={{0,64},{32,480},{64,128},{96,32},{128,192},{160,96},{192,256},{224... | collective-permute-start | bytes 1572872 | tf_op jit(solution)/shard_map/ppermute | solution.py:51
  7.9 30.3 %collective-permute-start.2 = (f32[2,4,128,128]{3,2,1,0:T(8,128)S(1)}, f32[2,4,128,128]{3,2,1,0:T(8,128)S(1)}, u32[]{:S(2)}, u32[]{:S(2)}) collective-permute-start(f32[2,4,128,128]{3,2,1,0:T(8,128)S(1)} %get-tuple-element.12), channel_id=1, source_target_pairs={{0,480},{32,64},{64,32},{96,128},{128,96},{160,192},{192,160},{224... | collective-permute-start | bytes 1572872 | tf_op jit(solution)/shard_map/ppermute | solution.py:51
  17.2 21.0 %collective-permute-start.1 = (f32[2,4,128,128]{3,2,1,0:T(8,128)S(1)}, f32[2,4,128,128]{3,2,1,0:T(8,128)S(1)}, u32[]{:S(2)}, u32[]{:S(2)}) collective-permute-start(f32[2,4,128,128]{3,2,1,0:T(8,128)S(1)} %get-tuple-element.13), channel_id=1, source_target_pairs={{0,32},{32,0},{64,96},{96,64},{128,160},{160,128},{192,224},{224,1... | collective-permute-start | bytes 1572872 | tf_op jit(solution)/shard_map/ppermute | solution.py:51
  39.3 113.6 %copy-start.2 = (f32[2,128]{1,0:T(2,128)S(1)}, f32[2,128]{1,0:T(2,128)}, u32[]{:S(2)}) copy-start(f32[2,128]{1,0:T(2,128)} %param.7) | copy-start | bytes 3076
  39.3 128.1 %copy-start = (f32[2,2048,128]{2,1,0:T(8,128)S(1)}, f32[2,2048,128]{2,1,0:T(8,128)}, u32[]{:S(2)}) copy-start(f32[2,2048,128]{2,1,0:T(8,128)} %param.5) | copy-start | bytes 6291460
  39.4 16.0 %collective-permute-start.3 = (f32[2,2,128,128]{3,2,1,0:T(8,128)S(1)}, f32[2,2,128,128]{3,2,1,0:T(8,128)S(1)}, u32[]{:S(2)}, u32[]{:S(2)}) collective-permute-start(f32[2,2,128,128]{3,2,1,0:T(8,128)S(1)} %constant_dynamic-slice_fusion), channel_id=1, source_target_pairs={{0,96},{32,448},{64,160},{96,0},{128,224},{160,64},{192,288},{224,... | collective-permute-start | bytes 786440 | tf_op jit(solution)/shard_map/ppermute | solution.py:51
  55.4 12.7 %collective-permute-start.4 = (f32[2,128,128]{2,1,0:T(8,128)S(1)}, f32[2,128,128]{2,1,0:T(8,128)S(1)}, u32[]{:S(2)}, u32[]{:S(2)}) collective-permute-start(f32[2,128,128]{2,1,0:T(8,128)S(1)} %fusion.2), channel_id=1, source_target_pairs={{0,352},{32,192},{64,416},{96,256},{128,480},{160,320},{192,32},{2... | collective-permute-start | bytes 393224 | tf_op jit(solution)/shard_map/ppermute | solution.py:51
  68.1 12.7 %collective-permute-start.5 = (f32[2,128,128]{2,1,0:T(8,128)S(1)}, f32[2,128,128]{2,1,0:T(8,128)S(1)}, u32[]{:S(2)}, u32[]{:S(2)}) collective-permute-start(f32[2,128,128]{2,1,0:T(8,128)S(1)} %fusion.4), channel_id=1, source_target_pairs={{0,352},{32,192},{64,416},{96,256},{128,480},{160,320},{192,32},{2... | collective-permute-start | bytes 393224 | tf_op jit(solution)/shard_map/ppermute | solution.py:51
  80.9 23.7 %collective-permute-start.6 = (f32[2,2,128,128]{3,2,1,0:T(8,128)S(1)}, f32[2,2,128,128]{3,2,1,0:T(8,128)S(1)}, u32[]{:S(2)}, u32[]{:S(2)}) collective-permute-start(f32[2,2,128,128]{3,2,1,0:T(8,128)S(1)} %maximum_select_fusion.1), channel_id=1, source_target_pairs={{0,96},{32,448},{64,160},{96,0},{128,224},{160,64},{192,288},{224,... | collective-permute-start | bytes 786440 | tf_op jit(solution)/shard_map/ppermute | solution.py:51
  119.6 20.9 %collective-permute-start.8 = (f32[16,128]{1,0:T(8,128)S(1)}, f32[16,128]{1,0:T(8,128)S(1)}, u32[]{:S(2)}, u32[]{:S(2)}) collective-permute-start(f32[16,128]{1,0:T(8,128)S(1)} %concatenate.19), channel_id=1, source_target_pairs={{0,32},{32,0},{64,96},{96,64},{128,160},{160,128},{192,224},{224,1... | collective-permute-start | bytes 24584 | tf_op jit(solution)/shard_map/ppermute | solution.py:51
  123.2 19.2 %collective-permute-start.7 = (f32[16,128]{1,0:T(8,128)S(1)}, f32[16,128]{1,0:T(8,128)S(1)}, u32[]{:S(2)}, u32[]{:S(2)}) collective-permute-start(f32[16,128]{1,0:T(8,128)S(1)} %concatenate.19), channel_id=1, source_target_pairs={{0,448},{32,96},{64,0},{96,160},{128,64},{160,224},{192,128},{224,... | collective-permute-start | bytes 24584 | tf_op jit(solution)/shard_map/ppermute | solution.py:51
  130.9 11.6 %collective-permute-start.9 = (f32[16,128]{1,0:T(8,128)S(1)}, f32[16,128]{1,0:T(8,128)S(1)}, u32[]{:S(2)}, u32[]{:S(2)}) collective-permute-start(f32[16,128]{1,0:T(8,128)S(1)} %concatenate.19), channel_id=1, source_target_pairs={{0,480},{32,64},{64,32},{96,128},{128,96},{160,192},{192,160},{224... | collective-permute-start | bytes 24584 | tf_op jit(solution)/shard_map/ppermute | solution.py:51
  132.8 34.6 %collective-permute-start.11 = (f32[4,2,128,128]{3,2,1,0:T(8,128)S(1)}, f32[4,2,128,128]{3,2,1,0:T(8,128)S(1)}, u32[]{:S(2)}, u32[]{:S(2)}) collective-permute-start(f32[4,2,128,128]{3,2,1,0:T(8,128)S(1)} %get-tuple-element.10.refs_0_), channel_id=1, source_target_pairs={{0,32},{32,0},{64,96},{96,64},{128,160},{160,128},{192,224},{224,1... | collective-permute-start | bytes 1572872 | tf_op jit(solution)/shard_map/ppermute | solution.py:51
  134.7 32.7 %collective-permute-start.10 = (f32[4,2,128,128]{3,2,1,0:T(8,128)S(1)}, f32[4,2,128,128]{3,2,1,0:T(8,128)}, u32[]{:S(2)}, u32[]{:S(2)}) collective-permute-start(f32[4,2,128,128]{3,2,1,0:T(8,128)S(1)} %get-tuple-element.10.refs_0_), channel_id=1, source_target_pairs={{0,448},{32,96},{64,0},{96,160},{128,64},{160,224},{192,128},{224,... | collective-permute-start | bytes 1572872 | tf_op jit(solution)/shard_map/ppermute | solution.py:51
  140.5 27.0 %collective-permute-start.12 = (f32[4,2,128,128]{3,2,1,0:T(8,128)S(1)}, f32[4,2,128,128]{3,2,1,0:T(8,128)}, u32[]{:S(2)}, u32[]{:S(2)}) collective-permute-start(f32[4,2,128,128]{3,2,1,0:T(8,128)S(1)} %get-tuple-element.10.refs_0_), channel_id=1, source_target_pairs={{0,480},{32,64},{64,32},{96,128},{128,96},{160,192},{192,160},{224... | collective-permute-start | bytes 1572872 | tf_op jit(solution)/shard_map/ppermute | solution.py:51
  153.0 17.9 %copy-start.1 = (f32[2,128]{1,0:T(2,128)}, f32[2,128]{1,0:T(2,128)S(1)}, u32[]{:S(2)}) copy-start(f32[2,128]{1,0:T(2,128)S(1)} %get-tuple-element.6) | copy-start | bytes 3076

commit v6 on v4

--- a/solution.py
+++ b/solution.py
@@ -31,7 +31,7 @@
     for r in range(0, size, 2):
         if r not in place:
             other = target(r, STEPS[0], size)
-            for q in (r, target(r, STEPS[1], size), other, target(other, STEPS[1], size)):
+            for q in (target(r, STEPS[1], size), r, other, target(other, STEPS[1], size)):
                 place[q], free = free, free + 1
     return [place[r] for r in range(size)]
 
@@ -69,22 +69,6 @@
     return lax.optimization_barrier(keep + reach(out, STEPS[1], size))
 
 
-def join(own, other, bit):
-    return jnp.where(bit == 0, jnp.concatenate([own, other]), jnp.concatenate([other, own]))
-
-
-def pairs_of(part, place, me):
-    return plain(join(part[None], reach(part, STEPS[1], len(place))[None], lookup(place, me) & 1))
-
-
-def class_of(pair, place, me):
-    return plain(join(pair, reach(pair, STEPS[0], len(place)), (lookup(place, me) // 2) & 1))
-
-
-def after(x, other):
-    return x + 0.0 * other[0, 0, : x.shape[0]]
-
-
 def row_statistics(part, row_state, mine):
     mats, count, width = part.shape
     squares = part * part + epsilon_one
@@ -110,47 +94,39 @@
     return col_new, scale
 
 
-def finish_kernel(place, class_ref, scale_ref, every_ref, right_ref, weight_ref, *refs):
-    parts, (out_ref, row_ref, held, left_ref, sems) = refs[:CLASSES], refs[CLASSES:]
+def finish_kernel(class_ref, scale_ref, left_ref, right_ref, weight_ref, *refs):
+    parts, out_ref, held, sems = refs[:CLASSES], refs[CLASSES], refs[CLASSES + 1], refs[CLASSES + 2]
     mats, _, blocks, rows, _ = weight_ref.shape
-    for b in range(CLASSES * blocks):
-        fresh = every_ref[place.index(b), 0:mats]
-        row_ref[:, b] = fresh
-        left_ref[b // blocks, b % blocks * mats : (b % blocks + 1) * mats] = lax.rsqrt(fresh)
     right = [right_ref[m : m + 1] * scale_ref[m] for m in range(mats)]
     copies = []
     for k in range(CLASSES):
         which = class_ref[k]
-        columns = jnp.transpose(left_ref[which])
+        columns = jnp.transpose(left_ref[k])
         for b in range(blocks):
             for m in range(mats):
                 factor = columns[:, b * mats + m : b * mats + m + 1] * right[m]
-                held[k, m, b] = weight_ref[m, which, b] - parts[k][b, m] * factor
+                held[k, m, b] = weight_ref[m, which, b] - parts[k][b, m * rows : (m + 1) * rows] * factor
         copies.append(pltpu.make_async_copy(held.at[k], out_ref.at[:, which], sems.at[k]))
         copies[-1].start()
     for copy in copies:
         copy.wait()
 
 
-def finish(place, parts, weight, everyone, right, scale, classes):
+def finish(parts, weight, left, right, scale, classes):
     whole = lambda space: pl.BlockSpec(memory_space=space)
     mats, _, blocks, rows, width = weight.shape
     return pl.pallas_call(
-        functools.partial(finish_kernel, place),
+        finish_kernel,
         in_specs=[whole(pltpu.SMEM)] * 2 + [whole(pltpu.VMEM)] * (3 + CLASSES),
-        out_specs=[whole(pltpu.HBM), whole(pltpu.VMEM)],
-        out_shape=[
-            jax.ShapeDtypeStruct(weight.shape, weight.dtype),
-            jax.ShapeDtypeStruct((mats, CLASSES * blocks, rows), weight.dtype),
-        ],
+        out_specs=whole(pltpu.HBM),
+        out_shape=jax.ShapeDtypeStruct(weight.shape, weight.dtype),
         scratch_shapes=[
             pltpu.VMEM((CLASSES, mats, blocks, rows, width), weight.dtype),
-            pltpu.VMEM((CLASSES, blocks * mats, rows), weight.dtype),
             pltpu.SemaphoreType.DMA((CLASSES,)),
         ],
         compiler_params=pltpu.CompilerParams(vmem_limit_bytes=20 << 20),
         cost_estimate=pl.CostEstimate(flops=2**21, bytes_accessed=6 * 2**20, transcendentals=0),
-    )(classes, scale, everyone, right, weight, *parts)
+    )(classes, scale, left, right, weight, *parts)
 
 
 def local(gradients, weight, row_state, col_state):
@@ -160,18 +136,24 @@
     place = owners(size)
     part = spread(gradients.reshape(mats, size, count, width), place, me)
     extra = row_statistics(part, row_state, lookup(place, me))
-    pair = pairs_of(part, place, me)
-    everyone = lax.all_gather(after(extra, pair), "dp")
-    own = class_of(pair, place, me)
+    sent = jnp.concatenate([part.reshape(mats * count, width), extra], axis=0)
+    members = [[place.index(c * blocks + b) for b in range(blocks)] for c in range(CLASSES)]
+    own = lax.all_gather(sent, "dp", axis_index_groups=members)
+    small = lax.optimization_barrier(own[:, mats * count :])
+    smalls = jnp.stack([small] + [reach(small, hop, size) for hop in BACK])
     parts = [own] + [reach(own, hop, size) for hop in BACK]
-    col_new, scale = col_statistics(after(jnp.sum(everyone, axis=0)[mats:], own), col_state)
     classes = [lookup([p // blocks for p in place], me)]
     for hop in BACK:
         source = {target(r, hop, size): r for r in range(size)}
         classes.append(lookup([place[source[r]] // blocks for r in range(size)], me))
+    placed = jnp.stack(classes)[None, :] == jnp.arange(CLASSES)[:, None]
+    smalls_placed = jnp.sum(jnp.where(placed[:, :, None, None, None], smalls[None], 0.0), axis=1)
+    row_new = jnp.transpose(smalls_placed[:, :, :mats].reshape(size, mats, count), (1, 0, 2)).reshape(mats, rows)
+    col_new, scale = col_statistics(jnp.sum(smalls_placed[:, :, mats:], axis=(0, 1)), col_state)
+    left = lax.rsqrt(smalls[:, :, :mats]).reshape(CLASSES, blocks * mats, count)
     split = weight.reshape(mats, CLASSES, blocks, count, width)
-    new_weight, row_new = finish(place, parts, split, everyone, lax.rsqrt(col_new), scale, jnp.stack(classes))
-    return (new_weight.reshape(weight.shape), row_new.reshape(mats, rows), col_new)
+    new_weight = finish(parts, split, left, lax.rsqrt(col_new), scale, jnp.stack(classes))
+    return (new_weight.reshape(weight.shape), row_new, col_new)
 
 
 def solution(mesh):

time: 167 us -> 160 us (0.958)
  starting transfers between devices: 52.1 us -> 47.7 us
  blocking collectives: 67.5 us -> 65 us
    all_gather x1, blocking collectives: 18.8 us -> 12.5 us  [col_statistics(): shares = lax.all_gather(sums[mats:2 * mats] / col_new, 'col')]
    ppermute x10 -> x11, starting transfers between devices: 52.1 us -> 47.7 us  [reach(): lax.ppermute(plain(x), 'dp', [(r, target(r, hop, size)) for r in range(si...]
    all_gather x1, blocking collectives: 25.6 us -> 29.2 us  [local(): own = lax.all_gather(sent, 'dp', axis_index_groups=members)]
    ppermute x10 -> x11, waiting for transfers between devices: 37.1 us -> 37.1 us  [reach(): lax.ppermute(plain(x), 'dp', [(r, target(r, hop, size)) for r in range(si...]
  transfers between devices with their start and end apart: 10 -> 11, of which waited for: 4 -> 4; matrix products, arithmetic and copies ran while one was open for 1% -> 1% of each run, Pallas kernels for 0% -> 0%
where the time goes in v6:
time: 160 us; the launch traced here: 159 us
  blocking collectives  65 us (41%)
  starting transfers between devices  47.7 us (30%)
  waiting for transfers between devices  37.1 us (23%)
  Pallas kernels  3.38 us (2%)
  other arithmetic  2.87 us (2%)
  local copies, waits for them, and re-layouts  2.26 us (1%)
    ppermute x11, starting transfers between devices, reach(): lax.ppermute(plain(x), 'dp', [(r, target(r, hop, size)) for r in range(si...  47.7 us
    ppermute x11, waiting for transfers between devices, reach(): lax.ppermute(plain(x), 'dp', [(r, target(r, hop, size)) for r in range(si...  37.1 us
    all_gather x1, blocking collectives, local(): own = lax.all_gather(sent, 'dp', axis_index_groups=members)  29.2 us
    all_gather x1, blocking collectives, row_statistics(): row_sum = jnp.sum(lax.all_gather(jnp.sum(squares, axis=2), 'col'), axis=0)  13.4 us
    all_gather x1, blocking collectives, col_statistics(): shares = lax.all_gather(sums[mats:2 * mats] / col_new, 'col')  12.5 us
    all_gather x1, blocking collectives, col_statistics(): sums = jnp.sum(lax.all_gather(sums, 'row'), axis=0)  9.94 us
    pallas_call x1, Pallas kernels, finish(): pl.pallas_call(finish_kernel, in_specs=[whole(pltpu.SMEM)] * 2 + [whole(p...  3.38 us
  transfers between devices with their start and end apart: 11, of which 4 were waited for; matrix products, arithmetic and copies ran while one was open for 1% of the time, Pallas kernels for 0%

profile of v6, /device:TPU:1, one launch (start us, length us, event | category | flops | bytes accessed | tf_op | source)
XLA Modules:
  0.0 159.2 jit_solution(3787986525820358352)
XLA Ops:
  0.7 1.5 constant_dynamic-slice_fusion.4
  2.1 5.7 %collective-permute-start = (f32[2,4,128,128]{3,2,1,0:T(8,128)S(1)}, f32[2,4,128,128]{3,2,1,0:T(8,128)S(1)}, u32[]{:S(2)}, u32[]{:S(2)}) collective-permute-start(f32[2,4,128,128]{3,2,1,0:T(8,128)S(1)} %get-tuple-element.9), channel_id=1, source_target_pairs={{0,64},{32,480},{64,128},{96,32},{128,192},{160,96},{192,256},{224... | collective-permute-start | bytes 1572872 | tf_op jit(solution)/shard_map/ppermute | solution.py:51
  7.9 9.3 %collective-permute-start.2 = (f32[2,4,128,128]{3,2,1,0:T(8,128)S(1)}, f32[2,4,128,128]{3,2,1,0:T(8,128)S(1)}, u32[]{:S(2)}, u32[]{:S(2)}) collective-permute-start(f32[2,4,128,128]{3,2,1,0:T(8,128)S(1)} %get-tuple-element.10), channel_id=1, source_target_pairs={{0,480},{32,64},{64,32},{96,128},{128,96},{160,192},{192,160},{224... | collective-permute-start | bytes 1572872 | tf_op jit(solution)/shard_map/ppermute | solution.py:51
  17.2 1.9 %collective-permute-start.1 = (f32[2,4,128,128]{3,2,1,0:T(8,128)S(1)}, f32[2,4,128,128]{3,2,1,0:T(8,128)}, u32[]{:S(2)}, u32[]{:S(2)}) collective-permute-start(f32[2,4,128,128]{3,2,1,0:T(8,128)S(1)} %get-tuple-element.11), channel_id=1, source_target_pairs={{0,32},{32,0},{64,96},{96,64},{128,160},{160,128},{192,224},{224,1... | collective-permute-start | bytes 1572872 | tf_op jit(solution)/shard_map/ppermute | solution.py:51
  19.2 7.1 %collective-permute-done = f32[2,4,128,128]{3,2,1,0:T(8,128)S(1)} collective-permute-done((f32[2,4,128,128]{3,2,1,0:T(8,128)S(1)}, f32[2,4,128,128]{3,2,1,0:T(8,128)S(1)}, u32[]{:S(2)}, u32[]{:S(2)}) %collective-permute-start) | collective-permute-done | bytes 524320 | tf_op jit(solution)/shard_map/ppermute | solution.py:51
  26.2 11.9 %collective-permute-done.2 = f32[2,4,128,128]{3,2,1,0:T(8,128)S(1)} collective-permute-done((f32[2,4,128,128]{3,2,1,0:T(8,128)S(1)}, f32[2,4,128,128]{3,2,1,0:T(8,128)S(1)}, u32[]{:S(2)}, u32[]{:S(2)}) %collective-permute-start.2) | collective-permute-done | bytes 524320 | tf_op jit(solution)/shard_map/ppermute | solution.py:51
  38.2 0.0 collective-permute-done.1
  38.2 1.3 add_add_fusion
  39.5 0.0 copy-start.2
  39.5 0.0 copy-start
  39.5 2.1 %collective-permute-start.3 = (f32[2,2,128,128]{3,2,1,0:T(8,128)S(1)}, f32[2,2,128,128]{3,2,1,0:T(8,128)S(1)}, u32[]{:S(2)}, u32[]{:S(2)}) collective-permute-start(f32[2,2,128,128]{3,2,1,0:T(8,128)S(1)} %constant_dynamic-slice_fusion.1), channel_id=1, source_target_pairs={{0,96},{32,448},{64,160},{96,0},{128,224},{160,64},{192,288},{224,... | collective-permute-start | bytes 786440 | tf_op jit(solution)/shard_map/ppermute | solution.py:51
  41.6 14.0 %collective-permute-done.3 = f32[2,2,128,128]{3,2,1,0:T(8,128)S(1)} collective-permute-done((f32[2,2,128,128]{3,2,1,0:T(8,128)S(1)}, f32[2,2,128,128]{3,2,1,0:T(8,128)S(1)}, u32[]{:S(2)}, u32[]{:S(2)}) %collective-permute-start.3) | collective-permute-done | bytes 262176 | tf_op jit(solution)/shard_map/ppermute | solution.py:51
  55.6 8.7 %collective-permute-start.4 = (f32[2,128,128]{2,1,0:T(8,128)S(1)}, f32[2,128,128]{2,1,0:T(8,128)S(1)}, u32[]{:S(2)}, u32[]{:S(2)}) collective-permute-start(f32[2,128,128]{2,1,0:T(8,128)S(1)} %fusion), channel_id=1, source_target_pairs={{0,352},{32,192},{64,416},{96,256},{128,480},{160,320},{192,32},{2... | collective-permute-start | bytes 393224 | tf_op jit(solution)/shard_map/ppermute | solution.py:51
  64.3 0.1 pad_add_fusion.class_ref
  64.4 4.1 %collective-permute-done.4 = f32[2,128,128]{2,1,0:T(8,128)S(1)} collective-permute-done((f32[2,128,128]{2,1,0:T(8,128)S(1)}, f32[2,128,128]{2,1,0:T(8,128)S(1)}, u32[]{:S(2)}, u32[]{:S(2)}) %collective-permute-start.4) | collective-permute-done | bytes 131104 | tf_op jit(solution)/shard_map/ppermute | solution.py:51
  68.5 0.1 fusion.4
  68.6 13.4 %all-gather.4 = f32[8,2,128]{2,1,0:T(2,128)S(1)} all-gather(f32[1,2,128]{2,1,0:T(2,128)S(1)} %bitcast.60), channel_id=2, replica_groups=mesh['dp'=16,'row'=4,'col'=8] {'col'}, dimensions={0}, use_global_device_ids=true | all-gather | bytes 9216 | tf_op jit(solution)/shard_map/all_gather | solution.py:76
  82.0 0.8 fusion.9
  82.8 0.1 multiply_reduce_fusion
  82.9 0.1 broadcast_in_dim.32
  83.0 29.2 %all-gather.1 = f32[1056,128]{1,0:T(8,128)S(1)} all-gather(f32[264,128]{1,0:T(8,128)S(1)} %concatenate.3), channel_id=3, replica_groups={{352,0,96,256},{416,64,160,320},{480,128,224,384},{32,192,288,448},{353..., dimensions={0}, use_global_device_ids=true | all-gather | bytes 675840 | tf_op jit(solution)/shard_map/all_gather | solution.py:141
  112.2 4.2 %collective-permute-start.6 = (f32[4,8,128]{2,1,0:T(8,128)S(1)}, f32[4,8,128]{2,1,0:T(8,128)S(1)}, u32[]{:S(2)}, u32[]{:S(2)}) collective-permute-start(f32[4,8,128]{2,1,0:T(8,128)S(1)} %slice.28), channel_id=1, source_target_pairs={{0,32},{32,0},{64,96},{96,64},{128,160},{160,128},{192,224},{224,1... | collective-permute-start | bytes 49160 | tf_op jit(solution)/shard_map/ppermute | solution.py:51
  116.4 3.5 %collective-permute-start.5 = (f32[4,8,128]{2,1,0:T(8,128)S(1)}, f32[4,8,128]{2,1,0:T(8,128)S(1)}, u32[]{:S(2)}, u32[]{:S(2)}) collective-permute-start(f32[4,8,128]{2,1,0:T(8,128)S(1)} %slice.28), channel_id=1, source_target_pairs={{0,448},{32,96},{64,0},{96,160},{128,64},{160,224},{192,128},{224,... | collective-permute-start | bytes 49160 | tf_op jit(solution)/shard_map/ppermute | solution.py:51
  119.9 2.7 %collective-permute-start.7 = (f32[4,8,128]{2,1,0:T(8,128)S(1)}, f32[4,8,128]{2,1,0:T(8,128)S(1)}, u32[]{:S(2)}, u32[]{:S(2)}) collective-permute-start(f32[4,8,128]{2,1,0:T(8,128)S(1)} %slice.28), channel_id=1, source_target_pairs={{0,480},{32,64},{64,32},{96,128},{128,96},{160,192},{192,160},{224... | collective-permute-start | bytes 49160 | tf_op jit(solution)/shard_map/ppermute | solution.py:51
  122.6 2.2 %collective-permute-start.9 = (f32[4,264,128]{2,1,0:T(8,128)S(1)}, f32[4,264,128]{2,1,0:T(8,128)S(1)}, u32[]{:S(2)}, u32[]{:S(2)}) collective-permute-start(f32[4,264,128]{2,1,0:T(8,128)S(1)} %bitcast.44), channel_id=1, source_target_pairs={{0,32},{32,0},{64,96},{96,64},{128,160},{160,128},{192,224},{224,1... | collective-permute-start | bytes 1622024 | tf_op jit(solution)/shard_map/ppermute | solution.py:51
  124.8 4.7 %collective-permute-start.8 = (f32[4,264,128]{2,1,0:T(8,128)S(1)}, f32[4,264,128]{2,1,0:T(8,128)}, u32[]{:S(2)}, u32[]{:S(2)}) collective-permute-start(f32[4,264,128]{2,1,0:T(8,128)S(1)} %bitcast.45), channel_id=1, source_target_pairs={{0,448},{32,96},{64,0},{96,160},{128,64},{160,224},{192,128},{224,... | collective-permute-start | bytes 1622024 | tf_op jit(solution)/shard_map/ppermute | solution.py:51
  129.5 0.0 collective-permute-done.6
  129.5 2.8 %collective-permute-start.10 = (f32[4,264,128]{2,1,0:T(8,128)S(1)}, f32[4,264,128]{2,1,0:T(8,128)}, u32[]{:S(2)}, u32[]{:S(2)}) collective-permute-start(f32[4,264,128]{2,1,0:T(8,128)S(1)} %bitcast.46), channel_id=1, source_target_pairs={{0,480},{32,64},{64,32},{96,128},{128,96},{160,192},{192,160},{224... | collective-permute-start | bytes 1622024 | tf_op jit(solution)/shard_map/ppermute | solution.py:51
  132.3 0.0 collective-permute-done.5
  132.3 0.0 collective-permute-done.7
  132.3 0.1 select_reduce_fusion
  132.4 0.6 slice.31
  133.0 9.9 %all-gather.5 = f32[4,6,128]{2,1,0:T(8,128)S(1)} all-gather(f32[1,6,128]{2,1,0:T(8,128)S(1)} %bitcast.55), channel_id=4, replica_groups=mesh['dp'=16,'row'=4,'col'=8] {'row'}, dimensions={0}, use_global_device_ids=true | all-gather | bytes 15360 | tf_op jit(solution)/shard_map/all_gather | solution.py:86
  143.0 0.0 copy-done.2
  143.0 0.0 copy-start.1
  143.0 12.5 %all-gather.6 = f32[8,2,128]{2,1,0:T(2,128)S(1)} all-gather(f32[1,2,128]{2,1,0:T(2,128)S(1)} %fusion.7), channel_id=5, replica_groups=mesh['dp'=16,'row'=4,'col'=8] {'col'}, dimensions={0}, use_global_device_ids=true | all-gather | bytes 9216 | tf_op jit(solution)/shard_map/all_gather | solution.py:89
  155.5 0.1 reduce_sum.89
  155.6 0.1 multiply_reduce_fusion.1
  155.8 0.0 collective-permute-done.9.refs_2_
  155.8 0.0 collective-permute-done.8.refs_1_
  155.8 0.0 collective-permute-done.10.refs_3_
  155.8 0.0 copy-done
  155.8 3.4 %shard_map.67 = f32[2,4,4,128,128]{4,3,2,1,0:T(8,128)} custom-call(s32[4]{0:T(128)S(1)} %pad_add_fusion.class_ref, f32[2]{0:T(128)S(1)} %maximum_divide_fusion.scale_ref, f32[4,8,128]{2,1,0:T(8,128)S(1)} %bitcast.49, f32[2,128]{1,0:T(2,128)S(1)} %get-tuple-element.5.right_ref, f32[2,4,4,128,128]{4,3,2,1,0:T(8,128)S(1)} %bitcast.48, ...), custom_call_target="tpu_custom_call" | custom-call | flops 2097152 | bytes 6291456 | tf_op jit(solution)/shard_map/pallas_call | solution.py:118
  159.2 0.0 copy-done.1
  (15 shorter events, 0.2 us)
Async XLA Ops:
  2.1 24.1 %collective-permute-start = (f32[2,4,128,128]{3,2,1,0:T(8,128)S(1)}, f32[2,4,128,128]{3,2,1,0:T(8,128)S(1)}, u32[]{:S(2)}, u32[]{:S(2)}) collective-permute-start(f32[2,4,128,128]{3,2,1,0:T(8,128)S(1)} %get-tuple-element.9), channel_id=1, source_target_pairs={{0,64},{32,480},{64,128},{96,32},{128,192},{160,96},{192,256},{224... | collective-permute-start | bytes 1572872 | tf_op jit(solution)/shard_map/ppermute | solution.py:51
  7.9 30.3 %collective-permute-start.2 = (f32[2,4,128,128]{3,2,1,0:T(8,128)S(1)}, f32[2,4,128,128]{3,2,1,0:T(8,128)S(1)}, u32[]{:S(2)}, u32[]{:S(2)}) collective-permute-start(f32[2,4,128,128]{3,2,1,0:T(8,128)S(1)} %get-tuple-element.10), channel_id=1, source_target_pairs={{0,480},{32,64},{64,32},{96,128},{128,96},{160,192},{192,160},{224... | collective-permute-start | bytes 1572872 | tf_op jit(solution)/shard_map/ppermute | solution.py:51
  17.2 21.0 %collective-permute-start.1 = (f32[2,4,128,128]{3,2,1,0:T(8,128)S(1)}, f32[2,4,128,128]{3,2,1,0:T(8,128)}, u32[]{:S(2)}, u32[]{:S(2)}) collective-permute-start(f32[2,4,128,128]{3,2,1,0:T(8,128)S(1)} %get-tuple-element.11), channel_id=1, source_target_pairs={{0,32},{32,0},{64,96},{96,64},{128,160},{160,128},{192,224},{224,1... | collective-permute-start | bytes 1572872 | tf_op jit(solution)/shard_map/ppermute | solution.py:51
  39.5 103.5 %copy-start.2 = (f32[2,128]{1,0:T(2,128)S(1)}, f32[2,128]{1,0:T(2,128)}, u32[]{:S(2)}) copy-start(f32[2,128]{1,0:T(2,128)} %param.7) | copy-start | bytes 3076
  39.5 116.3 %copy-start = (f32[2,2048,128]{2,1,0:T(8,128)S(1)}, f32[2,2048,128]{2,1,0:T(8,128)}, u32[]{:S(2)}) copy-start(f32[2,2048,128]{2,1,0:T(8,128)} %param.5) | copy-start | bytes 6291460
  39.5 16.1 %collective-permute-start.3 = (f32[2,2,128,128]{3,2,1,0:T(8,128)S(1)}, f32[2,2,128,128]{3,2,1,0:T(8,128)S(1)}, u32[]{:S(2)}, u32[]{:S(2)}) collective-permute-start(f32[2,2,128,128]{3,2,1,0:T(8,128)S(1)} %constant_dynamic-slice_fusion.1), channel_id=1, source_target_pairs={{0,96},{32,448},{64,160},{96,0},{128,224},{160,64},{192,288},{224,... | collective-permute-start | bytes 786440 | tf_op jit(solution)/shard_map/ppermute | solution.py:51
  55.6 12.8 %collective-permute-start.4 = (f32[2,128,128]{2,1,0:T(8,128)S(1)}, f32[2,128,128]{2,1,0:T(8,128)S(1)}, u32[]{:S(2)}, u32[]{:S(2)}) collective-permute-start(f32[2,128,128]{2,1,0:T(8,128)S(1)} %fusion), channel_id=1, source_target_pairs={{0,352},{32,192},{64,416},{96,256},{128,480},{160,320},{192,32},{2... | collective-permute-start | bytes 393224 | tf_op jit(solution)/shard_map/ppermute | solution.py:51
  112.2 17.3 %collective-permute-start.6 = (f32[4,8,128]{2,1,0:T(8,128)S(1)}, f32[4,8,128]{2,1,0:T(8,128)S(1)}, u32[]{:S(2)}, u32[]{:S(2)}) collective-permute-start(f32[4,8,128]{2,1,0:T(8,128)S(1)} %slice.28), channel_id=1, source_target_pairs={{0,32},{32,0},{64,96},{96,64},{128,160},{160,128},{192,224},{224,1... | collective-permute-start | bytes 49160 | tf_op jit(solution)/shard_map/ppermute | solution.py:51
  116.4 15.9 %collective-permute-start.5 = (f32[4,8,128]{2,1,0:T(8,128)S(1)}, f32[4,8,128]{2,1,0:T(8,128)S(1)}, u32[]{:S(2)}, u32[]{:S(2)}) collective-permute-start(f32[4,8,128]{2,1,0:T(8,128)S(1)} %slice.28), channel_id=1, source_target_pairs={{0,448},{32,96},{64,0},{96,160},{128,64},{160,224},{192,128},{224,... | collective-permute-start | bytes 49160 | tf_op jit(solution)/shard_map/ppermute | solution.py:51
  119.9 12.4 %collective-permute-start.7 = (f32[4,8,128]{2,1,0:T(8,128)S(1)}, f32[4,8,128]{2,1,0:T(8,128)S(1)}, u32[]{:S(2)}, u32[]{:S(2)}) collective-permute-start(f32[4,8,128]{2,1,0:T(8,128)S(1)} %slice.28), channel_id=1, source_target_pairs={{0,480},{32,64},{64,32},{96,128},{128,96},{160,192},{192,160},{224... | collective-permute-start | bytes 49160 | tf_op jit(solution)/shard_map/ppermute | solution.py:51
  122.6 33.1 %collective-permute-start.9 = (f32[4,264,128]{2,1,0:T(8,128)S(1)}, f32[4,264,128]{2,1,0:T(8,128)S(1)}, u32[]{:S(2)}, u32[]{:S(2)}) collective-permute-start(f32[4,264,128]{2,1,0:T(8,128)S(1)} %bitcast.44), channel_id=1, source_target_pairs={{0,32},{32,0},{64,96},{96,64},{128,160},{160,128},{192,224},{224,1... | collective-permute-start | bytes 1622024 | tf_op jit(solution)/shard_map/ppermute | solution.py:51
  124.8 31.0 %collective-permute-start.8 = (f32[4,264,128]{2,1,0:T(8,128)S(1)}, f32[4,264,128]{2,1,0:T(8,128)}, u32[]{:S(2)}, u32[]{:S(2)}) collective-permute-start(f32[4,264,128]{2,1,0:T(8,128)S(1)} %bitcast.45), channel_id=1, source_target_pairs={{0,448},{32,96},{64,0},{96,160},{128,64},{160,224},{192,128},{224,... | collective-permute-start | bytes 1622024 | tf_op jit(solution)/shard_map/ppermute | solution.py:51
  129.5 26.3 %collective-permute-start.10 = (f32[4,264,128]{2,1,0:T(8,128)S(1)}, f32[4,264,128]{2,1,0:T(8,128)}, u32[]{:S(2)}, u32[]{:S(2)}) collective-permute-start(f32[4,264,128]{2,1,0:T(8,128)S(1)} %bitcast.46), channel_id=1, source_target_pairs={{0,480},{32,64},{64,32},{96,128},{128,96},{160,192},{192,160},{224... | collective-permute-start | bytes 1622024 | tf_op jit(solution)/shard_map/ppermute | solution.py:51
  143.0 16.2 %copy-start.1 = (f32[2,128]{1,0:T(2,128)}, f32[2,128]{1,0:T(2,128)S(1)}, u32[]{:S(2)}) copy-start(f32[2,128]{1,0:T(2,128)S(1)} %get-tuple-element.6) | copy-start | bytes 3076

commit v7 on v6

--- a/solution.py
+++ b/solution.py
@@ -139,9 +139,8 @@
     sent = jnp.concatenate([part.reshape(mats * count, width), extra], axis=0)
     members = [[place.index(c * blocks + b) for b in range(blocks)] for c in range(CLASSES)]
     own = lax.all_gather(sent, "dp", axis_index_groups=members)
-    small = lax.optimization_barrier(own[:, mats * count :])
-    smalls = jnp.stack([small] + [reach(small, hop, size) for hop in BACK])
     parts = [own] + [reach(own, hop, size) for hop in BACK]
+    smalls = jnp.stack([p[:, mats * count :] for p in parts])
     classes = [lookup([p // blocks for p in place], me)]
     for hop in BACK:
         source = {target(r, hop, size): r for r in range(size)}

time: 160 us -> 173 us (1.081)
  waiting for transfers between devices: 37.1 us -> 57.2 us
  starting transfers between devices: 47.7 us -> 38.1 us
  local copies, waits for them, and re-layouts: 2.26 us -> 5.93 us
    ppermute x11 -> x8, waiting for transfers between devices: 37.1 us -> 57.2 us  [reach(): lax.ppermute(plain(x), 'dp', [(r, target(r, hop, size)) for r in range(si...]
    ppermute x11 -> x8, starting transfers between devices: 47.7 us -> 38.1 us  [reach(): lax.ppermute(plain(x), 'dp', [(r, target(r, hop, size)) for r in range(si...]
    unnamed x6 -> x14, local copies, waits for them, and re-layouts: 0.02 us -> 3.69 us
  transfers between devices with their start and end apart: 11 -> 8, of which waited for: 4 -> 6; matrix products, arithmetic and copies ran while one was open for 1% -> 0% of each run, Pallas kernels for 0% -> 0%
where the time goes in v7:
time: 173 us; the launch traced here: 172 us
  blocking collectives  64.5 us (37%)
  waiting for transfers between devices  57.2 us (33%)
  starting transfers between devices  38.1 us (22%)
  local copies, waits for them, and re-layouts  5.93 us (3%)
  other arithmetic  2.87 us (2%)
  Pallas kernels  2.73 us (2%)
    ppermute x8, waiting for transfers between devices, reach(): lax.ppermute(plain(x), 'dp', [(r, target(r, hop, size)) for r in range(si...  57.2 us
    ppermute x8, starting transfers between devices, reach(): lax.ppermute(plain(x), 'dp', [(r, target(r, hop, size)) for r in range(si...  38.1 us
    all_gather x1, blocking collectives, local(): own = lax.all_gather(sent, 'dp', axis_index_groups=members)  29.2 us
    all_gather x1, blocking collectives, row_statistics(): row_sum = jnp.sum(lax.all_gather(jnp.sum(squares, axis=2), 'col'), axis=0)  13.4 us
    all_gather x1, blocking collectives, col_statistics(): shares = lax.all_gather(sums[mats:2 * mats] / col_new, 'col')  12.6 us
    all_gather x1, blocking collectives, col_statistics(): sums = jnp.sum(lax.all_gather(sums, 'row'), axis=0)  9.38 us
    unnamed x14, local copies, waits for them, and re-layouts  3.69 us
  transfers between devices with their start and end apart: 8, of which 6 were waited for; matrix products, arithmetic and copies ran while one was open for 0% of the time, Pallas kernels for 0%

profile of v7, /device:TPU:1, one launch (start us, length us, event | category | flops | bytes accessed | tf_op | source)
XLA Modules:
  0.0 172.2 jit_solution(12366860000489978330)
XLA Ops:
  0.7 1.5 constant_dynamic-slice_fusion.4
  2.1 5.7 %collective-permute-start = (f32[2,4,128,128]{3,2,1,0:T(8,128)S(1)}, f32[2,4,128,128]{3,2,1,0:T(8,128)S(1)}, u32[]{:S(2)}, u32[]{:S(2)}) collective-permute-start(f32[2,4,128,128]{3,2,1,0:T(8,128)S(1)} %get-tuple-element.9), channel_id=1, source_target_pairs={{0,64},{32,480},{64,128},{96,32},{128,192},{160,96},{192,256},{224... | collective-permute-start | bytes 1572872 | tf_op jit(solution)/shard_map/ppermute | solution.py:51
  7.9 9.3 %collective-permute-start.2 = (f32[2,4,128,128]{3,2,1,0:T(8,128)S(1)}, f32[2,4,128,128]{3,2,1,0:T(8,128)S(1)}, u32[]{:S(2)}, u32[]{:S(2)}) collective-permute-start(f32[2,4,128,128]{3,2,1,0:T(8,128)S(1)} %get-tuple-element.10), channel_id=1, source_target_pairs={{0,480},{32,64},{64,32},{96,128},{128,96},{160,192},{192,160},{224... | collective-permute-start | bytes 1572872 | tf_op jit(solution)/shard_map/ppermute | solution.py:51
  17.2 1.9 %collective-permute-start.1 = (f32[2,4,128,128]{3,2,1,0:T(8,128)S(1)}, f32[2,4,128,128]{3,2,1,0:T(8,128)}, u32[]{:S(2)}, u32[]{:S(2)}) collective-permute-start(f32[2,4,128,128]{3,2,1,0:T(8,128)S(1)} %get-tuple-element.11), channel_id=1, source_target_pairs={{0,32},{32,0},{64,96},{96,64},{128,160},{160,128},{192,224},{224,1... | collective-permute-start | bytes 1572872 | tf_op jit(solution)/shard_map/ppermute | solution.py:51
  19.2 7.1 %collective-permute-done = f32[2,4,128,128]{3,2,1,0:T(8,128)S(1)} collective-permute-done((f32[2,4,128,128]{3,2,1,0:T(8,128)S(1)}, f32[2,4,128,128]{3,2,1,0:T(8,128)S(1)}, u32[]{:S(2)}, u32[]{:S(2)}) %collective-permute-start) | collective-permute-done | bytes 524320 | tf_op jit(solution)/shard_map/ppermute | solution.py:51
  26.2 11.9 %collective-permute-done.2 = f32[2,4,128,128]{3,2,1,0:T(8,128)S(1)} collective-permute-done((f32[2,4,128,128]{3,2,1,0:T(8,128)S(1)}, f32[2,4,128,128]{3,2,1,0:T(8,128)S(1)}, u32[]{:S(2)}, u32[]{:S(2)}) %collective-permute-start.2) | collective-permute-done | bytes 524320 | tf_op jit(solution)/shard_map/ppermute | solution.py:51
  38.2 0.0 collective-permute-done.1
  38.2 1.3 add_add_fusion
  39.5 0.0 copy-start.6
  39.5 0.0 copy-start
  39.5 2.1 %collective-permute-start.3 = (f32[2,2,128,128]{3,2,1,0:T(8,128)S(1)}, f32[2,2,128,128]{3,2,1,0:T(8,128)S(1)}, u32[]{:S(2)}, u32[]{:S(2)}) collective-permute-start(f32[2,2,128,128]{3,2,1,0:T(8,128)S(1)} %constant_dynamic-slice_fusion.1), channel_id=1, source_target_pairs={{0,96},{32,448},{64,160},{96,0},{128,224},{160,64},{192,288},{224,... | collective-permute-start | bytes 786440 | tf_op jit(solution)/shard_map/ppermute | solution.py:51
  41.6 14.0 %collective-permute-done.3 = f32[2,2,128,128]{3,2,1,0:T(8,128)S(1)} collective-permute-done((f32[2,2,128,128]{3,2,1,0:T(8,128)S(1)}, f32[2,2,128,128]{3,2,1,0:T(8,128)S(1)}, u32[]{:S(2)}, u32[]{:S(2)}) %collective-permute-start.3) | collective-permute-done | bytes 262176 | tf_op jit(solution)/shard_map/ppermute | solution.py:51
  55.6 8.7 %collective-permute-start.4 = (f32[2,128,128]{2,1,0:T(8,128)S(1)}, f32[2,128,128]{2,1,0:T(8,128)S(1)}, u32[]{:S(2)}, u32[]{:S(2)}) collective-permute-start(f32[2,128,128]{2,1,0:T(8,128)S(1)} %fusion), channel_id=1, source_target_pairs={{0,352},{32,192},{64,416},{96,256},{128,480},{160,320},{192,32},{2... | collective-permute-start | bytes 393224 | tf_op jit(solution)/shard_map/ppermute | solution.py:51
  64.3 4.1 %collective-permute-done.4 = f32[2,128,128]{2,1,0:T(8,128)S(1)} collective-permute-done((f32[2,128,128]{2,1,0:T(8,128)S(1)}, f32[2,128,128]{2,1,0:T(8,128)S(1)}, u32[]{:S(2)}, u32[]{:S(2)}) %collective-permute-start.4) | collective-permute-done | bytes 131104 | tf_op jit(solution)/shard_map/ppermute | solution.py:51
  68.5 0.1 fusion.4
  68.6 13.4 %all-gather.4 = f32[8,2,128]{2,1,0:T(2,128)S(1)} all-gather(f32[1,2,128]{2,1,0:T(2,128)S(1)} %bitcast.60), channel_id=2, replica_groups=mesh['dp'=16,'row'=4,'col'=8] {'col'}, dimensions={0}, use_global_device_ids=true | all-gather | bytes 9216 | tf_op jit(solution)/shard_map/all_gather | solution.py:76
  82.0 0.8 fusion.9
  82.8 0.1 multiply_reduce_fusion
  82.9 0.1 broadcast_in_dim.32
  83.0 29.2 %all-gather.1 = f32[1056,128]{1,0:T(8,128)S(1)} all-gather(f32[264,128]{1,0:T(8,128)S(1)} %concatenate.3), channel_id=3, replica_groups={{352,0,96,256},{416,64,160,320},{480,128,224,384},{32,192,288,448},{353..., dimensions={0}, use_global_device_ids=true | all-gather | bytes 675840 | tf_op jit(solution)/shard_map/all_gather | solution.py:141
  112.2 4.2 %collective-permute-start.6 = (f32[4,264,128]{2,1,0:T(8,128)S(1)}, f32[4,264,128]{2,1,0:T(8,128)S(1)}, u32[]{:S(2)}, u32[]{:S(2)}) collective-permute-start(f32[4,264,128]{2,1,0:T(8,128)S(1)} %bitcast.47), channel_id=1, source_target_pairs={{0,32},{32,0},{64,96},{96,64},{128,160},{160,128},{192,224},{224,1... | collective-permute-start | bytes 1622024 | tf_op jit(solution)/shard_map/ppermute | solution.py:51
  116.4 0.1 pad_add_fusion.class_ref
  116.5 3.5 %collective-permute-start.5 = (f32[4,264,128]{2,1,0:T(8,128)S(1)}, f32[4,264,128]{2,1,0:T(8,128)S(1)}, u32[]{:S(2)}, u32[]{:S(2)}) collective-permute-start(f32[4,264,128]{2,1,0:T(8,128)S(1)} %bitcast.48), channel_id=1, source_target_pairs={{0,448},{32,96},{64,0},{96,160},{128,64},{160,224},{192,128},{224,... | collective-permute-start | bytes 1622024 | tf_op jit(solution)/shard_map/ppermute | solution.py:51
  119.9 2.7 %collective-permute-start.7 = (f32[4,264,128]{2,1,0:T(8,128)S(1)}, f32[4,264,128]{2,1,0:T(8,128)S(1)}, u32[]{:S(2)}, u32[]{:S(2)}) collective-permute-start(f32[4,264,128]{2,1,0:T(8,128)S(1)} %bitcast.49), channel_id=1, source_target_pairs={{0,480},{32,64},{64,32},{96,128},{128,96},{160,192},{192,160},{224... | collective-permute-start | bytes 1622024 | tf_op jit(solution)/shard_map/ppermute | solution.py:51
  122.7 16.8 %collective-permute-done.6.refs_2_ = f32[4,264,128]{2,1,0:T(8,128)S(1)} collective-permute-done((f32[4,264,128]{2,1,0:T(8,128)S(1)}, f32[4,264,128]{2,1,0:T(8,128)S(1)}, u32[]{:S(2)}, u32[]{:S(2)}) %collective-permute-start.6) | collective-permute-done | bytes 540704 | tf_op jit(solution)/shard_map/ppermute | solution.py:51
  139.5 0.0 collective-permute-done.5.refs_1_
  139.5 0.0 copy-start.1
  139.5 0.8 copy-done.1
  140.3 3.3 %collective-permute-done.7.refs_3_ = f32[4,264,128]{2,1,0:T(8,128)S(1)} collective-permute-done((f32[4,264,128]{2,1,0:T(8,128)S(1)}, f32[4,264,128]{2,1,0:T(8,128)S(1)}, u32[]{:S(2)}, u32[]{:S(2)}) %collective-permute-start.7) | collective-permute-done | bytes 540704 | tf_op jit(solution)/shard_map/ppermute | solution.py:51
  143.6 0.0 copy-start.3
  143.6 0.8 copy-done.3
  144.4 0.1 select_reduce_fusion
  144.5 0.6 slice.46
  145.1 9.4 %all-gather.5 = f32[4,6,128]{2,1,0:T(8,128)S(1)} all-gather(f32[1,6,128]{2,1,0:T(8,128)S(1)} %bitcast.58), channel_id=4, replica_groups=mesh['dp'=16,'row'=4,'col'=8] {'row'}, dimensions={0}, use_global_device_ids=true | all-gather | bytes 15360 | tf_op jit(solution)/shard_map/all_gather | solution.py:86
  154.5 0.1 multiply_reduce_fusion.1
  154.6 0.0 copy-done.6
  154.7 0.0 copy-start.5
  154.7 12.6 %all-gather.6 = f32[8,2,128]{2,1,0:T(2,128)S(1)} all-gather(f32[1,2,128]{2,1,0:T(2,128)S(1)} %fusion.7), channel_id=5, replica_groups=mesh['dp'=16,'row'=4,'col'=8] {'col'}, dimensions={0}, use_global_device_ids=true | all-gather | bytes 9216 | tf_op jit(solution)/shard_map/all_gather | solution.py:89
  167.2 0.1 reduce_sum.89
  167.4 0.0 copy-done
  167.4 0.0 copy-start.2
  167.4 1.0 copy-done.2
  168.4 0.0 copy-start.4
  168.4 1.0 copy-done.4
  169.5 2.7 %shard_map.67 = f32[2,4,4,128,128]{4,3,2,1,0:T(8,128)} custom-call(s32[4]{0:T(128)S(1)} %pad_add_fusion.class_ref, f32[2]{0:T(128)S(1)} %maximum_divide_fusion.scale_ref, f32[4,8,128]{2,1,0:T(8,128)S(1)} %bitcast.53, f32[2,128]{1,0:T(2,128)S(1)} %get-tuple-element.5.right_ref, f32[2,4,4,128,128]{4,3,2,1,0:T(8,128)S(1)} %bitcast.52, ...), custom_call_target="tpu_custom_call" | custom-call | flops 2097152 | bytes 6291456 | tf_op jit(solution)/shard_map/pallas_call | solution.py:118
  172.2 0.0 copy-done.5
  (18 shorter events, 0.2 us)
Async XLA Ops:
  2.1 24.1 %collective-permute-start = (f32[2,4,128,128]{3,2,1,0:T(8,128)S(1)}, f32[2,4,128,128]{3,2,1,0:T(8,128)S(1)}, u32[]{:S(2)}, u32[]{:S(2)}) collective-permute-start(f32[2,4,128,128]{3,2,1,0:T(8,128)S(1)} %get-tuple-element.9), channel_id=1, source_target_pairs={{0,64},{32,480},{64,128},{96,32},{128,192},{160,96},{192,256},{224... | collective-permute-start | bytes 1572872 | tf_op jit(solution)/shard_map/ppermute | solution.py:51
  7.9 30.3 %collective-permute-start.2 = (f32[2,4,128,128]{3,2,1,0:T(8,128)S(1)}, f32[2,4,128,128]{3,2,1,0:T(8,128)S(1)}, u32[]{:S(2)}, u32[]{:S(2)}) collective-permute-start(f32[2,4,128,128]{3,2,1,0:T(8,128)S(1)} %get-tuple-element.10), channel_id=1, source_target_pairs={{0,480},{32,64},{64,32},{96,128},{128,96},{160,192},{192,160},{224... | collective-permute-start | bytes 1572872 | tf_op jit(solution)/shard_map/ppermute | solution.py:51
  17.2 21.0 %collective-permute-start.1 = (f32[2,4,128,128]{3,2,1,0:T(8,128)S(1)}, f32[2,4,128,128]{3,2,1,0:T(8,128)}, u32[]{:S(2)}, u32[]{:S(2)}) collective-permute-start(f32[2,4,128,128]{3,2,1,0:T(8,128)S(1)} %get-tuple-element.11), channel_id=1, source_target_pairs={{0,32},{32,0},{64,96},{96,64},{128,160},{160,128},{192,224},{224,1... | collective-permute-start | bytes 1572872 | tf_op jit(solution)/shard_map/ppermute | solution.py:51
  39.5 115.2 %copy-start.6 = (f32[2,128]{1,0:T(2,128)S(1)}, f32[2,128]{1,0:T(2,128)}, u32[]{:S(2)}) copy-start(f32[2,128]{1,0:T(2,128)} %param.7) | copy-start | bytes 3076
  39.5 127.9 %copy-start = (f32[2,2048,128]{2,1,0:T(8,128)S(1)}, f32[2,2048,128]{2,1,0:T(8,128)}, u32[]{:S(2)}) copy-start(f32[2,2048,128]{2,1,0:T(8,128)} %param.5) | copy-start | bytes 6291460
  39.5 16.1 %collective-permute-start.3 = (f32[2,2,128,128]{3,2,1,0:T(8,128)S(1)}, f32[2,2,128,128]{3,2,1,0:T(8,128)S(1)}, u32[]{:S(2)}, u32[]{:S(2)}) collective-permute-start(f32[2,2,128,128]{3,2,1,0:T(8,128)S(1)} %constant_dynamic-slice_fusion.1), channel_id=1, source_target_pairs={{0,96},{32,448},{64,160},{96,0},{128,224},{160,64},{192,288},{224,... | collective-permute-start | bytes 786440 | tf_op jit(solution)/shard_map/ppermute | solution.py:51
  55.6 12.8 %collective-permute-start.4 = (f32[2,128,128]{2,1,0:T(8,128)S(1)}, f32[2,128,128]{2,1,0:T(8,128)S(1)}, u32[]{:S(2)}, u32[]{:S(2)}) collective-permute-start(f32[2,128,128]{2,1,0:T(8,128)S(1)} %fusion), channel_id=1, source_target_pairs={{0,352},{32,192},{64,416},{96,256},{128,480},{160,320},{192,32},{2... | collective-permute-start | bytes 393224 | tf_op jit(solution)/shard_map/ppermute | solution.py:51
  112.2 27.3 %collective-permute-start.6 = (f32[4,264,128]{2,1,0:T(8,128)S(1)}, f32[4,264,128]{2,1,0:T(8,128)S(1)}, u32[]{:S(2)}, u32[]{:S(2)}) collective-permute-start(f32[4,264,128]{2,1,0:T(8,128)S(1)} %bitcast.47), channel_id=1, source_target_pairs={{0,32},{32,0},{64,96},{96,64},{128,160},{160,128},{192,224},{224,1... | collective-permute-start | bytes 1622024 | tf_op jit(solution)/shard_map/ppermute | solution.py:51
  116.5 23.0 %collective-permute-start.5 = (f32[4,264,128]{2,1,0:T(8,128)S(1)}, f32[4,264,128]{2,1,0:T(8,128)S(1)}, u32[]{:S(2)}, u32[]{:S(2)}) collective-permute-start(f32[4,264,128]{2,1,0:T(8,128)S(1)} %bitcast.48), channel_id=1, source_target_pairs={{0,448},{32,96},{64,0},{96,160},{128,64},{160,224},{192,128},{224,... | collective-permute-start | bytes 1622024 | tf_op jit(solution)/shard_map/ppermute | solution.py:51
  119.9 23.6 %collective-permute-start.7 = (f32[4,264,128]{2,1,0:T(8,128)S(1)}, f32[4,264,128]{2,1,0:T(8,128)S(1)}, u32[]{:S(2)}, u32[]{:S(2)}) collective-permute-start(f32[4,264,128]{2,1,0:T(8,128)S(1)} %bitcast.49), channel_id=1, source_target_pairs={{0,480},{32,64},{64,32},{96,128},{128,96},{160,192},{192,160},{224... | collective-permute-start | bytes 1622024 | tf_op jit(solution)/shard_map/ppermute | solution.py:51
  139.5 0.8 copy-start.1
  143.6 0.8 copy-start.3
  154.7 17.6 %copy-start.5 = (f32[2,128]{1,0:T(2,128)}, f32[2,128]{1,0:T(2,128)S(1)}, u32[]{:S(2)}) copy-start(f32[2,128]{1,0:T(2,128)S(1)} %get-tuple-element.6) | copy-start | bytes 3076
  167.4 1.1 copy-start.2
  168.4 1.0 copy-start.4

commit v8 on v6

--- a/solution.py
+++ b/solution.py
@@ -17,7 +17,7 @@
 step_size = 0.25
 
 CLASSES = 4
-HOPS = (2, 1, -1)
+HOPS = (2, -1, 1)
 STEPS = (3, -5)
 BACK = tuple(hop if hop % 2 else -hop for hop in HOPS)
 

time: 160 us -> 160 us (level)
  starting transfers between devices: 47.7 us -> 49.8 us
    ppermute x11, starting transfers between devices: 47.7 us -> 49.8 us  [reach(): lax.ppermute(plain(x), 'dp', [(r, target(r, hop, size)) for r in range(si...]
  transfers between devices with their start and end apart: 11 -> 11, of which waited for: 4 -> 5; matrix products, arithmetic and copies ran while one was open for 1% -> 1% of each run, Pallas kernels for 0% -> 0%
where the time goes in v8:
time: 160 us
  blocking collectives  63.5 us (40%)
  starting transfers between devices  49.8 us (31%)
  waiting for transfers between devices  36.9 us (23%)
  Pallas kernels  3.38 us (2%)
  other arithmetic  2.87 us (2%)
  local copies, waits for them, and re-layouts  2.26 us (1%)
    ppermute x11, starting transfers between devices, reach(): lax.ppermute(plain(x), 'dp', [(r, target(r, hop, size)) for r in range(si...  49.8 us
    ppermute x11, waiting for transfers between devices, reach(): lax.ppermute(plain(x), 'dp', [(r, target(r, hop, size)) for r in range(si...  36.9 us
    all_gather x1, blocking collectives, local(): own = lax.all_gather(sent, 'dp', axis_index_groups=members)  27.7 us
    all_gather x1, blocking collectives, row_statistics(): row_sum = jnp.sum(lax.all_gather(jnp.sum(squares, axis=2), 'col'), axis=0)  13.5 us
    all_gather x1, blocking collectives, col_statistics(): shares = lax.all_gather(sums[mats:2 * mats] / col_new, 'col')  12.4 us
    all_gather x1, blocking collectives, col_statistics(): sums = jnp.sum(lax.all_gather(sums, 'row'), axis=0)  9.99 us
    pallas_call x1, Pallas kernels, finish(): pl.pallas_call(finish_kernel, in_specs=[whole(pltpu.SMEM)] * 2 + [whole(p...  3.38 us
  transfers between devices with their start and end apart: 11, of which 5 were waited for; matrix products, arithmetic and copies ran while one was open for 1% of the time, Pallas kernels for 0%

profile of v8, /device:TPU:1, one launch (start us, length us, event | category | flops | bytes accessed | tf_op | source)
XLA Modules:
  0.0 159.7 jit_solution(15398899716356223175)
XLA Ops:
  0.7 1.5 constant_dynamic-slice_fusion.4
  2.1 5.7 %collective-permute-start = (f32[2,4,128,128]{3,2,1,0:T(8,128)S(1)}, f32[2,4,128,128]{3,2,1,0:T(8,128)S(1)}, u32[]{:S(2)}, u32[]{:S(2)}) collective-permute-start(f32[2,4,128,128]{3,2,1,0:T(8,128)S(1)} %get-tuple-element.9), channel_id=1, source_target_pairs={{0,64},{32,480},{64,128},{96,32},{128,192},{160,96},{192,256},{224... | collective-permute-start | bytes 1572872 | tf_op jit(solution)/shard_map/ppermute | solution.py:51
  7.9 9.3 %collective-permute-start.2 = (f32[2,4,128,128]{3,2,1,0:T(8,128)S(1)}, f32[2,4,128,128]{3,2,1,0:T(8,128)S(1)}, u32[]{:S(2)}, u32[]{:S(2)}) collective-permute-start(f32[2,4,128,128]{3,2,1,0:T(8,128)S(1)} %get-tuple-element.10), channel_id=1, source_target_pairs={{0,32},{32,0},{64,96},{96,64},{128,160},{160,128},{192,224},{224,1... | collective-permute-start | bytes 1572872 | tf_op jit(solution)/shard_map/ppermute | solution.py:51
  17.2 1.9 %collective-permute-start.1 = (f32[2,4,128,128]{3,2,1,0:T(8,128)S(1)}, f32[2,4,128,128]{3,2,1,0:T(8,128)}, u32[]{:S(2)}, u32[]{:S(2)}) collective-permute-start(f32[2,4,128,128]{3,2,1,0:T(8,128)S(1)} %get-tuple-element.11), channel_id=1, source_target_pairs={{0,480},{32,64},{64,32},{96,128},{128,96},{160,192},{192,160},{224... | collective-permute-start | bytes 1572872 | tf_op jit(solution)/shard_map/ppermute | solution.py:51
  19.2 7.1 %collective-permute-done = f32[2,4,128,128]{3,2,1,0:T(8,128)S(1)} collective-permute-done((f32[2,4,128,128]{3,2,1,0:T(8,128)S(1)}, f32[2,4,128,128]{3,2,1,0:T(8,128)S(1)}, u32[]{:S(2)}, u32[]{:S(2)}) %collective-permute-start) | collective-permute-done | bytes 524320 | tf_op jit(solution)/shard_map/ppermute | solution.py:51
  26.2 11.7 %collective-permute-done.2 = f32[2,4,128,128]{3,2,1,0:T(8,128)S(1)} collective-permute-done((f32[2,4,128,128]{3,2,1,0:T(8,128)S(1)}, f32[2,4,128,128]{3,2,1,0:T(8,128)S(1)}, u32[]{:S(2)}, u32[]{:S(2)}) %collective-permute-start.2) | collective-permute-done | bytes 524320 | tf_op jit(solution)/shard_map/ppermute | solution.py:51
  38.0 0.3 collective-permute-done.1
  38.3 1.3 add_add_fusion
  39.6 0.0 copy-start.2
  39.6 0.0 copy-start
  39.6 2.1 %collective-permute-start.3 = (f32[2,2,128,128]{3,2,1,0:T(8,128)S(1)}, f32[2,2,128,128]{3,2,1,0:T(8,128)S(1)}, u32[]{:S(2)}, u32[]{:S(2)}) collective-permute-start(f32[2,2,128,128]{3,2,1,0:T(8,128)S(1)} %constant_dynamic-slice_fusion.1), channel_id=1, source_target_pairs={{0,96},{32,448},{64,160},{96,0},{128,224},{160,64},{192,288},{224,... | collective-permute-start | bytes 786440 | tf_op jit(solution)/shard_map/ppermute | solution.py:51
  41.7 13.9 %collective-permute-done.3 = f32[2,2,128,128]{3,2,1,0:T(8,128)S(1)} collective-permute-done((f32[2,2,128,128]{3,2,1,0:T(8,128)S(1)}, f32[2,2,128,128]{3,2,1,0:T(8,128)S(1)}, u32[]{:S(2)}, u32[]{:S(2)}) %collective-permute-start.3) | collective-permute-done | bytes 262176 | tf_op jit(solution)/shard_map/ppermute | solution.py:51
  55.7 8.7 %collective-permute-start.4 = (f32[2,128,128]{2,1,0:T(8,128)S(1)}, f32[2,128,128]{2,1,0:T(8,128)S(1)}, u32[]{:S(2)}, u32[]{:S(2)}) collective-permute-start(f32[2,128,128]{2,1,0:T(8,128)S(1)} %fusion), channel_id=1, source_target_pairs={{0,352},{32,192},{64,416},{96,256},{128,480},{160,320},{192,32},{2... | collective-permute-start | bytes 393224 | tf_op jit(solution)/shard_map/ppermute | solution.py:51
  64.3 0.1 pad_add_fusion.class_ref
  64.4 3.8 %collective-permute-done.4 = f32[2,128,128]{2,1,0:T(8,128)S(1)} collective-permute-done((f32[2,128,128]{2,1,0:T(8,128)S(1)}, f32[2,128,128]{2,1,0:T(8,128)S(1)}, u32[]{:S(2)}, u32[]{:S(2)}) %collective-permute-start.4) | collective-permute-done | bytes 131104 | tf_op jit(solution)/shard_map/ppermute | solution.py:51
  68.3 0.1 fusion.4
  68.4 13.5 %all-gather.4 = f32[8,2,128]{2,1,0:T(2,128)S(1)} all-gather(f32[1,2,128]{2,1,0:T(2,128)S(1)} %bitcast.60), channel_id=2, replica_groups=mesh['dp'=16,'row'=4,'col'=8] {'col'}, dimensions={0}, use_global_device_ids=true | all-gather | bytes 9216 | tf_op jit(solution)/shard_map/all_gather | solution.py:76
  81.9 0.8 fusion.9
  82.7 0.1 multiply_reduce_fusion
  82.8 0.1 broadcast_in_dim.32
  82.9 27.7 %all-gather.1 = f32[1056,128]{1,0:T(8,128)S(1)} all-gather(f32[264,128]{1,0:T(8,128)S(1)} %concatenate.3), channel_id=3, replica_groups={{352,0,96,256},{416,64,160,320},{480,128,224,384},{32,192,288,448},{353..., dimensions={0}, use_global_device_ids=true | all-gather | bytes 675840 | tf_op jit(solution)/shard_map/all_gather | solution.py:141
  110.6 7.5 %collective-permute-start.6 = (f32[4,8,128]{2,1,0:T(8,128)S(1)}, f32[4,8,128]{2,1,0:T(8,128)S(1)}, u32[]{:S(2)}, u32[]{:S(2)}) collective-permute-start(f32[4,8,128]{2,1,0:T(8,128)S(1)} %slice.28), channel_id=1, source_target_pairs={{0,480},{32,64},{64,32},{96,128},{128,96},{160,192},{192,160},{224... | collective-permute-start | bytes 49160 | tf_op jit(solution)/shard_map/ppermute | solution.py:51
  118.1 1.9 %collective-permute-start.5 = (f32[4,8,128]{2,1,0:T(8,128)S(1)}, f32[4,8,128]{2,1,0:T(8,128)S(1)}, u32[]{:S(2)}, u32[]{:S(2)}) collective-permute-start(f32[4,8,128]{2,1,0:T(8,128)S(1)} %slice.28), channel_id=1, source_target_pairs={{0,448},{32,96},{64,0},{96,160},{128,64},{160,224},{192,128},{224,... | collective-permute-start | bytes 49160 | tf_op jit(solution)/shard_map/ppermute | solution.py:51
  120.0 1.9 %collective-permute-start.7 = (f32[4,8,128]{2,1,0:T(8,128)S(1)}, f32[4,8,128]{2,1,0:T(8,128)S(1)}, u32[]{:S(2)}, u32[]{:S(2)}) collective-permute-start(f32[4,8,128]{2,1,0:T(8,128)S(1)} %slice.28), channel_id=1, source_target_pairs={{0,32},{32,0},{64,96},{96,64},{128,160},{160,128},{192,224},{224,1... | collective-permute-start | bytes 49160 | tf_op jit(solution)/shard_map/ppermute | solution.py:51
  122.0 3.8 %collective-permute-start.9 = (f32[4,264,128]{2,1,0:T(8,128)S(1)}, f32[4,264,128]{2,1,0:T(8,128)S(1)}, u32[]{:S(2)}, u32[]{:S(2)}) collective-permute-start(f32[4,264,128]{2,1,0:T(8,128)S(1)} %bitcast.44), channel_id=1, source_target_pairs={{0,480},{32,64},{64,32},{96,128},{128,96},{160,192},{192,160},{224... | collective-permute-start | bytes 1622024 | tf_op jit(solution)/shard_map/ppermute | solution.py:51
  125.8 2.8 %collective-permute-start.8 = (f32[4,264,128]{2,1,0:T(8,128)S(1)}, f32[4,264,128]{2,1,0:T(8,128)}, u32[]{:S(2)}, u32[]{:S(2)}) collective-permute-start(f32[4,264,128]{2,1,0:T(8,128)S(1)} %bitcast.45), channel_id=1, source_target_pairs={{0,448},{32,96},{64,0},{96,160},{128,64},{160,224},{192,128},{224,... | collective-permute-start | bytes 1622024 | tf_op jit(solution)/shard_map/ppermute | solution.py:51
  128.6 0.0 collective-permute-done.6
  128.6 4.2 %collective-permute-start.10 = (f32[4,264,128]{2,1,0:T(8,128)S(1)}, f32[4,264,128]{2,1,0:T(8,128)}, u32[]{:S(2)}, u32[]{:S(2)}) collective-permute-start(f32[4,264,128]{2,1,0:T(8,128)S(1)} %bitcast.46), channel_id=1, source_target_pairs={{0,32},{32,0},{64,96},{96,64},{128,160},{160,128},{192,224},{224,1... | collective-permute-start | bytes 1622024 | tf_op jit(solution)/shard_map/ppermute | solution.py:51
  132.8 0.0 collective-permute-done.5
  132.8 0.0 collective-permute-done.7
  132.9 0.1 select_reduce_fusion
  133.0 0.6 slice.31
  133.6 10.0 %all-gather.5 = f32[4,6,128]{2,1,0:T(8,128)S(1)} all-gather(f32[1,6,128]{2,1,0:T(8,128)S(1)} %bitcast.55), channel_id=4, replica_groups=mesh['dp'=16,'row'=4,'col'=8] {'row'}, dimensions={0}, use_global_device_ids=true | all-gather | bytes 15360 | tf_op jit(solution)/shard_map/all_gather | solution.py:86
  143.6 0.0 copy-done.2
  143.6 0.0 copy-start.1
  143.6 12.4 %all-gather.6 = f32[8,2,128]{2,1,0:T(2,128)S(1)} all-gather(f32[1,2,128]{2,1,0:T(2,128)S(1)} %fusion.7), channel_id=5, replica_groups=mesh['dp'=16,'row'=4,'col'=8] {'col'}, dimensions={0}, use_global_device_ids=true | all-gather | bytes 9216 | tf_op jit(solution)/shard_map/all_gather | solution.py:89
  156.0 0.1 reduce_sum.89
  156.1 0.1 multiply_reduce_fusion.1
  156.3 0.0 collective-permute-done.9.refs_2_
  156.3 0.0 collective-permute-done.8.refs_1_
  156.3 0.0 collective-permute-done.10.refs_3_
  156.3 0.0 copy-done
  156.3 3.4 %shard_map.67 = f32[2,4,4,128,128]{4,3,2,1,0:T(8,128)} custom-call(s32[4]{0:T(128)S(1)} %pad_add_fusion.class_ref, f32[2]{0:T(128)S(1)} %maximum_divide_fusion.scale_ref, f32[4,8,128]{2,1,0:T(8,128)S(1)} %bitcast.49, f32[2,128]{1,0:T(2,128)S(1)} %get-tuple-element.5.right_ref, f32[2,4,4,128,128]{4,3,2,1,0:T(8,128)S(1)} %bitcast.48, ...), custom_call_target="tpu_custom_call" | custom-call | flops 2097152 | bytes 6291456 | tf_op jit(solution)/shard_map/pallas_call | solution.py:118
  159.7 0.0 copy-done.1
  (15 shorter events, 0.2 us)
Async XLA Ops:
  2.1 24.1 %collective-permute-start = (f32[2,4,128,128]{3,2,1,0:T(8,128)S(1)}, f32[2,4,128,128]{3,2,1,0:T(8,128)S(1)}, u32[]{:S(2)}, u32[]{:S(2)}) collective-permute-start(f32[2,4,128,128]{3,2,1,0:T(8,128)S(1)} %get-tuple-element.9), channel_id=1, source_target_pairs={{0,64},{32,480},{64,128},{96,32},{128,192},{160,96},{192,256},{224... | collective-permute-start | bytes 1572872 | tf_op jit(solution)/shard_map/ppermute | solution.py:51
  7.9 30.1 %collective-permute-start.2 = (f32[2,4,128,128]{3,2,1,0:T(8,128)S(1)}, f32[2,4,128,128]{3,2,1,0:T(8,128)S(1)}, u32[]{:S(2)}, u32[]{:S(2)}) collective-permute-start(f32[2,4,128,128]{3,2,1,0:T(8,128)S(1)} %get-tuple-element.10), channel_id=1, source_target_pairs={{0,32},{32,0},{64,96},{96,64},{128,160},{160,128},{192,224},{224,1... | collective-permute-start | bytes 1572872 | tf_op jit(solution)/shard_map/ppermute | solution.py:51
  17.2 21.1 %collective-permute-start.1 = (f32[2,4,128,128]{3,2,1,0:T(8,128)S(1)}, f32[2,4,128,128]{3,2,1,0:T(8,128)}, u32[]{:S(2)}, u32[]{:S(2)}) collective-permute-start(f32[2,4,128,128]{3,2,1,0:T(8,128)S(1)} %get-tuple-element.11), channel_id=1, source_target_pairs={{0,480},{32,64},{64,32},{96,128},{128,96},{160,192},{192,160},{224... | collective-permute-start | bytes 1572872 | tf_op jit(solution)/shard_map/ppermute | solution.py:51
  39.6 104.0 %copy-start.2 = (f32[2,128]{1,0:T(2,128)S(1)}, f32[2,128]{1,0:T(2,128)}, u32[]{:S(2)}) copy-start(f32[2,128]{1,0:T(2,128)} %param.7) | copy-start | bytes 3076
  39.6 116.8 %copy-start = (f32[2,2048,128]{2,1,0:T(8,128)S(1)}, f32[2,2048,128]{2,1,0:T(8,128)}, u32[]{:S(2)}) copy-start(f32[2,2048,128]{2,1,0:T(8,128)} %param.5) | copy-start | bytes 6291460
  39.6 16.0 %collective-permute-start.3 = (f32[2,2,128,128]{3,2,1,0:T(8,128)S(1)}, f32[2,2,128,128]{3,2,1,0:T(8,128)S(1)}, u32[]{:S(2)}, u32[]{:S(2)}) collective-permute-start(f32[2,2,128,128]{3,2,1,0:T(8,128)S(1)} %constant_dynamic-slice_fusion.1), channel_id=1, source_target_pairs={{0,96},{32,448},{64,160},{96,0},{128,224},{160,64},{192,288},{224,... | collective-permute-start | bytes 786440 | tf_op jit(solution)/shard_map/ppermute | solution.py:51
  55.7 12.6 %collective-permute-start.4 = (f32[2,128,128]{2,1,0:T(8,128)S(1)}, f32[2,128,128]{2,1,0:T(8,128)S(1)}, u32[]{:S(2)}, u32[]{:S(2)}) collective-permute-start(f32[2,128,128]{2,1,0:T(8,128)S(1)} %fusion), channel_id=1, source_target_pairs={{0,352},{32,192},{64,416},{96,256},{128,480},{160,320},{192,32},{2... | collective-permute-start | bytes 393224 | tf_op jit(solution)/shard_map/ppermute | solution.py:51
  110.6 18.0 %collective-permute-start.6 = (f32[4,8,128]{2,1,0:T(8,128)S(1)}, f32[4,8,128]{2,1,0:T(8,128)S(1)}, u32[]{:S(2)}, u32[]{:S(2)}) collective-permute-start(f32[4,8,128]{2,1,0:T(8,128)S(1)} %slice.28), channel_id=1, source_target_pairs={{0,480},{32,64},{64,32},{96,128},{128,96},{160,192},{192,160},{224... | collective-permute-start | bytes 49160 | tf_op jit(solution)/shard_map/ppermute | solution.py:51
  118.1 14.7 %collective-permute-start.5 = (f32[4,8,128]{2,1,0:T(8,128)S(1)}, f32[4,8,128]{2,1,0:T(8,128)S(1)}, u32[]{:S(2)}, u32[]{:S(2)}) collective-permute-start(f32[4,8,128]{2,1,0:T(8,128)S(1)} %slice.28), channel_id=1, source_target_pairs={{0,448},{32,96},{64,0},{96,160},{128,64},{160,224},{192,128},{224,... | collective-permute-start | bytes 49160 | tf_op jit(solution)/shard_map/ppermute | solution.py:51
  120.0 12.8 %collective-permute-start.7 = (f32[4,8,128]{2,1,0:T(8,128)S(1)}, f32[4,8,128]{2,1,0:T(8,128)S(1)}, u32[]{:S(2)}, u32[]{:S(2)}) collective-permute-start(f32[4,8,128]{2,1,0:T(8,128)S(1)} %slice.28), channel_id=1, source_target_pairs={{0,32},{32,0},{64,96},{96,64},{128,160},{160,128},{192,224},{224,1... | collective-permute-start | bytes 49160 | tf_op jit(solution)/shard_map/ppermute | solution.py:51
  122.0 34.3 %collective-permute-start.9 = (f32[4,264,128]{2,1,0:T(8,128)S(1)}, f32[4,264,128]{2,1,0:T(8,128)S(1)}, u32[]{:S(2)}, u32[]{:S(2)}) collective-permute-start(f32[4,264,128]{2,1,0:T(8,128)S(1)} %bitcast.44), channel_id=1, source_target_pairs={{0,480},{32,64},{64,32},{96,128},{128,96},{160,192},{192,160},{224... | collective-permute-start | bytes 1622024 | tf_op jit(solution)/shard_map/ppermute | solution.py:51
  125.8 30.5 %collective-permute-start.8 = (f32[4,264,128]{2,1,0:T(8,128)S(1)}, f32[4,264,128]{2,1,0:T(8,128)}, u32[]{:S(2)}, u32[]{:S(2)}) collective-permute-start(f32[4,264,128]{2,1,0:T(8,128)S(1)} %bitcast.45), channel_id=1, source_target_pairs={{0,448},{32,96},{64,0},{96,160},{128,64},{160,224},{192,128},{224,... | collective-permute-start | bytes 1622024 | tf_op jit(solution)/shard_map/ppermute | solution.py:51
  128.6 27.7 %collective-permute-start.10 = (f32[4,264,128]{2,1,0:T(8,128)S(1)}, f32[4,264,128]{2,1,0:T(8,128)}, u32[]{:S(2)}, u32[]{:S(2)}) collective-permute-start(f32[4,264,128]{2,1,0:T(8,128)S(1)} %bitcast.46), channel_id=1, source_target_pairs={{0,32},{32,0},{64,96},{96,64},{128,160},{160,128},{192,224},{224,1... | collective-permute-start | bytes 1622024 | tf_op jit(solution)/shard_map/ppermute | solution.py:51
  143.6 16.1 %copy-start.1 = (f32[2,128]{1,0:T(2,128)}, f32[2,128]{1,0:T(2,128)S(1)}, u32[]{:S(2)}) copy-start(f32[2,128]{1,0:T(2,128)S(1)} %get-tuple-element.6) | copy-start | bytes 3076

commit v9 on v6

--- a/solution.py
+++ b/solution.py
@@ -124,7 +124,7 @@
             pltpu.VMEM((CLASSES, mats, blocks, rows, width), weight.dtype),
             pltpu.SemaphoreType.DMA((CLASSES,)),
         ],
-        compiler_params=pltpu.CompilerParams(vmem_limit_bytes=20 << 20),
+        compiler_params=pltpu.CompilerParams(vmem_limit_bytes=10 << 20),
         cost_estimate=pl.CostEstimate(flops=2**21, bytes_accessed=6 * 2**20, transcendentals=0),
     )(classes, scale, left, right, weight, *parts)
 

time: 160 us -> 160 us (level)
  no operation moved by 1% of the time
where the time goes in v9:
time: 160 us; the launch traced here: 159 us
  blocking collectives  65 us (41%)
  starting transfers between devices  47.7 us (30%)
  waiting for transfers between devices  37.1 us (23%)
  Pallas kernels  3.38 us (2%)
  other arithmetic  2.87 us (2%)
  local copies, waits for them, and re-layouts  2.26 us (1%)
    ppermute x11, starting transfers between devices, reach(): lax.ppermute(plain(x), 'dp', [(r, target(r, hop, size)) for r in range(si...  47.7 us
    ppermute x11, waiting for transfers between devices, reach(): lax.ppermute(plain(x), 'dp', [(r, target(r, hop, size)) for r in range(si...  37.1 us
    all_gather x1, blocking collectives, local(): own = lax.all_gather(sent, 'dp', axis_index_groups=members)  29.2 us
    all_gather x1, blocking collectives, row_statistics(): row_sum = jnp.sum(lax.all_gather(jnp.sum(squares, axis=2), 'col'), axis=0)  13.4 us
    all_gather x1, blocking collectives, col_statistics(): shares = lax.all_gather(sums[mats:2 * mats] / col_new, 'col')  12.5 us
    all_gather x1, blocking collectives, col_statistics(): sums = jnp.sum(lax.all_gather(sums, 'row'), axis=0)  9.94 us
    pallas_call x1, Pallas kernels, finish(): pl.pallas_call(finish_kernel, in_specs=[whole(pltpu.SMEM)] * 2 + [whole(p...  3.38 us
  transfers between devices with their start and end apart: 11, of which 4 were waited for; matrix products, arithmetic and copies ran while one was open for 1% of the time, Pallas kernels for 0%

profile of v9, /device:TPU:1, one launch (start us, length us, event | category | flops | bytes accessed | tf_op | source)
XLA Modules:
  0.0 159.2 jit_solution(6973026249424595871)
XLA Ops:
  0.7 1.5 constant_dynamic-slice_fusion.4
  2.1 5.7 %collective-permute-start = (f32[2,4,128,128]{3,2,1,0:T(8,128)S(1)}, f32[2,4,128,128]{3,2,1,0:T(8,128)S(1)}, u32[]{:S(2)}, u32[]{:S(2)}) collective-permute-start(f32[2,4,128,128]{3,2,1,0:T(8,128)S(1)} %get-tuple-element.9), channel_id=1, source_target_pairs={{0,64},{32,480},{64,128},{96,32},{128,192},{160,96},{192,256},{224... | collective-permute-start | bytes 1572872 | tf_op jit(solution)/shard_map/ppermute | solution.py:51
  7.9 9.3 %collective-permute-start.2 = (f32[2,4,128,128]{3,2,1,0:T(8,128)S(1)}, f32[2,4,128,128]{3,2,1,0:T(8,128)S(1)}, u32[]{:S(2)}, u32[]{:S(2)}) collective-permute-start(f32[2,4,128,128]{3,2,1,0:T(8,128)S(1)} %get-tuple-element.10), channel_id=1, source_target_pairs={{0,480},{32,64},{64,32},{96,128},{128,96},{160,192},{192,160},{224... | collective-permute-start | bytes 1572872 | tf_op jit(solution)/shard_map/ppermute | solution.py:51
  17.2 1.9 %collective-permute-start.1 = (f32[2,4,128,128]{3,2,1,0:T(8,128)S(1)}, f32[2,4,128,128]{3,2,1,0:T(8,128)}, u32[]{:S(2)}, u32[]{:S(2)}) collective-permute-start(f32[2,4,128,128]{3,2,1,0:T(8,128)S(1)} %get-tuple-element.11), channel_id=1, source_target_pairs={{0,32},{32,0},{64,96},{96,64},{128,160},{160,128},{192,224},{224,1... | collective-permute-start | bytes 1572872 | tf_op jit(solution)/shard_map/ppermute | solution.py:51
  19.2 7.1 %collective-permute-done = f32[2,4,128,128]{3,2,1,0:T(8,128)S(1)} collective-permute-done((f32[2,4,128,128]{3,2,1,0:T(8,128)S(1)}, f32[2,4,128,128]{3,2,1,0:T(8,128)S(1)}, u32[]{:S(2)}, u32[]{:S(2)}) %collective-permute-start) | collective-permute-done | bytes 524320 | tf_op jit(solution)/shard_map/ppermute | solution.py:51
  26.2 11.9 %collective-permute-done.2 = f32[2,4,128,128]{3,2,1,0:T(8,128)S(1)} collective-permute-done((f32[2,4,128,128]{3,2,1,0:T(8,128)S(1)}, f32[2,4,128,128]{3,2,1,0:T(8,128)S(1)}, u32[]{:S(2)}, u32[]{:S(2)}) %collective-permute-start.2) | collective-permute-done | bytes 524320 | tf_op jit(solution)/shard_map/ppermute | solution.py:51
  38.2 0.0 collective-permute-done.1
  38.2 1.3 add_add_fusion
  39.5 0.0 copy-start.2
  39.5 0.0 copy-start
  39.5 2.1 %collective-permute-start.3 = (f32[2,2,128,128]{3,2,1,0:T(8,128)S(1)}, f32[2,2,128,128]{3,2,1,0:T(8,128)S(1)}, u32[]{:S(2)}, u32[]{:S(2)}) collective-permute-start(f32[2,2,128,128]{3,2,1,0:T(8,128)S(1)} %constant_dynamic-slice_fusion.1), channel_id=1, source_target_pairs={{0,96},{32,448},{64,160},{96,0},{128,224},{160,64},{192,288},{224,... | collective-permute-start | bytes 786440 | tf_op jit(solution)/shard_map/ppermute | solution.py:51
  41.6 14.0 %collective-permute-done.3 = f32[2,2,128,128]{3,2,1,0:T(8,128)S(1)} collective-permute-done((f32[2,2,128,128]{3,2,1,0:T(8,128)S(1)}, f32[2,2,128,128]{3,2,1,0:T(8,128)S(1)}, u32[]{:S(2)}, u32[]{:S(2)}) %collective-permute-start.3) | collective-permute-done | bytes 262176 | tf_op jit(solution)/shard_map/ppermute | solution.py:51
  55.6 8.7 %collective-permute-start.4 = (f32[2,128,128]{2,1,0:T(8,128)S(1)}, f32[2,128,128]{2,1,0:T(8,128)S(1)}, u32[]{:S(2)}, u32[]{:S(2)}) collective-permute-start(f32[2,128,128]{2,1,0:T(8,128)S(1)} %fusion), channel_id=1, source_target_pairs={{0,352},{32,192},{64,416},{96,256},{128,480},{160,320},{192,32},{2... | collective-permute-start | bytes 393224 | tf_op jit(solution)/shard_map/ppermute | solution.py:51
  64.3 0.1 pad_add_fusion.class_ref
  64.4 4.1 %collective-permute-done.4 = f32[2,128,128]{2,1,0:T(8,128)S(1)} collective-permute-done((f32[2,128,128]{2,1,0:T(8,128)S(1)}, f32[2,128,128]{2,1,0:T(8,128)S(1)}, u32[]{:S(2)}, u32[]{:S(2)}) %collective-permute-start.4) | collective-permute-done | bytes 131104 | tf_op jit(solution)/shard_map/ppermute | solution.py:51
  68.5 0.1 fusion.4
  68.6 13.4 %all-gather.4 = f32[8,2,128]{2,1,0:T(2,128)S(1)} all-gather(f32[1,2,128]{2,1,0:T(2,128)S(1)} %bitcast.60), channel_id=2, replica_groups=mesh['dp'=16,'row'=4,'col'=8] {'col'}, dimensions={0}, use_global_device_ids=true | all-gather | bytes 9216 | tf_op jit(solution)/shard_map/all_gather | solution.py:76
  82.0 0.8 fusion.9
  82.8 0.1 multiply_reduce_fusion
  82.9 0.1 broadcast_in_dim.32
  83.0 29.2 %all-gather.1 = f32[1056,128]{1,0:T(8,128)S(1)} all-gather(f32[264,128]{1,0:T(8,128)S(1)} %concatenate.3), channel_id=3, replica_groups={{352,0,96,256},{416,64,160,320},{480,128,224,384},{32,192,288,448},{353..., dimensions={0}, use_global_device_ids=true | all-gather | bytes 675840 | tf_op jit(solution)/shard_map/all_gather | solution.py:141
  112.2 4.2 %collective-permute-start.6 = (f32[4,8,128]{2,1,0:T(8,128)S(1)}, f32[4,8,128]{2,1,0:T(8,128)S(1)}, u32[]{:S(2)}, u32[]{:S(2)}) collective-permute-start(f32[4,8,128]{2,1,0:T(8,128)S(1)} %slice.28), channel_id=1, source_target_pairs={{0,32},{32,0},{64,96},{96,64},{128,160},{160,128},{192,224},{224,1... | collective-permute-start | bytes 49160 | tf_op jit(solution)/shard_map/ppermute | solution.py:51
  116.4 3.5 %collective-permute-start.5 = (f32[4,8,128]{2,1,0:T(8,128)S(1)}, f32[4,8,128]{2,1,0:T(8,128)S(1)}, u32[]{:S(2)}, u32[]{:S(2)}) collective-permute-start(f32[4,8,128]{2,1,0:T(8,128)S(1)} %slice.28), channel_id=1, source_target_pairs={{0,448},{32,96},{64,0},{96,160},{128,64},{160,224},{192,128},{224,... | collective-permute-start | bytes 49160 | tf_op jit(solution)/shard_map/ppermute | solution.py:51
  119.9 2.7 %collective-permute-start.7 = (f32[4,8,128]{2,1,0:T(8,128)S(1)}, f32[4,8,128]{2,1,0:T(8,128)S(1)}, u32[]{:S(2)}, u32[]{:S(2)}) collective-permute-start(f32[4,8,128]{2,1,0:T(8,128)S(1)} %slice.28), channel_id=1, source_target_pairs={{0,480},{32,64},{64,32},{96,128},{128,96},{160,192},{192,160},{224... | collective-permute-start | bytes 49160 | tf_op jit(solution)/shard_map/ppermute | solution.py:51
  122.6 2.2 %collective-permute-start.9 = (f32[4,264,128]{2,1,0:T(8,128)S(1)}, f32[4,264,128]{2,1,0:T(8,128)S(1)}, u32[]{:S(2)}, u32[]{:S(2)}) collective-permute-start(f32[4,264,128]{2,1,0:T(8,128)S(1)} %bitcast.44), channel_id=1, source_target_pairs={{0,32},{32,0},{64,96},{96,64},{128,160},{160,128},{192,224},{224,1... | collective-permute-start | bytes 1622024 | tf_op jit(solution)/shard_map/ppermute | solution.py:51
  124.8 4.7 %collective-permute-start.8 = (f32[4,264,128]{2,1,0:T(8,128)S(1)}, f32[4,264,128]{2,1,0:T(8,128)}, u32[]{:S(2)}, u32[]{:S(2)}) collective-permute-start(f32[4,264,128]{2,1,0:T(8,128)S(1)} %bitcast.45), channel_id=1, source_target_pairs={{0,448},{32,96},{64,0},{96,160},{128,64},{160,224},{192,128},{224,... | collective-permute-start | bytes 1622024 | tf_op jit(solution)/shard_map/ppermute | solution.py:51
  129.5 0.0 collective-permute-done.6
  129.5 2.8 %collective-permute-start.10 = (f32[4,264,128]{2,1,0:T(8,128)S(1)}, f32[4,264,128]{2,1,0:T(8,128)}, u32[]{:S(2)}, u32[]{:S(2)}) collective-permute-start(f32[4,264,128]{2,1,0:T(8,128)S(1)} %bitcast.46), channel_id=1, source_target_pairs={{0,480},{32,64},{64,32},{96,128},{128,96},{160,192},{192,160},{224... | collective-permute-start | bytes 1622024 | tf_op jit(solution)/shard_map/ppermute | solution.py:51
  132.3 0.0 collective-permute-done.5
  132.3 0.0 collective-permute-done.7
  132.3 0.1 select_reduce_fusion
  132.4 0.6 slice.31
  133.0 9.9 %all-gather.5 = f32[4,6,128]{2,1,0:T(8,128)S(1)} all-gather(f32[1,6,128]{2,1,0:T(8,128)S(1)} %bitcast.55), channel_id=4, replica_groups=mesh['dp'=16,'row'=4,'col'=8] {'row'}, dimensions={0}, use_global_device_ids=true | all-gather | bytes 15360 | tf_op jit(solution)/shard_map/all_gather | solution.py:86
  143.0 0.0 copy-done.2
  143.0 0.0 copy-start.1
  143.0 12.5 %all-gather.6 = f32[8,2,128]{2,1,0:T(2,128)S(1)} all-gather(f32[1,2,128]{2,1,0:T(2,128)S(1)} %fusion.7), channel_id=5, replica_groups=mesh['dp'=16,'row'=4,'col'=8] {'col'}, dimensions={0}, use_global_device_ids=true | all-gather | bytes 9216 | tf_op jit(solution)/shard_map/all_gather | solution.py:89
  155.5 0.1 reduce_sum.89
  155.6 0.1 multiply_reduce_fusion.1
  155.8 0.0 collective-permute-done.9.refs_2_
  155.8 0.0 collective-permute-done.8.refs_1_
  155.8 0.0 collective-permute-done.10.refs_3_
  155.8 0.0 copy-done
  155.8 3.4 %shard_map.67 = f32[2,4,4,128,128]{4,3,2,1,0:T(8,128)} custom-call(s32[4]{0:T(128)S(1)} %pad_add_fusion.class_ref, f32[2]{0:T(128)S(1)} %maximum_divide_fusion.scale_ref, f32[4,8,128]{2,1,0:T(8,128)S(1)} %bitcast.49, f32[2,128]{1,0:T(2,128)S(1)} %get-tuple-element.5.right_ref, f32[2,4,4,128,128]{4,3,2,1,0:T(8,128)S(1)} %bitcast.48, ...), custom_call_target="tpu_custom_call" | custom-call | flops 2097152 | bytes 6291456 | tf_op jit(solution)/shard_map/pallas_call | solution.py:118
  159.2 0.0 copy-done.1
  (15 shorter events, 0.2 us)
Async XLA Ops:
  2.1 24.1 %collective-permute-start = (f32[2,4,128,128]{3,2,1,0:T(8,128)S(1)}, f32[2,4,128,128]{3,2,1,0:T(8,128)S(1)}, u32[]{:S(2)}, u32[]{:S(2)}) collective-permute-start(f32[2,4,128,128]{3,2,1,0:T(8,128)S(1)} %get-tuple-element.9), channel_id=1, source_target_pairs={{0,64},{32,480},{64,128},{96,32},{128,192},{160,96},{192,256},{224... | collective-permute-start | bytes 1572872 | tf_op jit(solution)/shard_map/ppermute | solution.py:51
  7.9 30.3 %collective-permute-start.2 = (f32[2,4,128,128]{3,2,1,0:T(8,128)S(1)}, f32[2,4,128,128]{3,2,1,0:T(8,128)S(1)}, u32[]{:S(2)}, u32[]{:S(2)}) collective-permute-start(f32[2,4,128,128]{3,2,1,0:T(8,128)S(1)} %get-tuple-element.10), channel_id=1, source_target_pairs={{0,480},{32,64},{64,32},{96,128},{128,96},{160,192},{192,160},{224... | collective-permute-start | bytes 1572872 | tf_op jit(solution)/shard_map/ppermute | solution.py:51
  17.2 21.0 %collective-permute-start.1 = (f32[2,4,128,128]{3,2,1,0:T(8,128)S(1)}, f32[2,4,128,128]{3,2,1,0:T(8,128)}, u32[]{:S(2)}, u32[]{:S(2)}) collective-permute-start(f32[2,4,128,128]{3,2,1,0:T(8,128)S(1)} %get-tuple-element.11), channel_id=1, source_target_pairs={{0,32},{32,0},{64,96},{96,64},{128,160},{160,128},{192,224},{224,1... | collective-permute-start | bytes 1572872 | tf_op jit(solution)/shard_map/ppermute | solution.py:51
  39.5 103.5 %copy-start.2 = (f32[2,128]{1,0:T(2,128)S(1)}, f32[2,128]{1,0:T(2,128)}, u32[]{:S(2)}) copy-start(f32[2,128]{1,0:T(2,128)} %param.7) | copy-start | bytes 3076
  39.5 116.3 %copy-start = (f32[2,2048,128]{2,1,0:T(8,128)S(1)}, f32[2,2048,128]{2,1,0:T(8,128)}, u32[]{:S(2)}) copy-start(f32[2,2048,128]{2,1,0:T(8,128)} %param.5) | copy-start | bytes 6291460
  39.5 16.1 %collective-permute-start.3 = (f32[2,2,128,128]{3,2,1,0:T(8,128)S(1)}, f32[2,2,128,128]{3,2,1,0:T(8,128)S(1)}, u32[]{:S(2)}, u32[]{:S(2)}) collective-permute-start(f32[2,2,128,128]{3,2,1,0:T(8,128)S(1)} %constant_dynamic-slice_fusion.1), channel_id=1, source_target_pairs={{0,96},{32,448},{64,160},{96,0},{128,224},{160,64},{192,288},{224,... | collective-permute-start | bytes 786440 | tf_op jit(solution)/shard_map/ppermute | solution.py:51
  55.6 12.8 %collective-permute-start.4 = (f32[2,128,128]{2,1,0:T(8,128)S(1)}, f32[2,128,128]{2,1,0:T(8,128)S(1)}, u32[]{:S(2)}, u32[]{:S(2)}) collective-permute-start(f32[2,128,128]{2,1,0:T(8,128)S(1)} %fusion), channel_id=1, source_target_pairs={{0,352},{32,192},{64,416},{96,256},{128,480},{160,320},{192,32},{2... | collective-permute-start | bytes 393224 | tf_op jit(solution)/shard_map/ppermute | solution.py:51
  112.2 17.3 %collective-permute-start.6 = (f32[4,8,128]{2,1,0:T(8,128)S(1)}, f32[4,8,128]{2,1,0:T(8,128)S(1)}, u32[]{:S(2)}, u32[]{:S(2)}) collective-permute-start(f32[4,8,128]{2,1,0:T(8,128)S(1)} %slice.28), channel_id=1, source_target_pairs={{0,32},{32,0},{64,96},{96,64},{128,160},{160,128},{192,224},{224,1... | collective-permute-start | bytes 49160 | tf_op jit(solution)/shard_map/ppermute | solution.py:51
  116.4 15.9 %collective-permute-start.5 = (f32[4,8,128]{2,1,0:T(8,128)S(1)}, f32[4,8,128]{2,1,0:T(8,128)S(1)}, u32[]{:S(2)}, u32[]{:S(2)}) collective-permute-start(f32[4,8,128]{2,1,0:T(8,128)S(1)} %slice.28), channel_id=1, source_target_pairs={{0,448},{32,96},{64,0},{96,160},{128,64},{160,224},{192,128},{224,... | collective-permute-start | bytes 49160 | tf_op jit(solution)/shard_map/ppermute | solution.py:51
  119.9 12.4 %collective-permute-start.7 = (f32[4,8,128]{2,1,0:T(8,128)S(1)}, f32[4,8,128]{2,1,0:T(8,128)S(1)}, u32[]{:S(2)}, u32[]{:S(2)}) collective-permute-start(f32[4,8,128]{2,1,0:T(8,128)S(1)} %slice.28), channel_id=1, source_target_pairs={{0,480},{32,64},{64,32},{96,128},{128,96},{160,192},{192,160},{224... | collective-permute-start | bytes 49160 | tf_op jit(solution)/shard_map/ppermute | solution.py:51
  122.6 33.1 %collective-permute-start.9 = (f32[4,264,128]{2,1,0:T(8,128)S(1)}, f32[4,264,128]{2,1,0:T(8,128)S(1)}, u32[]{:S(2)}, u32[]{:S(2)}) collective-permute-start(f32[4,264,128]{2,1,0:T(8,128)S(1)} %bitcast.44), channel_id=1, source_target_pairs={{0,32},{32,0},{64,96},{96,64},{128,160},{160,128},{192,224},{224,1... | collective-permute-start | bytes 1622024 | tf_op jit(solution)/shard_map/ppermute | solution.py:51
  124.8 31.0 %collective-permute-start.8 = (f32[4,264,128]{2,1,0:T(8,128)S(1)}, f32[4,264,128]{2,1,0:T(8,128)}, u32[]{:S(2)}, u32[]{:S(2)}) collective-permute-start(f32[4,264,128]{2,1,0:T(8,128)S(1)} %bitcast.45), channel_id=1, source_target_pairs={{0,448},{32,96},{64,0},{96,160},{128,64},{160,224},{192,128},{224,... | collective-permute-start | bytes 1622024 | tf_op jit(solution)/shard_map/ppermute | solution.py:51
  129.5 26.3 %collective-permute-start.10 = (f32[4,264,128]{2,1,0:T(8,128)S(1)}, f32[4,264,128]{2,1,0:T(8,128)}, u32[]{:S(2)}, u32[]{:S(2)}) collective-permute-start(f32[4,264,128]{2,1,0:T(8,128)S(1)} %bitcast.46), channel_id=1, source_target_pairs={{0,480},{32,64},{64,32},{96,128},{128,96},{160,192},{192,160},{224... | collective-permute-start | bytes 1622024 | tf_op jit(solution)/shard_map/ppermute | solution.py:51
  143.0 16.2 %copy-start.1 = (f32[2,128]{1,0:T(2,128)}, f32[2,128]{1,0:T(2,128)S(1)}, u32[]{:S(2)}) copy-start(f32[2,128]{1,0:T(2,128)S(1)} %get-tuple-element.6) | copy-start | bytes 3076
